TPU v7x, 512 devices: a whole 4x8x8 slice. The times are simulated.
512 devices in a mesh: space: 128 (over y, z, core), chan: 4 (over x).
Axes of the slice: x: 4, y: 8, z: 8, core: 2. Of those that a mesh axis runs over, the one named last changes fastest.
Arguments:
- features: bfloat16 [128, 256, 512], P('chan', 'space'), may hold values from -6 to 6
- mask_packed: int32 [256, 16], P('space'), may hold values from -2147483648 to 2147483646
- neighbours: int32 [256, 26], P('space'), may hold values from 0 to 10, as said below
- send_list: int32 [128, 8, 1], P('space'), may hold values from 0 to 2, as said below
- weights: bfloat16 [27, 128, 128], P(None, 'chan'), may hold values from -0.109375 to 0.109375
- cotangent: bfloat16 [128, 256, 512], P('chan', 'space'), may hold values from -6 to 6
Outputs:
- activated: bfloat16 [128, 256, 512], P('chan', 'space')
- grad_features: bfloat16 [128, 256, 512], P('chan', 'space')
- grad_weights: float32 [27, 128, 128], P(None, 'chan')
Inputs may be any that keep to these rules, and one draw needn't show every extreme that they name: `neighbours`: entry j of a brick's row names the neighbour at the j-th of the 26 offsets as a row of its partition's table: 0 to 1 the partition's own bricks, 2 + k + s the s-th brick received from the adjacent tile in the k-th planar move, used only where the offset's planar part is that move and the tile exists, 10 none. Every slot that is named is filled in send_list. send_list[q, k, s] is the local index of the s-th brick that partition q sends to the partition whose tile lies at q's tile moved by minus the k-th planar move, or 2 where that slot is empty; a slot is filled exactly when some brick of that partition names it.
All inputs are finite; a program needn't handle non-finite values.
Results may differ from a plain program's by a relative error of at most 0.005.
Values may be sent and summed in bfloat16 or wider, within the bound.
No kernel may reach another device: no remote copies, remote signals or barrier semaphores. Data moves between devices by JAX's collectives and lax.ppermute only.
A program may use at most 128 MiB of HBM per device.

v0:
```python
import math

import jax
import jax.numpy as jnp
from jax import lax
from jax.sharding import PartitionSpec as P

BRICK = 8
VOX = 512


all_offsets = [
    (along_x, along_y, along_z)
    for along_x in (-1, 0, 1)
    for along_y in (-1, 0, 1)
    for along_z in (-1, 0, 1)
]
tile_moves = [
    (move_a, move_b) for move_a in (-1, 0, 1) for move_b in (-1, 0, 1) if (move_a, move_b) != (0, 0)
]
tile_steps = [move_a * 4 + move_b for move_a, move_b in tile_moves]


def passed_along(shard, axis, by):
    count = lax.axis_size(axis)
    pairs = [(i, i + by) for i in range(count) if 0 <= i + by < count]
    return lax.ppermute(shard, axis, pairs)


def unpack_mask(packed):
    shifts = jnp.arange(32, dtype=jnp.int32)
    bitflags = lax.shift_right_logical(packed[:, :, None], shifts[None, None, :]) & 1
    return bitflags.reshape(packed.shape[0], packed.shape[1] * 32).astype(jnp.float32)


def side_slice(direction, extent):
    if direction == -1:
        return slice(extent - 1, extent)
    if direction == 0:
        return slice(0, extent)
    return slice(0, 1)


def cycle_slice(direction, extent):
    if direction == -1:
        return slice(0, 1)
    if direction == 0:
        return slice(1, extent + 1)
    return slice(extent + 1, extent + 2)


def neighbour_slot(along_x, along_y, along_z):
    linear = (along_x + 1) * 9 + (along_y + 1) * 3 + (along_z + 1)
    return linear if linear < 13 else linear - 1


def window_start(extent):
    padded = extent + 2
    return padded * padded + padded + 1


def flat_length(extent):
    padded = extent + 2
    needed = 2 * (padded * padded + padded + 1) + extent * padded * padded
    return (needed + 127) // 128 * 128


def assemble(source_table, center, indices, extent):
    channels, brick_count = (center.shape[0], center.shape[1])
    planes = []
    for along_x in (-1, 0, 1):
        columns = []
        for along_y in (-1, 0, 1):
            pieces = []
            for along_z in (-1, 0, 1):
                if (along_x, along_y, along_z) == (0, 0, 0):
                    source = center
                else:
                    source = jnp.take(
                        source_table, indices[:, neighbour_slot(along_x, along_y, along_z)], axis=1
                    )
                source = source.reshape(channels, brick_count, extent, extent, extent)
                pieces.append(
                    source[
                        :,
                        :,
                        side_slice(along_x, extent),
                        side_slice(along_y, extent),
                        side_slice(along_z, extent),
                    ]
                )
            columns.append(jnp.concatenate(pieces, axis=4))
        planes.append(jnp.concatenate(columns, axis=3))
    padded_cube = jnp.concatenate(planes, axis=2)
    padded_edge = extent + 2
    flattened = padded_cube.reshape(channels, brick_count, padded_edge**3)
    return jnp.pad(flattened, ((0, 0), (0, 0), (0, flat_length(extent) - padded_edge**3)))


def columns_of(padded_block, extent):
    padded = extent + 2
    anchor = window_start(extent)
    length = extent * padded * padded
    windows = []
    for along_x, along_y, along_z in all_offsets:
        offset_flat = along_x * padded * padded + along_y * padded + along_z
        windows.append(padded_block[:, :, anchor + offset_flat : anchor + offset_flat + length])
    return jnp.stack(windows, axis=0)


def interior(window, extent):
    padded = extent + 2
    leading = window.shape[:-1]
    shaped = window.reshape(leading + (extent, padded, padded))[..., :extent, :extent]
    return shaped.reshape(leading + (extent**3,))


def embed_window(values, extent):
    padded = extent + 2
    leading = values.shape[:-1]
    shaped = values.reshape(leading + (extent, extent, extent))
    widths = [(0, 0)] * len(leading) + [(0, 0), (0, padded - extent), (0, padded - extent)]
    return jnp.pad(shaped, widths).reshape(leading + (extent * padded * padded,))


def spread(products, extent, full_length, first_offset):
    padded = extent + 2
    anchor = window_start(extent)
    length = products.shape[-1]
    result = jnp.zeros(products.shape[1:-1] + (full_length,), jnp.float32)
    for position in range(products.shape[0]):
        along_x, along_y, along_z = all_offsets[first_offset + position]
        placed_at = anchor + along_x * padded * padded + along_y * padded + along_z
        result = result + jnp.pad(
            products[position], ((0, 0), (0, 0), (placed_at, full_length - placed_at - length))
        )
    return result


def scatter_block(grad_block, indices, table_rows, extent):
    channels, brick_count = (grad_block.shape[0], grad_block.shape[1])
    padded = extent + 2
    padded_cube = grad_block[:, :, : padded**3].reshape(
        channels, brick_count, padded, padded, padded
    )
    interior_span = slice(1, extent + 1)
    center = padded_cube[:, :, interior_span, interior_span, interior_span].reshape(
        channels, brick_count, extent**3
    )
    accumulated = jnp.zeros((channels, table_rows, extent, extent, extent), jnp.float32)
    for along_x, along_y, along_z in all_offsets:
        if (along_x, along_y, along_z) == (0, 0, 0):
            continue
        column = neighbour_slot(along_x, along_y, along_z)
        rim_piece = padded_cube[
            :,
            :,
            cycle_slice(along_x, extent),
            cycle_slice(along_y, extent),
            cycle_slice(along_z, extent),
        ]
        accumulated = accumulated.at[
            :,
            indices[:, column],
            side_slice(along_x, extent),
            side_slice(along_y, extent),
            side_slice(along_z, extent),
        ].add(rim_piece)
    return (center, accumulated.reshape(channels, table_rows, extent**3))


def on_device(features, mask_packed, neighbours, send_list, weights, cotangent):
    groups = lax.axis_size("space")
    chan_width = features.shape[0]
    brick_count = features.shape[1]
    total_width = weights.shape[2]
    slot_count = send_list.shape[2]
    empty_row = brick_count + 8 * slot_count
    mask_full = unpack_mask(mask_packed)
    masked = features * mask_full[None].astype(jnp.bfloat16)
    with_zero = jnp.concatenate([masked, jnp.zeros((chan_width, 1, VOX), jnp.bfloat16)], axis=1)
    send_local = send_list[0]
    arrivals = []
    for move in range(8):
        outgoing = jnp.take(with_zero, send_local[move], axis=1)
        arrivals.append(passed_along(outgoing, "space", -tile_steps[move]))
    received = jnp.concatenate(arrivals, axis=1)
    source_table = jnp.concatenate(
        [masked, received, jnp.zeros((chan_width, 1, VOX), jnp.bfloat16)], axis=1
    )
    padded_block = assemble(source_table, masked, neighbours, BRICK)
    full_length = padded_block.shape[2]
    stacked = columns_of(padded_block, BRICK).reshape(27 * chan_width, brick_count, -1)
    weight_rows = weights.reshape(27 * chan_width, total_width)
    picked = weight_rows
    summed = lax.psum_scatter(
        interior(
            jnp.einsum("rc,rbt->cbt", picked, stacked, preferred_element_type=jnp.float32), BRICK
        ),
        "chan",
        scatter_dimension=0,
        tiled=True,
    )
    pre_act = summed * mask_full[None]
    gate_value = jax.nn.sigmoid(pre_act)
    activated = (pre_act * gate_value).astype(jnp.bfloat16)
    grad_conv = (
        cotangent.astype(jnp.float32)
        * mask_full[None]
        * gate_value
        * (1.0 + pre_act * (1.0 - gate_value))
    ).astype(jnp.bfloat16)
    grad_block = jnp.zeros((chan_width, brick_count, full_length), jnp.float32)
    window = embed_window(lax.all_gather(grad_conv, "chan", axis=0, tiled=True), BRICK)
    part_weight = jnp.einsum("rbt,cbt->rc", stacked, window, preferred_element_type=jnp.float32)
    grad_weight = part_weight
    picked = weight_rows
    for group_index in range(3):
        row_block = picked[group_index * 9 * chan_width : (group_index + 1) * 9 * chan_width]
        products = jnp.einsum("rc,cbt->rbt", row_block, window, preferred_element_type=jnp.float32)
        products = products.reshape(9, chan_width, brick_count, -1)
        grad_block = grad_block + spread(products, BRICK, full_length, group_index * 9)
    grad_weight, grad_block = (grad_weight, grad_block)
    grad_scale = 1.0 / math.sqrt(brick_count * groups * VOX)
    grad_weights = (lax.psum(grad_weight, "space") * grad_scale).reshape(
        27, chan_width, total_width
    )
    center, accumulated = scatter_block(grad_block, neighbours, empty_row + 1, BRICK)
    own_total = center + accumulated[:, :brick_count]
    going_back = accumulated[:, brick_count:empty_row].astype(jnp.bfloat16)
    pieces_back = []
    for move in range(8):
        back_piece = going_back[:, move * slot_count : (move + 1) * slot_count]
        pieces_back.append(passed_along(back_piece, "space", tile_steps[move]).astype(jnp.float32))
    returned = jnp.concatenate(pieces_back, axis=1)
    return_rows = send_local.reshape(-1)
    own_padded = jnp.concatenate([own_total, jnp.zeros((chan_width, 1, VOX), jnp.float32)], axis=1)
    own_padded = own_padded.at[:, return_rows].add(returned)
    grad_features = (own_padded[:, :brick_count] * mask_full[None]).astype(jnp.bfloat16)
    return (activated, grad_features, grad_weights)


def solution(mesh):
    return jax.shard_map(
        on_device,
        mesh=mesh,
        in_specs=(
            P("chan", "space", None),
            P("space", None),
            P("space", None),
            P("space", None, None),
            P(None, "chan", None),
            P("chan", "space", None),
        ),
        out_specs=(P("chan", "space", None), P("chan", "space", None), P(None, "chan", None)),
        check_vma=False,
    )
```

profile of v0, /device:TPU:1, one launch (start us, length us, event | category | flops | bytes accessed | tf_op | source)
XLA Modules:
  0.0 862.3 jit_solution(18423136964617345270)
XLA Ops:
  105.8 18.5 %reduce-scatter.2.cloned.1.call-done = f32[32,2,512]{2,0,1:T(8,128)} async-done(((f32[128,2,512]{2,0,1:T(8,128)}), f32[32,2,512]{2,0,1:T(8,128)}) %reduce-scatter.2.cloned.1.call-update) | async-done | bytes 131088 | tf_op jit(solution)/shard_map/reduce_scatter | solution.py:196
  146.3 26.5 %while.27 = (s32[]{:T(128)}, f32[32,11,8,8,8]{0,4,3,2,1:T(8,128)S(1)}, s32[2,4]{1,0:T(2,128)}, f32[2,32,1,1,1]{1,4,3,2,0:T(1,128)}, s32[]{:T(128)}, /*index=5*/s32[5]{0:T(128)}, s32[1]{0:T(128)}, s32[]{:T(128)}) while((s32[]{:T(128)}, f32[32,11,8,8,8]{0,4,3,2,1:T(8,128)S(1)}, s32[2,4]{1,0:T(2,128)}, f32[2,32,1,1,1]{1,4,3,2,0:T(1,128)}, s32[]{:T(128)}, ...), condition=%wide.while_cond.1, body=%wide.while_body.1.sunk | while | flops 85 | bytes 899 | solution.py:168
  172.8 16.9 %while.28 = (s32[]{:T(128)}, f32[32,11,8,8,8]{0,4,3,2,1:T(8,128)S(1)}, s32[2,3]{1,0:T(2,128)}, f32[2,32,1,1,8]{1,0,4,3,2:T(2,128)}, s32[]{:T(128)}, /*index=5*/s32[5]{0:T(128)}, s32[1]{0:T(128)}) while((s32[]{:T(128)}, f32[32,11,8,8,8]{0,4,3,2,1:T(8,128)S(1)}, s32[2,3]{1,0:T(2,128)}, f32[2,32,1,1,8]{1,0,4,3,2:T(2,128)}, s32[]{:T(128)}, ...), condition=%wide.while_cond.2, body=%wide.while_body.2.sunk | while | flops 533 | bytes 14563 | solution.py:168
  189.7 27.3 %while.29 = (s32[]{:T(128)}, f32[32,11,8,8,8]{0,4,3,2,1:T(8,128)S(1)}, s32[2,4]{1,0:T(2,128)}, f32[2,32,1,1,1]{1,4,3,2,0:T(1,128)}, s32[]{:T(128)}, /*index=5*/s32[5]{0:T(128)}, s32[1]{0:T(128)}, s32[]{:T(128)}) while((s32[]{:T(128)}, f32[32,11,8,8,8]{0,4,3,2,1:T(8,128)S(1)}, s32[2,4]{1,0:T(2,128)}, f32[2,32,1,1,1]{1,4,3,2,0:T(1,128)}, s32[]{:T(128)}, ...), condition=%wide.while_cond.3, body=%wide.while_body.3.sunk | while | flops 85 | bytes 899 | solution.py:168
  217.0 23.3 %while.30 = (s32[]{:T(128)}, f32[32,11,8,8,8]{0,4,3,2,1:T(8,128)S(1)}, s32[2,3]{1,0:T(2,128)}, f32[2,32,1,8,1]{1,0,4,3,2:T(2,128)}, s32[]{:T(128)}, /*index=5*/s32[5]{0:T(128)}, s32[1]{0:T(128)}, s32[]{:T(128)}) while((s32[]{:T(128)}, f32[32,11,8,8,8]{0,4,3,2,1:T(8,128)S(1)}, s32[2,3]{1,0:T(2,128)}, f32[2,32,1,8,1]{1,0,4,3,2:T(2,128)}, s32[]{:T(128)}, ...), condition=%wide.while_cond.4, body=%wide.while_body.4.sunk | while | flops 533 | bytes 5359 | solution.py:168
  240.4 14.4 %while.31 = (s32[]{:T(128)}, f32[32,11,8,8,8]{0,4,3,2,1:T(8,128)S(1)}, s32[2,2]{1,0:T(2,128)}, f32[2,32,1,8,8]{1,0,4,3,2:T(2,128)}, s32[]{:T(128)}, /*index=5*/s32[5]{0:T(128)}, s32[1]{0:T(128)}) while((s32[]{:T(128)}, f32[32,11,8,8,8]{0,4,3,2,1:T(8,128)S(1)}, s32[2,2]{1,0:T(2,128)}, f32[2,32,1,8,8]{1,0,4,3,2:T(2,128)}, s32[]{:T(128)}, ...), condition=%wide.while_cond.5, body=%wide.while_body.5.sunk | while | flops 4117 | bytes 114895 | solution.py:168
  254.8 23.1 %while.32 = (s32[]{:T(128)}, f32[32,11,8,8,8]{0,4,3,2,1:T(8,128)S(1)}, s32[2,3]{1,0:T(2,128)}, f32[2,32,1,8,1]{1,0,4,3,2:T(2,128)}, s32[]{:T(128)}, /*index=5*/s32[5]{0:T(128)}, s32[1]{0:T(128)}, s32[]{:T(128)}) while((s32[]{:T(128)}, f32[32,11,8,8,8]{0,4,3,2,1:T(8,128)S(1)}, s32[2,3]{1,0:T(2,128)}, f32[2,32,1,8,1]{1,0,4,3,2:T(2,128)}, s32[]{:T(128)}, ...), condition=%wide.while_cond.6, body=%wide.while_body.6.sunk | while | flops 533 | bytes 5359 | solution.py:168
  278.0 26.8 %while.33 = (s32[]{:T(128)}, f32[32,11,8,8,8]{0,4,3,2,1:T(8,128)S(1)}, s32[2,4]{1,0:T(2,128)}, f32[2,32,1,1,1]{1,4,3,2,0:T(1,128)}, s32[]{:T(128)}, /*index=5*/s32[5]{0:T(128)}, s32[1]{0:T(128)}, s32[]{:T(128)}) while((s32[]{:T(128)}, f32[32,11,8,8,8]{0,4,3,2,1:T(8,128)S(1)}, s32[2,4]{1,0:T(2,128)}, f32[2,32,1,1,1]{1,4,3,2,0:T(1,128)}, s32[]{:T(128)}, ...), condition=%wide.while_cond.7, body=%wide.while_body.7.sunk | while | flops 85 | bytes 899 | solution.py:168
  304.8 16.8 %while.34 = (s32[]{:T(128)}, f32[32,11,8,8,8]{0,4,3,2,1:T(8,128)S(1)}, s32[2,3]{1,0:T(2,128)}, f32[2,32,1,1,8]{1,0,4,3,2:T(2,128)}, s32[]{:T(128)}, /*index=5*/s32[5]{0:T(128)}, s32[1]{0:T(128)}) while((s32[]{:T(128)}, f32[32,11,8,8,8]{0,4,3,2,1:T(8,128)S(1)}, s32[2,3]{1,0:T(2,128)}, f32[2,32,1,1,8]{1,0,4,3,2:T(2,128)}, s32[]{:T(128)}, ...), condition=%wide.while_cond.8, body=%wide.while_body.8.sunk | while | flops 533 | bytes 14563 | solution.py:168
  321.6 26.1 %while.35 = (s32[]{:T(128)}, f32[32,11,8,8,8]{0,4,3,2,1:T(8,128)S(1)}, s32[2,4]{1,0:T(2,128)}, f32[2,32,1,1,1]{1,4,3,2,0:T(1,128)}, s32[]{:T(128)}, /*index=5*/s32[5]{0:T(128)}, s32[1]{0:T(128)}, s32[]{:T(128)}) while((s32[]{:T(128)}, f32[32,11,8,8,8]{0,4,3,2,1:T(8,128)S(1)}, s32[2,4]{1,0:T(2,128)}, f32[2,32,1,1,1]{1,4,3,2,0:T(1,128)}, s32[]{:T(128)}, ...), condition=%wide.while_cond.9, body=%wide.while_body.9.sunk | while | flops 85 | bytes 899 | solution.py:168
  347.7 22.8 %while.36 = (s32[]{:T(128)}, f32[32,11,8,8,8]{0,4,3,2,1:T(8,128)S(1)}, s32[2,3]{1,0:T(2,128)}, f32[2,32,8,1,1]{1,0,4,3,2:T(2,128)}, s32[]{:T(128)}, /*index=5*/s32[5]{0:T(128)}, s32[1]{0:T(128)}, s32[]{:T(128)}) while((s32[]{:T(128)}, f32[32,11,8,8,8]{0,4,3,2,1:T(8,128)S(1)}, s32[2,3]{1,0:T(2,128)}, f32[2,32,8,1,1]{1,0,4,3,2:T(2,128)}, s32[]{:T(128)}, ...), condition=%wide.while_cond.10, body=%wide.while_body.10.sunk | while | flops 533 | bytes 5359 | solution.py:168
  383.1 18.9 %while.38 = (s32[]{:T(128)}, f32[32,11,8,8,8]{0,4,3,2,1:T(8,128)S(1)}, s32[2,3]{1,0:T(2,128)}, f32[2,32,8,1,1]{1,0,4,3,2:T(2,128)}, s32[]{:T(128)}, /*index=5*/s32[5]{0:T(128)}, s32[1]{0:T(128)}, s32[]{:T(128)}) while((s32[]{:T(128)}, f32[32,11,8,8,8]{0,4,3,2,1:T(8,128)S(1)}, s32[2,3]{1,0:T(2,128)}, f32[2,32,8,1,1]{1,0,4,3,2:T(2,128)}, s32[]{:T(128)}, ...), condition=%wide.while_cond.12, body=%wide.while_body.12.sunk | while | flops 533 | bytes 5359 | solution.py:168
  402.1 14.9 %while.39 = (s32[]{:T(128)}, f32[32,11,8,8,8]{0,4,3,2,1:T(8,128)S(1)}, s32[2,2]{1,0:T(2,128)}, f32[2,32,8,8,1]{1,0,4,3,2:T(2,128)S(1)}, s32[]{:T(128)}, /*index=5*/s32[5]{0:T(128)}, s32[1]{0:T(128)}, s32[]{:T(128)}) while((s32[]{:T(128)}, f32[32,11,8,8,8]{0,4,3,2,1:T(8,128)S(1)}, s32[2,2]{1,0:T(2,128)}, f32[2,32,8,8,1]{1,0,4,3,2:T(2,128)S(1)}, ...), condition=%wide.while_cond.13, body=%wide.while_body.13.sunk | while | flops 4117 | bytes 41179 | solution.py:168
  417.1 14.9 %while.40 = (s32[]{:T(128)}, f32[32,11,8,8,8]{0,4,3,2,1:T(8,128)S(1)}, s32[2,2]{1,0:T(2,128)}, f32[2,32,8,8,1]{1,0,4,3,2:T(2,128)S(1)}, s32[]{:T(128)}, /*index=5*/s32[5]{0:T(128)}, s32[1]{0:T(128)}, s32[]{:T(128)}) while((s32[]{:T(128)}, f32[32,11,8,8,8]{0,4,3,2,1:T(8,128)S(1)}, s32[2,2]{1,0:T(2,128)}, f32[2,32,8,8,1]{1,0,4,3,2:T(2,128)S(1)}, ...), condition=%wide.while_cond.14, body=%wide.while_body.14.sunk | while | flops 4117 | bytes 41179 | solution.py:168
  432.1 19.5 %while.41 = (s32[]{:T(128)}, f32[32,11,8,8,8]{0,4,3,2,1:T(8,128)S(1)}, s32[2,3]{1,0:T(2,128)}, f32[2,32,8,1,1]{1,0,4,3,2:T(2,128)}, s32[]{:T(128)}, /*index=5*/s32[5]{0:T(128)}, s32[1]{0:T(128)}, s32[]{:T(128)}) while((s32[]{:T(128)}, f32[32,11,8,8,8]{0,4,3,2,1:T(8,128)S(1)}, s32[2,3]{1,0:T(2,128)}, f32[2,32,8,1,1]{1,0,4,3,2:T(2,128)}, s32[]{:T(128)}, ...), condition=%wide.while_cond.15, body=%wide.while_body.15.sunk | while | flops 533 | bytes 5359 | solution.py:168
  451.6 13.6 %while.42 = (s32[]{:T(128)}, f32[32,11,8,8,8]{0,4,3,2,1:T(8,128)S(1)}, s32[2,2]{1,0:T(2,128)}, f32[2,32,8,1,8]{1,0,4,3,2:T(2,128)}, s32[]{:T(128)}, /*index=5*/s32[5]{0:T(128)}, s32[1]{0:T(128)}) while((s32[]{:T(128)}, f32[32,11,8,8,8]{0,4,3,2,1:T(8,128)S(1)}, s32[2,2]{1,0:T(2,128)}, f32[2,32,8,1,8]{1,0,4,3,2:T(2,128)}, s32[]{:T(128)}, ...), condition=%wide.while_cond.16, body=%wide.while_body.16.sunk | while | flops 4117 | bytes 114895 | solution.py:168
  465.3 18.3 %while.43 = (s32[]{:T(128)}, f32[32,11,8,8,8]{0,4,3,2,1:T(8,128)S(1)}, s32[2,3]{1,0:T(2,128)}, f32[2,32,8,1,1]{1,0,4,3,2:T(2,128)S(1)}, s32[]{:T(128)}, /*index=5*/s32[5]{0:T(128)}, s32[1]{0:T(128)}, s32[]{:T(128)}) while((s32[]{:T(128)}, f32[32,11,8,8,8]{0,4,3,2,1:T(8,128)S(1)}, s32[2,3]{1,0:T(2,128)}, f32[2,32,8,1,1]{1,0,4,3,2:T(2,128)S(1)}, ...), condition=%wide.while_cond.17, body=%wide.while_body.17.sunk | while | flops 533 | bytes 5359 | solution.py:168
  483.6 19.4 %while.44 = (s32[]{:T(128)}, f32[32,11,8,8,8]{0,4,3,2,1:T(8,128)S(1)}, s32[2,4]{1,0:T(2,128)S(1)}, f32[2,32,1,1,1]{1,4,3,2,0:T(1,128)S(1)}, s32[]{:T(128)}, /*index=5*/s32[5]{0:T(128)S(1)}, s32[1]{0:T(128)}, s32[]{:T(128)}) while((s32[]{:T(128)}, f32[32,11,8,8,8]{0,4,3,2,1:T(8,128)S(1)}, s32[2,4]{1,0:T(2,128)S(1)}, ...), condition=%wide.while_cond.18, body=%wide.while_body.18.sunk | while | flops 85 | bytes 899 | solution.py:168
  514.5 18.9 %while.46 = (s32[]{:T(128)}, f32[32,11,8,8,8]{0,4,3,2,1:T(8,128)S(1)}, s32[2,4]{1,0:T(2,128)S(1)}, f32[2,32,1,1,1]{1,4,3,2,0:T(1,128)S(1)}, s32[]{:T(128)}, /*index=5*/s32[5]{0:T(128)S(1)}, s32[1]{0:T(128)}, s32[]{:T(128)}) while((s32[]{:T(128)}, f32[32,11,8,8,8]{0,4,3,2,1:T(8,128)S(1)}, s32[2,4]{1,0:T(2,128)S(1)}, ...), condition=%wide.while_cond.20, body=%wide.while_body.20.sunk | while | flops 85 | bytes 899 | solution.py:168
  533.5 15.6 %while.47 = (s32[]{:T(128)}, f32[32,11,8,8,8]{0,4,3,2,1:T(8,128)S(1)}, s32[2,3]{1,0:T(2,128)S(1)}, f32[2,32,1,8,1]{1,0,4,3,2:T(2,128)S(1)}, s32[]{:T(128)}, /*index=5*/s32[5]{0:T(128)S(1)}, s32[1]{0:T(128)}, s32[]{:T(128)}) while((s32[]{:T(128)}, f32[32,11,8,8,8]{0,4,3,2,1:T(8,128)S(1)}, s32[2,3]{1,0:T(2,128)S(1)}, ...), condition=%wide.while_cond.21, body=%wide.while_body.21.sunk | while | flops 533 | bytes 5359 | solution.py:168
  561.0 15.6 %while.49 = (s32[]{:T(128)}, f32[32,11,8,8,8]{0,4,3,2,1:T(8,128)S(1)}, s32[2,3]{1,0:T(2,128)S(1)}, f32[2,32,1,8,1]{1,0,4,3,2:T(2,128)S(1)}, s32[]{:T(128)}, /*index=5*/s32[5]{0:T(128)S(1)}, s32[1]{0:T(128)}, s32[]{:T(128)}) while((s32[]{:T(128)}, f32[32,11,8,8,8]{0,4,3,2,1:T(8,128)S(1)}, s32[2,3]{1,0:T(2,128)S(1)}, ...), condition=%wide.while_cond.23, body=%wide.while_body.23.sunk | while | flops 533 | bytes 5359 | solution.py:168
  576.6 19.8 %while.50 = (s32[]{:T(128)}, f32[32,11,8,8,8]{0,4,3,2,1:T(8,128)S(1)}, s32[2,4]{1,0:T(2,128)S(1)}, f32[2,32,1,1,1]{1,4,3,2,0:T(1,128)S(1)}, s32[]{:T(128)}, /*index=5*/s32[5]{0:T(128)S(1)}, s32[1]{0:T(128)}, s32[]{:T(128)}) while((s32[]{:T(128)}, f32[32,11,8,8,8]{0,4,3,2,1:T(8,128)S(1)}, s32[2,4]{1,0:T(2,128)S(1)}, ...), condition=%wide.while_cond.24, body=%wide.while_body.24.sunk | while | flops 85 | bytes 899 | solution.py:168
  608.2 19.5 %while.52 = (s32[]{:T(128)}, f32[32,11,8,8,8]{0,4,3,2,1:T(8,128)S(1)}, s32[2,4]{1,0:T(2,128)S(1)}, f32[2,32,1,1,1]{1,4,3,2,0:T(1,128)S(1)}, s32[]{:T(128)}, /*index=5*/s32[5]{0:T(128)S(1)}, s32[1]{0:T(128)}, s32[]{:T(128)}) while((s32[]{:T(128)}, f32[32,11,8,8,8]{0,4,3,2,1:T(8,128)S(1)}, s32[2,4]{1,0:T(2,128)S(1)}, ...), condition=%wide.while_cond.26, body=%wide.while_body.26.sunk | while | flops 85 | bytes 899 | solution.py:168
  680.2 173.4 %all-reduce.45.cloned.1.call-done = f32[864,128]{1,0:T(8,128)} async-done(((f32[864,128]{1,0:T(8,128)}), f32[864,128]{1,0:T(8,128)}) %all-reduce.45.cloned.1.call-update) | async-done | bytes 442384 | tf_op jit(solution)/shard_map/psum | solution.py:225
  (704 shorter events, 685.6 us)
Async XLA Ops:
  7.2 117.1 %reduce-scatter.2.cloned.1.call-start = ((), (), s32[]{:S(2)}) async-start(), calls=%async_computation.1 | async-start | bytes 655360 | tf_op jit(solution)/shard_map/reduce_scatter | solution.py:196
  22.0 34.6 %collective-permute-start.2 = (bf16[32,1,512]{2,0,1:T(8,128)(2,1)S(1)}, bf16[32,1,512]{2,0,1:T(8,128)(2,1)S(1)}, u32[]{:S(2)}, u32[]{:S(2)}) collective-permute-start(bf16[32,1,512]{2,0,1:T(8,128)(2,1)S(1)} %get-tuple-element.826), channel_id=1, source_target_pairs={{0,12},{4,16},{8,20},{12,24},{16,28},{20,32},{24,36},{28,40},{32,4... | collective-permute-start | bytes 98312 | tf_op jit(solution)/shard_map/ppermute | solution.py:27
  33.0 21.0 %collective-permute-start = (bf16[32,1,512]{2,0,1:T(8,128)(2,1)S(1)}, bf16[32,1,512]{2,0,1:T(8,128)(2,1)S(1)}, u32[]{:S(2)}, u32[]{:S(2)}) collective-permute-start(bf16[32,1,512]{2,0,1:T(8,128)(2,1)S(1)} %get-tuple-element.832), channel_id=1, source_target_pairs={{0,20},{4,24},{8,28},{12,32},{16,36},{20,40},{24,44},{28,48},{32,5... | collective-permute-start | bytes 98312 | tf_op jit(solution)/shard_map/ppermute | solution.py:27
  39.7 15.5 %collective-permute-start.1 = (bf16[32,1,512]{2,0,1:T(8,128)(2,1)S(1)}, bf16[32,1,512]{2,0,1:T(8,128)(2,1)S(1)}, u32[]{:S(2)}, u32[]{:S(2)}) collective-permute-start(bf16[32,1,512]{2,0,1:T(8,128)(2,1)S(1)} %get-tuple-element.831), channel_id=1, source_target_pairs={{0,16},{4,20},{8,24},{12,28},{16,32},{20,36},{24,40},{28,44},{32,4... | collective-permute-start | bytes 98312 | tf_op jit(solution)/shard_map/ppermute | solution.py:27
  43.7 14.2 %collective-permute-start.3 = (bf16[32,1,512]{2,0,1:T(8,128)(2,1)S(1)}, bf16[32,1,512]{2,0,1:T(8,128)(2,1)S(1)}, u32[]{:S(2)}, u32[]{:S(2)}) collective-permute-start(bf16[32,1,512]{2,0,1:T(8,128)(2,1)S(1)} %get-tuple-element.827), channel_id=1, source_target_pairs={{0,4},{4,8},{8,12},{12,16},{16,20},{20,24},{24,28},{28,32},{32,36}... | collective-permute-start | bytes 98312 | tf_op jit(solution)/shard_map/ppermute | solution.py:27
  47.7 10.2 %collective-permute-start.4 = (bf16[32,1,512]{2,0,1:T(8,128)(2,1)S(1)}, bf16[32,1,512]{2,0,1:T(8,128)(2,1)S(1)}, u32[]{:S(2)}, u32[]{:S(2)}) collective-permute-start(bf16[32,1,512]{2,0,1:T(8,128)(2,1)S(1)} %get-tuple-element.828), channel_id=1, source_target_pairs={{4,0},{8,4},{12,8},{16,12},{20,16},{24,20},{28,24},{32,28},{36,32}... | collective-permute-start | bytes 98312 | tf_op jit(solution)/shard_map/ppermute | solution.py:27
  53.9 6.7 collective-permute-start.5
  55.3 7.4 collective-permute-start.6
  56.6 8.6 collective-permute-start.7
  95.3 758.3 %all-reduce.45.cloned.1.call-start = ((), (), s32[]{:S(2)}) async-start(), calls=%async_computation.2 | async-start | bytes 884736 | tf_op jit(solution)/shard_map/psum | solution.py:225
  417.1 159.5 %copy-start.17 = (f32[32,2,1,1,1]{0,1,4,3,2:T(2,128)S(1)}, f32[32,2,1,1,1]{0,1,4,3,2:T(2,128)}, u32[]{:S(2)}) copy-start(f32[32,2,1,1,1]{0,1,4,3,2:T(2,128)} %get-tuple-element.795) | copy-start | bytes 772
  417.1 159.5 %copy-start.23 = (s32[2,4]{1,0:T(2,128)S(1)}, s32[2,4]{1,0:T(2,128)}, u32[]{:S(2)}) copy-start(s32[2,4]{1,0:T(2,128)} %get-tuple-element.2284) | copy-start | bytes 100
  432.0 164.4 %copy-start.7 = (f32[2,32,1,1,8]{1,0,4,3,2:T(2,128)S(1)}, f32[2,32,1,1,8]{1,0,4,3,2:T(2,128)}, u32[]{:S(2)}) copy-start(f32[2,32,1,1,8]{1,0,4,3,2:T(2,128)} %get-tuple-element.2309) | copy-start | bytes 6148
  432.0 164.4 %copy-start.25 = (s32[2,3]{1,0:T(2,128)S(1)}, s32[2,3]{1,0:T(2,128)}, u32[]{:S(2)}) copy-start(s32[2,3]{1,0:T(2,128)} %concatenate.171) | copy-start | bytes 76
  432.0 176.1 %copy-start.16 = (f32[32,2,1,1,1]{0,1,4,3,2:T(2,128)S(1)}, f32[32,2,1,1,1]{0,1,4,3,2:T(2,128)}, u32[]{:S(2)}) copy-start(f32[32,2,1,1,1]{0,1,4,3,2:T(2,128)} %get-tuple-element.794) | copy-start | bytes 772
  432.0 176.1 %copy-start.22 = (s32[2,4]{1,0:T(2,128)S(1)}, s32[2,4]{1,0:T(2,128)}, u32[]{:S(2)}) copy-start(s32[2,4]{1,0:T(2,128)} %get-tuple-element.2329) | copy-start | bytes 100
  628.7 18.0 %collective-permute-start.8 = (bf16[32,1,512]{0,2,1:T(8,128)(2,1)S(1)}, bf16[32,1,512]{0,2,1:T(8,128)(2,1)S(1)}, u32[]{:S(2)}, u32[]{:S(2)}) collective-permute-start(bf16[32,1,512]{0,2,1:T(8,128)(2,1)S(1)} %get-tuple-element.793), channel_id=1, source_target_pairs={{20,0},{24,4},{28,8},{32,12},{36,16},{40,20},{44,24},{48,28},{52,3... | collective-permute-start | bytes 98312 | tf_op jit(solution)/shard_map/ppermute | solution.py:27
  630.1 22.2 %collective-permute-start.9 = (bf16[32,1,512]{0,2,1:T(8,128)(2,1)S(1)}, bf16[32,1,512]{0,2,1:T(8,128)(2,1)S(1)}, u32[]{:S(2)}, u32[]{:S(2)}) collective-permute-start(bf16[32,1,512]{0,2,1:T(8,128)(2,1)S(1)} %get-tuple-element.792), channel_id=1, source_target_pairs={{16,0},{20,4},{24,8},{28,12},{32,16},{36,20},{40,24},{44,28},{48,3... | collective-permute-start | bytes 98312 | tf_op jit(solution)/shard_map/ppermute | solution.py:27
  631.4 25.0 %collective-permute-start.10 = (bf16[32,1,512]{0,2,1:T(8,128)(2,1)S(1)}, bf16[32,1,512]{0,2,1:T(8,128)(2,1)S(1)}, u32[]{:S(2)}, u32[]{:S(2)}) collective-permute-start(bf16[32,1,512]{0,2,1:T(8,128)(2,1)S(1)} %get-tuple-element.791), channel_id=1, source_target_pairs={{12,0},{16,4},{20,8},{24,12},{28,16},{32,20},{36,24},{40,28},{44,3... | collective-permute-start | bytes 98312 | tf_op jit(solution)/shard_map/ppermute | solution.py:27
  633.2 38.8 %collective-permute-start.11 = (bf16[32,1,512]{0,2,1:T(8,128)(2,1)}, bf16[32,1,512]{0,2,1:T(8,128)(2,1)}, u32[]{:S(2)}, u32[]{:S(2)}) collective-permute-start(bf16[32,1,512]{0,2,1:T(8,128)(2,1)} %get-tuple-element.790), channel_id=1, source_target_pairs={{4,0},{8,4},{12,8},{16,12},{20,16},{24,20},{28,24},{32,28},{36,32}... | collective-permute-start | bytes 98312 | tf_op jit(solution)/shard_map/ppermute | solution.py:27
  639.4 33.7 %collective-permute-start.12 = (bf16[32,1,512]{0,2,1:T(8,128)(2,1)}, bf16[32,1,512]{0,2,1:T(8,128)(2,1)}, u32[]{:S(2)}, u32[]{:S(2)}) collective-permute-start(bf16[32,1,512]{0,2,1:T(8,128)(2,1)} %get-tuple-element.789), channel_id=1, source_target_pairs={{0,4},{4,8},{8,12},{12,16},{16,20},{20,24},{24,28},{28,32},{32,36}... | collective-permute-start | bytes 98312 | tf_op jit(solution)/shard_map/ppermute | solution.py:27
  646.7 27.4 %collective-permute-start.13 = (bf16[32,1,512]{0,2,1:T(8,128)(2,1)}, bf16[32,1,512]{0,2,1:T(8,128)(2,1)}, u32[]{:S(2)}, u32[]{:S(2)}) collective-permute-start(bf16[32,1,512]{0,2,1:T(8,128)(2,1)} %get-tuple-element.788), channel_id=1, source_target_pairs={{0,12},{4,16},{8,20},{12,24},{16,28},{20,32},{24,36},{28,40},{32,4... | collective-permute-start | bytes 98312 | tf_op jit(solution)/shard_map/ppermute | solution.py:27
  652.3 22.9 %collective-permute-start.14 = (bf16[32,1,512]{0,2,1:T(8,128)(2,1)S(1)}, bf16[32,1,512]{0,2,1:T(8,128)(2,1)}, u32[]{:S(2)}, u32[]{:S(2)}) collective-permute-start(bf16[32,1,512]{0,2,1:T(8,128)(2,1)S(1)} %get-tuple-element.787), channel_id=1, source_target_pairs={{0,16},{4,20},{8,24},{12,28},{16,32},{20,36},{24,40},{28,44},{32,4... | collective-permute-start | bytes 98312 | tf_op jit(solution)/shard_map/ppermute | solution.py:27
  656.4 19.8 %collective-permute-start.15 = (bf16[32,1,512]{0,2,1:T(8,128)(2,1)S(1)}, bf16[32,1,512]{0,2,1:T(8,128)(2,1)}, u32[]{:S(2)}, u32[]{:S(2)}) collective-permute-start(bf16[32,1,512]{0,2,1:T(8,128)(2,1)S(1)} %get-tuple-element.786), channel_id=1, source_target_pairs={{0,20},{4,24},{8,28},{12,32},{16,36},{20,40},{24,44},{28,48},{32,5... | collective-permute-start | bytes 98312 | tf_op jit(solution)/shard_map/ppermute | solution.py:27
  (28 other events, 1746.4 us)
Sparse Core Ops, SparseCore 0:
  95.5 28.7 reduce-scatter.1
  665.0 188.5 all-reduce.44
where the time goes:
time: 870 us; the launch traced here: 862 us
  local copies, waits for them, and re-layouts  328 us (38%)
  other arithmetic  229 us (26%)
  waiting for transfers between devices  204 us (23%)
  starting transfers between devices  54.4 us (6%)
  between operations  31.2 us (4%)
  blocking collectives  10.5 us (1%)
    scatter-add x208, local copies, waits for them, and re-layouts  267 us
    scatter-add x104, other arithmetic  212 us
    psum x1, waiting for transfers between devices, on_device(): lax.psum(grad_weight, 'space') * grad_scale  173 us
    ppermute x16, starting transfers between devices, passed_along(): return lax.ppermute(shard, axis, pairs)  54.3 us
    reduce_scatter x1, waiting for transfers between devices, on_device(): lax.psum_scatter(interior(jnp.einsum('rc,rbt->cbt', picked, stacked, pref...  18.5 us
  transfers between devices with their start and end apart: 18, of which 7 were waited for; matrix products, arithmetic and copies ran while one was open for 4% of the time, Pallas kernels for 0%

commit v1 on v0

v1 whole, which is shorter than its diff:
```python
import math

import jax
import jax.numpy as jnp
from jax import lax
from jax.experimental import pallas as pl
from jax.experimental.pallas import tpu as pltpu
from jax.sharding import PartitionSpec as P

BF = jnp.bfloat16
F32 = jnp.float32
SIDE = {-1: slice(7, 8), 0: slice(0, 8), 1: slice(0, 1)}
RIM = {-1: slice(0, 1), 0: slice(1, 9), 1: slice(9, 10)}
PLANAR = [(a, b) for a in (-1, 0, 1) for b in (-1, 0, 1)]
MOVES = [m for m in PLANAR if m != (0, 0)]
DW_ROWS = 28 * 32


def slot_of(dx, dy, dz):
    linear = (dx + 1) * 9 + (dy + 1) * 3 + dz + 1
    return linear if linear < 13 else linear - 1


def planar_slots(dx, dy):
    return [None if (dx, dy, dz) == (0, 0, 0) else slot_of(dx, dy, dz) for dz in (-1, 0, 1)]


def tiles(ref_or_value, dx, dy):
    part = ref_or_value[SIDE[dx], SIDE[dy]]
    return part.reshape(-1, 8, 128)


def rims_kernel(send, mask, gathered, local, to_b, face_a):
    for brick in range(2):
        rows = gathered[:, 0, brick].reshape(128, 512).astype(F32) * mask[brick : brick + 1, :]
        local[brick] = rows.T.reshape(8, 8, 8, 128)

    def chosen(move):
        s = send[MOVES.index(move)]
        first, second = (tiles(local[brick], *move) for brick in range(2))
        return jnp.where(s == 0, first, jnp.where(s == 1, second, 0.0))

    for i, b in enumerate((-1, 1)):
        parts = [chosen((0, b)), chosen((-1, b)), chosen((1, b))]
        to_b[i] = jnp.concatenate(parts, axis=0).reshape(80, 128).astype(BF)
    for i, a in enumerate((-1, 1)):
        face_a[i] = chosen((a, 0)).reshape(64, 128).astype(BF)


def main_kernel(
    near, chan, mask, local, from_bm, from_bp, from_am, from_ap, gathered, weights, own_weights,
    act_out, dw_out, own_out, ret_a, ret_b,
    blocks, grads, own_block, act_all, terms,
):
    z = lax.broadcasted_iota(jnp.int32, (1, 8, 128), 1)
    from_b = {-1: from_bm, 1: from_bp}
    from_a = {-1: from_am, 1: from_ap}

    def arrived(dx, dy):
        if dx == 0:
            return from_b[dy][0:64].astype(F32).reshape(8, 8, 128)
        if dy == 0:
            return from_a[dx][0:64].astype(F32).reshape(8, 8, 128)
        edges = from_a[dx][64:80].astype(F32).reshape(2, 8, 128)
        return edges[0:1] if dy == -1 else edges[1:2]

    for dx, dy in PLANAR:
        options = [tiles(local[0], dx, dy), tiles(local[1], dx, dy)]
        rows = [0, 1]
        if (dx, dy) != (0, 0):
            options.append(arrived(dx, dy))
            rows.append(2 + MOVES.index((dx, dy)))

        def pick(r):
            value = 0.0
            for row, option in zip(rows, options):
                value = jnp.where(r == row, option, value)
            return value

        shifted = [[], [], []]
        for brick in range(2):
            below, level, above = planar_slots(dx, dy)
            center = options[brick] if level is None else pick(near[brick, level])
            under, over = pick(near[brick, below]), pick(near[brick, above])
            shifted[0].append(pltpu.roll(jnp.where(z == 7, under, center), 1, 1))
            shifted[1].append(center)
            shifted[2].append(pltpu.roll(jnp.where(z == 0, over, center), 7, 1))
        for i in range(3):
            both = jnp.stack(shifted[i], axis=1)
            count = both.shape[0]
            nx = 8 if dx == 0 else 1
            blocks[i, RIM[dx], RIM[dy]] = both.reshape(nx, count // nx, 16, 128).astype(BF)

    pre = jnp.zeros((1024, 128), F32)
    for dx in range(3):
        left = jnp.concatenate(
            [
                blocks[dz, dx : dx + 8, dy : dy + 8].reshape(1024, 128)
                for dy in range(3)
                for dz in range(3)
            ],
            axis=1,
        )
        right = jnp.concatenate([weights[:, 9 * dx + o].reshape(128, 128) for o in range(9)], axis=0)
        pre = pre + jnp.dot(left, right, preferred_element_type=F32)
    pre = pre.reshape(64, 2, 8, 128)

    back = []
    for brick in range(2):
        on = mask[brick : brick + 1, :]
        pre_act = pre[:, brick].reshape(512, 128).T * on
        gate = jax.nn.sigmoid(pre_act)
        act_all[brick] = (pre_act * gate).astype(BF)
        cotangent = gathered[:, 1, brick].reshape(128, 512).astype(F32)
        grad = cotangent * on * gate * (1.0 + pre_act * (1.0 - gate))
        back.append(grad.T.reshape(64, 8, 128))
    start = pl.multiple_of(chan[0] * 32, 32)
    for brick in range(2):
        act_out[brick] = act_all[brick, pl.ds(start, 32), :]
    back = jnp.stack(back, axis=1).reshape(1024, 128)
    grads[...] = jnp.zeros(grads.shape, BF)
    grads[2:10, 2:10] = back.astype(BF).reshape(8, 8, 16, 128)
    back_t = back.T.astype(BF)

    row = lax.broadcasted_iota(jnp.int32, (384, 128), 0)
    column = lax.broadcasted_iota(jnp.int32, (384, 128), 1)
    wanted = (row >> 7 == column >> 5) & ((row & 127) == chan[0] * 32 + (column & 31))
    select = jnp.where(wanted, 1.0, 0.0).astype(BF)
    stacked = jnp.concatenate([blocks[dz].reshape(1600, 128) for dz in range(3)], axis=1)
    own_block[...] = (
        jnp.dot(stacked, select, preferred_element_type=F32).astype(BF).reshape(10, 10, 16, 128)
    )
    for i, (dx, dy) in enumerate(PLANAR):
        window = own_block[dx + 1 : dx + 9, dy + 1 : dy + 9].reshape(1024, 128)
        product = jnp.dot(back_t, window, preferred_element_type=F32)
        dw_out[96 * i : 96 * i + 96] = product.T[0:96].astype(BF)
    dw_out[864:896] = jnp.zeros((32, 128), BF)

    spread = jnp.zeros((1600, 128), F32)
    for dx in (-1, 0, 1):
        left = jnp.concatenate(
            [
                grads[1 - dx : 11 - dx, 1 - dy : 11 - dy].reshape(1600, 128)
                for dy in (-1, 0, 1)
            ],
            axis=1,
        )
        rights = []
        for dy in (-1, 0, 1):
            first = (dx + 1) * 9 + (dy + 1) * 3
            piece = own_weights[first : first + 3].reshape(96, 128).astype(F32)
            piece = jnp.concatenate([piece, jnp.zeros((32, 128), F32)], axis=0)
            rights.append(piece.T.astype(BF))
        spread = spread + jnp.dot(left, jnp.concatenate(rights, axis=0), preferred_element_type=F32)
    spread = spread.reshape(100, 2, 8, 128)
    for brick in range(2):
        part = spread[:, brick]
        up = pltpu.roll(part, 7, 1)
        down = pltpu.roll(pltpu.roll(part, 64, 2), 1, 1)
        center = (
            pltpu.roll(part, 96, 2) + jnp.where(z < 7, up, 0.0) + jnp.where(z > 0, down, 0.0)
        )
        terms[0, brick] = jnp.where(z == 7, up, 0.0).reshape(10, 10, 8, 128)
        terms[1, brick] = center.reshape(10, 10, 8, 128)
        terms[2, brick] = jnp.where(z == 0, down, 0.0).reshape(10, 10, 8, 128)
    for brick in range(2):
        own_out[brick] = terms[1, brick, 1:9, 1:9]
    edges = {}
    for dx, dy in PLANAR:
        pieces = [
            (near[brick, slot], terms[i, brick, RIM[dx], RIM[dy]])
            for brick in range(2)
            for i, slot in enumerate(planar_slots(dx, dy))
            if slot is not None
        ]

        def collected(target):
            total = 0.0
            for r, piece in pieces:
                total = total + jnp.where(r == target, piece, 0.0)
            return total

        for brick in range(2):
            own_out[brick, SIDE[dx], SIDE[dy]] += collected(brick)
        if (dx, dy) != (0, 0):
            edges[dx, dy] = collected(2 + MOVES.index((dx, dy))).reshape(-1, 8, 128)
    for i, a in enumerate((-1, 1)):
        parts = [edges[a, 0], edges[a, -1], edges[a, 1]]
        ret_a[i] = jnp.concatenate(parts, axis=0).reshape(80, 128).astype(BF)
    for i, b in enumerate((-1, 1)):
        ret_b[i] = edges[0, b].reshape(64, 128).astype(BF)


def final_kernel(send, mask, own, from_am, from_ap, from_bm, from_bp, out, total):
    total[...] = own[...]
    from_a = {-1: from_am, 1: from_ap}
    from_b = {-1: from_bm, 1: from_bp}
    for dx, dy in MOVES:
        s = send[MOVES.index((dx, dy))]
        if dy == 0:
            piece = from_a[dx][0:64].astype(F32).reshape(1, 8, 8, 128)
        elif dx == 0:
            piece = from_b[dy][0:64].astype(F32).reshape(8, 1, 8, 128)
        else:
            both = from_b[dy][64:80].astype(F32).reshape(2, 1, 1, 8, 128)
            piece = both[0] if dx == -1 else both[1]
        for brick in range(2):
            total[brick, SIDE[dx], SIDE[dy]] += jnp.where(s == brick, piece, 0.0)
    for brick in range(2):
        rows = total[brick].reshape(512, 128).T[0:32] * mask[brick : brick + 1, :]
        out[brick] = rows.astype(BF)


SMEM = pl.BlockSpec(memory_space=pltpu.SMEM)
VMEM = pl.BlockSpec(memory_space=pltpu.VMEM)


def call(kernel, name, smem, vmem, outs, scratch, limit):
    shapes = [jax.ShapeDtypeStruct(s, d) for s, d in outs]
    return pl.pallas_call(
        kernel,
        out_shape=shapes,
        in_specs=[SMEM] * len(smem) + [VMEM] * len(vmem),
        out_specs=[VMEM] * len(outs),
        scratch_shapes=[pltpu.VMEM(s, d) for s, d in scratch],
        compiler_params=pltpu.CompilerParams(vmem_limit_bytes=limit << 20),
        name=name,
    )(*smem, *vmem)


def passed_along(shard, by):
    count = lax.axis_size("space")
    pairs = [(i, i + by) for i in range(count) if 0 <= i + by < count]
    return lax.ppermute(shard, "space", pairs)


def unpack_mask(packed):
    shifts = jnp.arange(32, dtype=jnp.int32)
    bits = lax.shift_right_logical(packed[:, :, None], shifts[None, None, :]) & 1
    return bits.reshape(packed.shape[0], packed.shape[1] * 32).astype(F32)


def summed_over_space(part, scale):
    count = lax.axis_size("space")
    inner = 16 if count == 128 else count // 2
    outer = count // inner
    near = [[j * inner + i for i in range(inner)] for j in range(outer)]
    far = [[j * inner + i for j in range(outer)] for i in range(inner)]
    rows = DW_ROWS // inner

    def exchange(values, groups):
        return lax.all_to_all(values, "space", 0, 0, tiled=True, axis_index_groups=groups)

    mine = exchange(part, near).astype(F32).reshape(inner, rows, 128).sum(0)
    mine = exchange(jnp.tile(mine, (outer, 1)), far).reshape(outer, rows, 128).sum(0)
    mine = (mine * scale).astype(BF)
    return exchange(jnp.tile(mine, (inner, 1)), near)


def on_device(features, mask_packed, neighbours, send_list, weights, cotangent):
    chan = lax.axis_index("chan").astype(jnp.int32).reshape(1)
    send = send_list.reshape(8)
    mask = unpack_mask(mask_packed)
    values = jnp.stack([features.transpose(1, 0, 2), cotangent.transpose(1, 0, 2)])
    gathered = lax.all_gather(values, "chan", axis=0)
    all_weights = lax.all_gather(weights, "chan", axis=0)
    local, to_b, face_a = call(
        rims_kernel, "rims", [send], [mask, gathered],
        [((2, 8, 8, 8, 128), F32), ((2, 80, 128), BF), ((2, 64, 128), BF)], [], 16,
    )
    from_bm, from_bp = passed_along(to_b[0], 1), passed_along(to_b[1], -1)
    to_am = jnp.concatenate([face_a[0], from_bm[64:72], from_bp[64:72]], axis=0)
    to_ap = jnp.concatenate([face_a[1], from_bm[72:80], from_bp[72:80]], axis=0)
    from_am, from_ap = passed_along(to_am, 4), passed_along(to_ap, -4)
    act, dw, own, ret_a, ret_b = call(
        main_kernel, "conv", [neighbours, chan],
        [mask, local, from_bm, from_bp, from_am, from_ap, gathered, all_weights, weights],
        [
            ((2, 32, 512), BF), ((DW_ROWS, 128), BF), ((2, 8, 8, 8, 128), F32),
            ((2, 80, 128), BF), ((2, 64, 128), BF),
        ],
        [
            ((3, 10, 10, 16, 128), BF), ((12, 12, 16, 128), BF), ((10, 10, 16, 128), BF),
            ((2, 128, 512), BF), ((3, 2, 10, 10, 8, 128), F32),
        ],
        40,
    )
    back_am, back_ap = passed_along(ret_a[0], -4), passed_along(ret_a[1], 4)
    to_bm = jnp.concatenate([ret_b[0], back_am[64:72], back_ap[64:72]], axis=0)
    to_bp = jnp.concatenate([ret_b[1], back_am[72:80], back_ap[72:80]], axis=0)
    back_bm, back_bp = passed_along(to_bm, -1), passed_along(to_bp, 1)
    scale = 1.0 / math.sqrt(2 * lax.axis_size("space") * 512)
    grad_weights = summed_over_space(dw, scale)[:864].astype(F32).reshape(27, 32, 128)
    (grad,) = call(
        final_kernel, "grad", [send], [mask, own, back_am, back_ap, back_bm, back_bp],
        [((2, 32, 512), BF)], [((2, 8, 8, 8, 128), F32)], 16,
    )
    return act.transpose(1, 0, 2), grad.transpose(1, 0, 2), grad_weights


def solution(mesh):
    return jax.shard_map(
        on_device,
        mesh=mesh,
        in_specs=(
            P("chan", "space", None),
            P("space", None),
            P("space", None),
            P("space", None, None),
            P(None, "chan", None),
            P("chan", "space", None),
        ),
        out_specs=(P("chan", "space", None), P("chan", "space", None), P(None, "chan", None)),
        check_vma=False,
    )
```

time: 870 us -> 119 us (0.14)
  local copies, waits for them, and re-layouts: 328 us -> 5.93 us
  other arithmetic: 229 us -> 0.92 us
  waiting for transfers between devices: 204 us -> 22.1 us
  between operations: 31.2 us -> 0.87 us
  blocking collectives: 10.5 us -> 23.4 us
    scatter-add x208 -> x0, local copies, waits for them, and re-layouts: 267 us -> none
    scatter-add x105 -> x0, other arithmetic: 213 us -> none
    psum x1 -> x0, waiting for transfers between devices: 173 us -> none  [on_device(): lax.psum(grad_weight, 'space') * grad_scale]
    all_to_all x0 -> x3, starting transfers between devices: none -> 28.5 us  [exchange(): lax.all_to_all(values, 'space', 0, 0, tiled=True, axis_index_groups=groups)]
    ppermute x16 -> x8, starting transfers between devices: 54.3 us -> 27.4 us  [passed_along(): return lax.ppermute(shard, 'space', pairs)]
    all_to_all x0 -> x3, waiting for transfers between devices: none -> 19.4 us  [exchange(): lax.all_to_all(values, 'space', 0, 0, tiled=True, axis_index_groups=groups)]
    reduce_scatter x1 -> x0, waiting for transfers between devices: 18.5 us -> none  [on_device(): lax.psum_scatter(interior(jnp.einsum('rc,rbt->cbt', picked, stacked, pref...]
    gather x26 -> x0, local copies, waits for them, and re-layouts: 14.3 us -> none  [assemble(): jnp.take(source_table, indices[:, neighbour_slot(along_x, along_y, along_...]
  transfers between devices with their start and end apart: 18 -> 11, of which waited for: 7 -> 5; matrix products, arithmetic and copies ran while one was open for 4% -> 3% of each run, Pallas kernels for 0% -> 1%
where the time goes in v1:
time: 119 us; the launch traced here: 117 us
  starting transfers between devices  55.8 us (47%)
  blocking collectives  23.4 us (20%)
  waiting for transfers between devices  22.1 us (19%)
  Pallas kernels  7.87 us (7%)
  local copies, waits for them, and re-layouts  5.93 us (5%)
    all_to_all x3, starting transfers between devices, exchange(): lax.all_to_all(values, 'space', 0, 0, tiled=True, axis_index_groups=groups)  28.5 us
    ppermute x8, starting transfers between devices, passed_along(): return lax.ppermute(shard, 'space', pairs)  27.4 us
    all_to_all x3, waiting for transfers between devices, exchange(): lax.all_to_all(values, 'space', 0, 0, tiled=True, axis_index_groups=groups)  19.4 us
    all_gather x1, blocking collectives, on_device(): all_weights = lax.all_gather(weights, 'chan', axis=0)  12.3 us
    all_gather x1, blocking collectives, on_device(): gathered = lax.all_gather(values, 'chan', axis=0)  11.1 us
    pallas_call x3, Pallas kernels, call(): pl.pallas_call(kernel, out_shape=shapes, in_specs=[SMEM] * len(smem) + [V...  7.87 us
    unnamed x10, local copies, waits for them, and re-layouts  3.34 us
    ppermute x8, waiting for transfers between devices, passed_along(): return lax.ppermute(shard, 'space', pairs)  2.79 us
  transfers between devices with their start and end apart: 11, of which 5 were waited for; matrix products, arithmetic and copies ran while one was open for 3% of the time, Pallas kernels for 1%

profile of v1, /device:TPU:1, one launch (start us, length us, event | category | flops | bytes accessed | tf_op | source)
XLA Modules:
  0.0 116.9 jit_solution(3710678308514186080)
XLA Ops:
  1.5 0.9 copy_bitcast_fusion
  2.4 11.1 %all-gather = bf16[8,2,32,512]{3,2,1,0:T(8,128)(2,1)S(1)} all-gather(bf16[2,2,32,512]{3,2,1,0:T(8,128)(2,1)S(1)} %pad_maximum_fusion), channel_id=2, replica_groups=mesh['space'=128,'chan'=4] {'chan'}, dimensions={0}, use_global_device_ids=true | all-gather | bytes 655360 | tf_op jit(solution)/shard_map/all_gather | solution.py:265
  14.1 0.7 rims.1
  14.9 10.6 %collective-permute-start.1 = (bf16[80,128]{1,0:T(8,128)(2,1)S(1)}, bf16[80,128]{1,0:T(8,128)(2,1)S(1)}, u32[]{:S(2)}, u32[]{:S(2)}) collective-permute-start(bf16[80,128]{1,0:T(8,128)(2,1)S(1)} %get-tuple-element.30), channel_id=1, source_target_pairs={{4,0},{8,4},{12,8},{16,12},{20,16},{24,20},{28,24},{32,28},{36,32}... | collective-permute-start | bytes 61448 | tf_op jit(solution)/shard_map/ppermute | solution.py:234
  25.5 1.9 %collective-permute-start = (bf16[80,128]{1,0:T(8,128)(2,1)S(1)}, bf16[80,128]{1,0:T(8,128)(2,1)S(1)}, u32[]{:S(2)}, u32[]{:S(2)}) collective-permute-start(bf16[80,128]{1,0:T(8,128)(2,1)S(1)} %get-tuple-element.31), channel_id=1, source_target_pairs={{0,4},{4,8},{8,12},{12,16},{16,20},{20,24},{24,28},{28,32},{32,36}... | collective-permute-start | bytes 61448 | tf_op jit(solution)/shard_map/ppermute | solution.py:234
  27.5 1.1 collective-permute-done.from_bm
  28.6 2.5 %collective-permute-start.2 = (bf16[80,128]{1,0:T(8,128)(2,1)S(1)}, bf16[80,128]{1,0:T(8,128)(2,1)S(1)}, u32[]{:S(2)}, u32[]{:S(2)}) collective-permute-start(bf16[80,128]{1,0:T(8,128)(2,1)S(1)} %pad_maximum_fusion.1), channel_id=1, source_target_pairs={{0,16},{4,20},{8,24},{12,28},{16,32},{20,36},{24,40},{28,44},{32,4... | collective-permute-start | bytes 61448 | tf_op jit(solution)/shard_map/ppermute | solution.py:234
  31.1 1.3 %collective-permute-start.3 = (bf16[80,128]{1,0:T(8,128)(2,1)S(1)}, bf16[80,128]{1,0:T(8,128)(2,1)S(1)}, u32[]{:S(2)}, u32[]{:S(2)}) collective-permute-start(bf16[80,128]{1,0:T(8,128)(2,1)S(1)} %pad_maximum_fusion.2), channel_id=1, source_target_pairs={{16,0},{20,4},{24,8},{28,12},{32,16},{36,20},{40,24},{44,28},{48,3... | collective-permute-start | bytes 61448 | tf_op jit(solution)/shard_map/ppermute | solution.py:234
  32.4 12.3 %all-gather.1 = bf16[108,32,128]{2,1,0:T(8,128)(2,1)S(1)} all-gather(bf16[27,32,128]{2,1,0:T(8,128)(2,1)S(1)} %copy-done), channel_id=3, replica_groups=mesh['space'=128,'chan'=4] {'chan'}, dimensions={0}, use_global_device_ids=true | all-gather | bytes 1105920 | tf_op jit(solution)/shard_map/all_gather | solution.py:266
  45.4 6.4 %conv.1 = (bf16[2,32,512]{2,1,0:T(8,128)(2,1)S(1)}, bf16[896,128]{1,0:T(8,128)(2,1)}, f32[2,8,8,8,128]{4,3,2,1,0:T(8,128)S(1)}, bf16[2,80,128]{2,1,0:T(8,128)(2,1)S(1)}, bf16[2,64,128]{2,1,0:T(8,128)(2,1)S(1)}) custom-call(s32[2,26]{1,0:T(2,128)S(1)} %copy-done.2, s32[1]{0:T(128)} %bitcast.chan, f32[2,512]{1,0:T(2,128)S(1)} %and_convert_fusion.mask, ...), custom_call_target="tpu_custom_call" | custom-call | tf_op jit(solution)/shard_map/conv/pallas_call | solution.py:220
  51.9 14.7 %all-to-all-start = ((bf16[16,56,128]{2,1,0:T(8,128)(2,1)}), bf16[16,56,128]{2,1,0:T(8,128)(2,1)S(1)}, u32[]{:S(2)}, u32[]{:S(2)}) async-start(bf16[16,56,128]{2,1,0:T(8,128)(2,1)} %bitcast.18), calls=%async_computation | async-start | bytes 458752 | tf_op jit(solution)/shard_map/all_to_all | solution.py:252
  66.6 4.2 %collective-permute-start.5 = (bf16[80,128]{1,0:T(8,128)(2,1)S(1)}, bf16[80,128]{1,0:T(8,128)(2,1)S(1)}, u32[]{:S(2)}, u32[]{:S(2)}) collective-permute-start(bf16[80,128]{1,0:T(8,128)(2,1)S(1)} %get-tuple-element.28), channel_id=1, source_target_pairs={{0,16},{4,20},{8,24},{12,28},{16,32},{20,36},{24,40},{28,44},{32,4... | collective-permute-start | bytes 61448 | tf_op jit(solution)/shard_map/ppermute | solution.py:234
  70.8 7.3 %all-to-all-done = bf16[16,56,128]{2,1,0:T(8,128)(2,1)S(1)} async-done(((bf16[16,56,128]{2,1,0:T(8,128)(2,1)}), bf16[16,56,128]{2,1,0:T(8,128)(2,1)S(1)}, u32[]{:S(2)}, u32[]{:S(2)}) %all-to-all-start) | async-done | bytes 229408 | tf_op jit(solution)/shard_map/all_to_all | solution.py:252
  78.8 10.1 %all-to-all-start.1 = ((f32[8,56,128]{2,1,0:T(8,128)}), f32[8,56,128]{2,1,0:T(8,128)S(1)}, u32[]{:S(2)}, u32[]{:S(2)}) async-start(f32[8,56,128]{2,1,0:T(8,128)} %tile.4), calls=%async_computation.1 | async-start | bytes 458752 | tf_op jit(solution)/shard_map/all_to_all | solution.py:252
  88.9 1.3 %collective-permute-start.4 = (bf16[80,128]{1,0:T(8,128)(2,1)S(1)}, bf16[80,128]{1,0:T(8,128)(2,1)S(1)}, u32[]{:S(2)}, u32[]{:S(2)}) collective-permute-start(bf16[80,128]{1,0:T(8,128)(2,1)S(1)} %get-tuple-element.29), channel_id=1, source_target_pairs={{16,0},{20,4},{24,8},{28,12},{32,16},{36,20},{40,24},{44,28},{48,3... | collective-permute-start | bytes 61448 | tf_op jit(solution)/shard_map/ppermute | solution.py:234
  90.2 10.3 %all-to-all-done.1 = f32[8,56,128]{2,1,0:T(8,128)S(1)} async-done(((f32[8,56,128]{2,1,0:T(8,128)}), f32[8,56,128]{2,1,0:T(8,128)S(1)}, u32[]{:S(2)}, u32[]{:S(2)}) %all-to-all-start.1) | async-done | bytes 229408 | tf_op jit(solution)/shard_map/all_to_all | solution.py:252
  100.5 0.7 tile.5
  101.2 3.7 %all-to-all-start.2 = ((bf16[16,56,128]{2,1,0:T(8,128)(2,1)}), bf16[16,56,128]{2,1,0:T(8,128)(2,1)S(1)}, u32[]{:S(2)}, u32[]{:S(2)}) async-start(bf16[16,56,128]{2,1,0:T(8,128)(2,1)} %tile.5), calls=%async_computation.2 | async-start | bytes 458752 | tf_op jit(solution)/shard_map/all_to_all | solution.py:252
  105.0 2.1 %collective-permute-start.6 = (bf16[80,128]{1,0:T(8,128)(2,1)S(1)}, bf16[80,128]{1,0:T(8,128)(2,1)S(1)}, u32[]{:S(2)}, u32[]{:S(2)}) collective-permute-start(bf16[80,128]{1,0:T(8,128)(2,1)S(1)} %pad_maximum_fusion.3), channel_id=1, source_target_pairs={{4,0},{8,4},{12,8},{16,12},{20,16},{24,20},{28,24},{32,28},{36,32}... | collective-permute-start | bytes 61448 | tf_op jit(solution)/shard_map/ppermute | solution.py:234
  107.1 3.4 %collective-permute-start.7 = (bf16[80,128]{1,0:T(8,128)(2,1)S(1)}, bf16[80,128]{1,0:T(8,128)(2,1)S(1)}, u32[]{:S(2)}, u32[]{:S(2)}) collective-permute-start(bf16[80,128]{1,0:T(8,128)(2,1)S(1)} %pad_maximum_fusion.4), channel_id=1, source_target_pairs={{0,4},{4,8},{8,12},{12,16},{16,20},{20,24},{24,28},{28,32},{32,36}... | collective-permute-start | bytes 61448 | tf_op jit(solution)/shard_map/ppermute | solution.py:234
  111.2 1.7 %collective-permute-done.6.from_bm = bf16[80,128]{1,0:T(8,128)(2,1)S(1)} collective-permute-done((bf16[80,128]{1,0:T(8,128)(2,1)S(1)}, bf16[80,128]{1,0:T(8,128)(2,1)S(1)}, u32[]{:S(2)}, u32[]{:S(2)}) %collective-permute-start.6) | collective-permute-done | bytes 20512 | tf_op jit(solution)/shard_map/ppermute | solution.py:234
  112.9 0.7 grad.1
  114.3 1.8 %all-to-all-done.2 = bf16[16,56,128]{2,1,0:T(8,128)(2,1)S(1)} async-done(((bf16[16,56,128]{2,1,0:T(8,128)(2,1)}), bf16[16,56,128]{2,1,0:T(8,128)(2,1)S(1)}, u32[]{:S(2)}, u32[]{:S(2)}) %all-to-all-start.2) | async-done | bytes 229408 | tf_op jit(solution)/shard_map/all_to_all | solution.py:252
  116.1 0.8 convert.1
  (39 shorter events, 4.4 us)
Async XLA Ops:
  0.6 0.7 copy-start.3
  13.5 0.7 copy-start.1
  14.9 17.6 %copy-start = (bf16[27,32,128]{2,1,0:T(8,128)(2,1)S(1)}, bf16[27,32,128]{2,1,0:T(8,128)(2,1)}, u32[]{:S(2)}) copy-start(bf16[27,32,128]{2,1,0:T(8,128)(2,1)} %own_weights.1) | copy-start | bytes 663556
  14.9 12.6 %collective-permute-start.1 = (bf16[80,128]{1,0:T(8,128)(2,1)S(1)}, bf16[80,128]{1,0:T(8,128)(2,1)S(1)}, u32[]{:S(2)}, u32[]{:S(2)}) collective-permute-start(bf16[80,128]{1,0:T(8,128)(2,1)S(1)} %get-tuple-element.30), channel_id=1, source_target_pairs={{4,0},{8,4},{12,8},{16,12},{20,16},{24,20},{28,24},{32,28},{36,32}... | collective-permute-start | bytes 61448 | tf_op jit(solution)/shard_map/ppermute | solution.py:234
  25.5 3.1 %collective-permute-start = (bf16[80,128]{1,0:T(8,128)(2,1)S(1)}, bf16[80,128]{1,0:T(8,128)(2,1)S(1)}, u32[]{:S(2)}, u32[]{:S(2)}) collective-permute-start(bf16[80,128]{1,0:T(8,128)(2,1)S(1)} %get-tuple-element.31), channel_id=1, source_target_pairs={{0,4},{4,8},{8,12},{12,16},{16,20},{20,24},{24,28},{28,32},{32,36}... | collective-permute-start | bytes 61448 | tf_op jit(solution)/shard_map/ppermute | solution.py:234
  28.6 16.1 %collective-permute-start.2 = (bf16[80,128]{1,0:T(8,128)(2,1)S(1)}, bf16[80,128]{1,0:T(8,128)(2,1)S(1)}, u32[]{:S(2)}, u32[]{:S(2)}) collective-permute-start(bf16[80,128]{1,0:T(8,128)(2,1)S(1)} %pad_maximum_fusion.1), channel_id=1, source_target_pairs={{0,16},{4,20},{8,24},{12,28},{16,32},{20,36},{24,40},{28,44},{32,4... | collective-permute-start | bytes 61448 | tf_op jit(solution)/shard_map/ppermute | solution.py:234
  31.1 13.6 %collective-permute-start.3 = (bf16[80,128]{1,0:T(8,128)(2,1)S(1)}, bf16[80,128]{1,0:T(8,128)(2,1)S(1)}, u32[]{:S(2)}, u32[]{:S(2)}) collective-permute-start(bf16[80,128]{1,0:T(8,128)(2,1)S(1)} %pad_maximum_fusion.2), channel_id=1, source_target_pairs={{16,0},{20,4},{24,8},{28,12},{32,16},{36,20},{40,24},{44,28},{48,3... | collective-permute-start | bytes 61448 | tf_op jit(solution)/shard_map/ppermute | solution.py:234
  44.8 0.7 copy-start.2
  51.9 26.2 %all-to-all-start = ((bf16[16,56,128]{2,1,0:T(8,128)(2,1)}), bf16[16,56,128]{2,1,0:T(8,128)(2,1)S(1)}, u32[]{:S(2)}, u32[]{:S(2)}) async-start(bf16[16,56,128]{2,1,0:T(8,128)(2,1)} %bitcast.18), calls=%async_computation | async-start | bytes 458752 | tf_op jit(solution)/shard_map/all_to_all | solution.py:252
  66.6 23.6 %collective-permute-start.5 = (bf16[80,128]{1,0:T(8,128)(2,1)S(1)}, bf16[80,128]{1,0:T(8,128)(2,1)S(1)}, u32[]{:S(2)}, u32[]{:S(2)}) collective-permute-start(bf16[80,128]{1,0:T(8,128)(2,1)S(1)} %get-tuple-element.28), channel_id=1, source_target_pairs={{0,16},{4,20},{8,24},{12,28},{16,32},{20,36},{24,40},{28,44},{32,4... | collective-permute-start | bytes 61448 | tf_op jit(solution)/shard_map/ppermute | solution.py:234
  78.8 21.6 %all-to-all-start.1 = ((f32[8,56,128]{2,1,0:T(8,128)}), f32[8,56,128]{2,1,0:T(8,128)S(1)}, u32[]{:S(2)}, u32[]{:S(2)}) async-start(f32[8,56,128]{2,1,0:T(8,128)} %tile.4), calls=%async_computation.1 | async-start | bytes 458752 | tf_op jit(solution)/shard_map/all_to_all | solution.py:252
  88.9 16.1 %collective-permute-start.4 = (bf16[80,128]{1,0:T(8,128)(2,1)S(1)}, bf16[80,128]{1,0:T(8,128)(2,1)S(1)}, u32[]{:S(2)}, u32[]{:S(2)}) collective-permute-start(bf16[80,128]{1,0:T(8,128)(2,1)S(1)} %get-tuple-element.29), channel_id=1, source_target_pairs={{16,0},{20,4},{24,8},{28,12},{32,16},{36,20},{40,24},{44,28},{48,3... | collective-permute-start | bytes 61448 | tf_op jit(solution)/shard_map/ppermute | solution.py:234
  101.2 14.9 %all-to-all-start.2 = ((bf16[16,56,128]{2,1,0:T(8,128)(2,1)}), bf16[16,56,128]{2,1,0:T(8,128)(2,1)S(1)}, u32[]{:S(2)}, u32[]{:S(2)}) async-start(bf16[16,56,128]{2,1,0:T(8,128)(2,1)} %tile.5), calls=%async_computation.2 | async-start | bytes 458752 | tf_op jit(solution)/shard_map/all_to_all | solution.py:252
  105.0 7.9 %collective-permute-start.6 = (bf16[80,128]{1,0:T(8,128)(2,1)S(1)}, bf16[80,128]{1,0:T(8,128)(2,1)S(1)}, u32[]{:S(2)}, u32[]{:S(2)}) collective-permute-start(bf16[80,128]{1,0:T(8,128)(2,1)S(1)} %pad_maximum_fusion.3), channel_id=1, source_target_pairs={{4,0},{8,4},{12,8},{16,12},{20,16},{24,20},{28,24},{32,28},{36,32}... | collective-permute-start | bytes 61448 | tf_op jit(solution)/shard_map/ppermute | solution.py:234
  107.1 5.8 %collective-permute-start.7 = (bf16[80,128]{1,0:T(8,128)(2,1)S(1)}, bf16[80,128]{1,0:T(8,128)(2,1)S(1)}, u32[]{:S(2)}, u32[]{:S(2)}) collective-permute-start(bf16[80,128]{1,0:T(8,128)(2,1)S(1)} %pad_maximum_fusion.4), channel_id=1, source_target_pairs={{0,4},{4,8},{8,12},{12,16},{16,20},{20,24},{24,28},{28,32},{32,36}... | collective-permute-start | bytes 61448 | tf_op jit(solution)/shard_map/ppermute | solution.py:234

commit v2 on v1

--- a/solution.py
+++ b/solution.py
@@ -257,13 +257,19 @@
     return exchange(jnp.tile(mine, (inner, 1)), near)
 
 
+def from_all_chan(part):
+    count = lax.axis_size("chan")
+    copies = jnp.broadcast_to(part[None], (count,) + part.shape)
+    return lax.all_to_all(copies, "chan", 0, 0, tiled=True)
+
+
 def on_device(features, mask_packed, neighbours, send_list, weights, cotangent):
     chan = lax.axis_index("chan").astype(jnp.int32).reshape(1)
     send = send_list.reshape(8)
     mask = unpack_mask(mask_packed)
     values = jnp.stack([features.transpose(1, 0, 2), cotangent.transpose(1, 0, 2)])
-    gathered = lax.all_gather(values, "chan", axis=0)
-    all_weights = lax.all_gather(weights, "chan", axis=0)
+    all_weights = from_all_chan(weights)
+    gathered = from_all_chan(values)
     local, to_b, face_a = call(
         rims_kernel, "rims", [send], [mask, gathered],
         [((2, 8, 8, 8, 128), F32), ((2, 80, 128), BF), ((2, 64, 128), BF)], [], 16,

time: 119 us -> 110 us (0.924); the launches traced: 117 us -> 109 us
  blocking collectives: 23.4 us -> 0 us
  waiting for transfers between devices: 22.1 us -> 30.7 us
  starting transfers between devices: 55.8 us -> 61.7 us
    all_gather x2 -> x0, blocking collectives: 23.4 us -> none  [the longest x1 12.3 us: on_device(): all_weights = lax.all_gather(weights, 'chan', axis=0)]
    all_to_all x0 -> x2, starting transfers between devices: none -> 8.48 us  [from_all_chan(): return lax.all_to_all(copies, 'chan', 0, 0, tiled=True)]
    all_to_all x0 -> x2, waiting for transfers between devices: none -> 6.68 us  [from_all_chan(): return lax.all_to_all(copies, 'chan', 0, 0, tiled=True)]
    all_to_all x3, starting transfers between devices: 28.5 us -> 24 us  [exchange(): lax.all_to_all(values, 'space', 0, 0, tiled=True, axis_index_groups=groups)]
    ppermute x8, waiting for transfers between devices: 2.79 us -> 6.57 us  [passed_along(): return lax.ppermute(shard, 'space', pairs)]
    broadcast_in_dim x0 -> x2, local copies, waits for them, and re-layouts: none -> 1.9 us  [from_all_chan(): copies = jnp.broadcast_to(part[None], (count,) + part.shape)]
    all_to_all x3, waiting for transfers between devices: 19.4 us -> 17.5 us  [exchange(): lax.all_to_all(values, 'space', 0, 0, tiled=True, axis_index_groups=groups)]
    ppermute x8, starting transfers between devices: 27.4 us -> 29.2 us  [passed_along(): return lax.ppermute(shard, 'space', pairs)]
  transfers between devices with their start and end apart: 11 -> 13, of which waited for: 5 -> 7; matrix products, arithmetic and copies ran while one was open for 3% -> 3% of each run, Pallas kernels for 1% -> 1%
where the time goes in v2:
time: 110 us; the launch traced here: 109 us
  starting transfers between devices  61.7 us (56%)
  waiting for transfers between devices  30.7 us (28%)
  Pallas kernels  7.85 us (7%)
  local copies, waits for them, and re-layouts  6.36 us (6%)
  other arithmetic  1.97 us (2%)
    ppermute x8, starting transfers between devices, passed_along(): return lax.ppermute(shard, 'space', pairs)  29.2 us
    all_to_all x3, starting transfers between devices, exchange(): lax.all_to_all(values, 'space', 0, 0, tiled=True, axis_index_groups=groups)  24 us
    all_to_all x3, waiting for transfers between devices, exchange(): lax.all_to_all(values, 'space', 0, 0, tiled=True, axis_index_groups=groups)  17.5 us
    all_to_all x2, starting transfers between devices, from_all_chan(): return lax.all_to_all(copies, 'chan', 0, 0, tiled=True)  8.48 us
    pallas_call x3, Pallas kernels, call(): pl.pallas_call(kernel, out_shape=shapes, in_specs=[SMEM] * len(smem) + [V...  7.85 us
    all_to_all x2, waiting for transfers between devices, from_all_chan(): return lax.all_to_all(copies, 'chan', 0, 0, tiled=True)  6.68 us
    ppermute x8, waiting for transfers between devices, passed_along(): return lax.ppermute(shard, 'space', pairs)  6.57 us
    unnamed x10, local copies, waits for them, and re-layouts  2.75 us
  transfers between devices with their start and end apart: 13, of which 7 were waited for; matrix products, arithmetic and copies ran while one was open for 3% of the time, Pallas kernels for 1%

profile of v2, /device:TPU:1, one launch (start us, length us, event | category | flops | bytes accessed | tf_op | source)
XLA Modules:
  0.0 109.5 jit_solution(10840161935739400176)
XLA Ops:
  0.6 1.1 pad_maximum_fusion
  1.7 0.9 broadcast_in_dim.4
  2.6 5.0 %all-to-all-start = ((bf16[4,2,2,32,512]{4,3,2,1,0:T(8,128)(2,1)}), bf16[4,2,2,32,512]{4,3,2,1,0:T(8,128)(2,1)S(1)}, u32[]{:S(2)}, u32[]{:S(2)}) async-start(bf16[4,2,2,32,512]{4,3,2,1,0:T(8,128)(2,1)} %broadcast_in_dim.4), calls=%async_computation | async-start | bytes 1048576 | tf_op jit(solution)/shard_map/all_to_all | solution.py:263
  7.8 6.7 %all-to-all-done.gathered = bf16[4,2,2,32,512]{4,3,2,1,0:T(8,128)(2,1)S(1)} async-done(((bf16[4,2,2,32,512]{4,3,2,1,0:T(8,128)(2,1)}), bf16[4,2,2,32,512]{4,3,2,1,0:T(8,128)(2,1)S(1)}, u32[]{:S(2)}, u32[]{:S(2)}) %all-to-all-start) | async-done | bytes 524320 | tf_op jit(solution)/shard_map/all_to_all | solution.py:263
  14.5 1.0 broadcast_in_dim.5
  15.5 3.5 %all-to-all-start.1 = ((bf16[4,27,32,128]{3,2,1,0:T(8,128)(2,1)}), bf16[4,27,32,128]{3,2,1,0:T(8,128)(2,1)S(1)}, u32[]{:S(2)}, u32[]{:S(2)}) async-start(bf16[4,27,32,128]{3,2,1,0:T(8,128)(2,1)} %broadcast_in_dim.5), calls=%async_computation.1 | async-start | bytes 1769472 | tf_op jit(solution)/shard_map/all_to_all | solution.py:263
  20.5 7.4 %collective-permute-start = (bf16[80,128]{1,0:T(8,128)(2,1)S(1)}, bf16[80,128]{1,0:T(8,128)(2,1)S(1)}, u32[]{:S(2)}, u32[]{:S(2)}) collective-permute-start(bf16[80,128]{1,0:T(8,128)(2,1)S(1)} %get-tuple-element.28), channel_id=1, source_target_pairs={{0,4},{4,8},{8,12},{12,16},{16,20},{20,24},{24,28},{28,32},{32,36}... | collective-permute-start | bytes 61448 | tf_op jit(solution)/shard_map/ppermute | solution.py:234
  27.9 2.4 %collective-permute-start.1 = (bf16[80,128]{1,0:T(8,128)(2,1)S(1)}, bf16[80,128]{1,0:T(8,128)(2,1)S(1)}, u32[]{:S(2)}, u32[]{:S(2)}) collective-permute-start(bf16[80,128]{1,0:T(8,128)(2,1)S(1)} %get-tuple-element.27), channel_id=1, source_target_pairs={{4,0},{8,4},{12,8},{16,12},{20,16},{24,20},{28,24},{32,28},{36,32}... | collective-permute-start | bytes 61448 | tf_op jit(solution)/shard_map/ppermute | solution.py:234
  30.3 2.9 %collective-permute-done.1.from_bp = bf16[80,128]{1,0:T(8,128)(2,1)S(1)} collective-permute-done((bf16[80,128]{1,0:T(8,128)(2,1)S(1)}, bf16[80,128]{1,0:T(8,128)(2,1)S(1)}, u32[]{:S(2)}, u32[]{:S(2)}) %collective-permute-start.1) | collective-permute-done | bytes 20512 | tf_op jit(solution)/shard_map/ppermute | solution.py:234
  33.3 1.3 %collective-permute-start.3 = (bf16[80,128]{1,0:T(8,128)(2,1)S(1)}, bf16[80,128]{1,0:T(8,128)(2,1)S(1)}, u32[]{:S(2)}, u32[]{:S(2)}) collective-permute-start(bf16[80,128]{1,0:T(8,128)(2,1)S(1)} %pad_maximum_fusion.2), channel_id=1, source_target_pairs={{16,0},{20,4},{24,8},{28,12},{32,16},{36,20},{40,24},{44,28},{48,3... | collective-permute-start | bytes 61448 | tf_op jit(solution)/shard_map/ppermute | solution.py:234
  34.6 6.4 %collective-permute-start.2 = (bf16[80,128]{1,0:T(8,128)(2,1)S(1)}, bf16[80,128]{1,0:T(8,128)(2,1)S(1)}, u32[]{:S(2)}, u32[]{:S(2)}) collective-permute-start(bf16[80,128]{1,0:T(8,128)(2,1)S(1)} %pad_maximum_fusion.1), channel_id=1, source_target_pairs={{0,16},{4,20},{8,24},{12,28},{16,32},{20,36},{24,40},{28,44},{32,4... | collective-permute-start | bytes 61448 | tf_op jit(solution)/shard_map/ppermute | solution.py:234
  41.0 0.9 collective-permute-done.2.from_am
  42.6 6.4 %conv.1 = (bf16[2,32,512]{2,1,0:T(8,128)(2,1)S(1)}, bf16[896,128]{1,0:T(8,128)(2,1)}, f32[2,8,8,8,128]{4,3,2,1,0:T(8,128)S(1)}, bf16[2,80,128]{2,1,0:T(8,128)(2,1)S(1)}, bf16[2,64,128]{2,1,0:T(8,128)(2,1)S(1)}) custom-call(s32[2,26]{1,0:T(2,128)S(1)} %copy-done.2, s32[1]{0:T(128)} %bitcast.chan, f32[2,512]{1,0:T(2,128)S(1)} %and_convert_fusion.mask, ...), custom_call_target="tpu_custom_call" | custom-call | tf_op jit(solution)/shard_map/conv/pallas_call | solution.py:220
  49.0 11.8 %all-to-all-start.2 = ((bf16[16,56,128]{2,1,0:T(8,128)(2,1)}), bf16[16,56,128]{2,1,0:T(8,128)(2,1)S(1)}, u32[]{:S(2)}, u32[]{:S(2)}) async-start(bf16[16,56,128]{2,1,0:T(8,128)(2,1)} %bitcast.16), calls=%async_computation.2 | async-start | bytes 458752 | tf_op jit(solution)/shard_map/all_to_all | solution.py:252
  60.8 1.3 %collective-permute-start.4 = (bf16[80,128]{1,0:T(8,128)(2,1)S(1)}, bf16[80,128]{1,0:T(8,128)(2,1)S(1)}, u32[]{:S(2)}, u32[]{:S(2)}) collective-permute-start(bf16[80,128]{1,0:T(8,128)(2,1)S(1)} %get-tuple-element.26), channel_id=1, source_target_pairs={{16,0},{20,4},{24,8},{28,12},{32,16},{36,20},{40,24},{44,28},{48,3... | collective-permute-start | bytes 61448 | tf_op jit(solution)/shard_map/ppermute | solution.py:234
  62.1 4.9 %collective-permute-start.5 = (bf16[80,128]{1,0:T(8,128)(2,1)S(1)}, bf16[80,128]{1,0:T(8,128)(2,1)S(1)}, u32[]{:S(2)}, u32[]{:S(2)}) collective-permute-start(bf16[80,128]{1,0:T(8,128)(2,1)S(1)} %get-tuple-element.25), channel_id=1, source_target_pairs={{0,16},{4,20},{8,24},{12,28},{16,32},{20,36},{24,40},{28,44},{32,4... | collective-permute-start | bytes 61448 | tf_op jit(solution)/shard_map/ppermute | solution.py:234
  67.0 4.8 %all-to-all-done.2 = bf16[16,56,128]{2,1,0:T(8,128)(2,1)S(1)} async-done(((bf16[16,56,128]{2,1,0:T(8,128)(2,1)}), bf16[16,56,128]{2,1,0:T(8,128)(2,1)S(1)}, u32[]{:S(2)}, u32[]{:S(2)}) %all-to-all-start.2) | async-done | bytes 229408 | tf_op jit(solution)/shard_map/all_to_all | solution.py:252
  72.6 8.5 %all-to-all-start.3 = ((f32[8,56,128]{2,1,0:T(8,128)}), f32[8,56,128]{2,1,0:T(8,128)S(1)}, u32[]{:S(2)}, u32[]{:S(2)}) async-start(f32[8,56,128]{2,1,0:T(8,128)} %tile.4), calls=%async_computation.3 | async-start | bytes 458752 | tf_op jit(solution)/shard_map/all_to_all | solution.py:252
  81.1 11.7 %all-to-all-done.3 = f32[8,56,128]{2,1,0:T(8,128)S(1)} async-done(((f32[8,56,128]{2,1,0:T(8,128)}), f32[8,56,128]{2,1,0:T(8,128)S(1)}, u32[]{:S(2)}, u32[]{:S(2)}) %all-to-all-start.3) | async-done | bytes 229408 | tf_op jit(solution)/shard_map/all_to_all | solution.py:252
  93.5 3.7 %all-to-all-start.4 = ((bf16[16,56,128]{2,1,0:T(8,128)(2,1)}), bf16[16,56,128]{2,1,0:T(8,128)(2,1)S(1)}, u32[]{:S(2)}, u32[]{:S(2)}) async-start(bf16[16,56,128]{2,1,0:T(8,128)(2,1)} %tile.5), calls=%async_computation.4 | async-start | bytes 458752 | tf_op jit(solution)/shard_map/all_to_all | solution.py:252
  97.3 3.5 %collective-permute-start.7 = (bf16[80,128]{1,0:T(8,128)(2,1)S(1)}, bf16[80,128]{1,0:T(8,128)(2,1)S(1)}, u32[]{:S(2)}, u32[]{:S(2)}) collective-permute-start(bf16[80,128]{1,0:T(8,128)(2,1)S(1)} %pad_maximum_fusion.4), channel_id=1, source_target_pairs={{0,4},{4,8},{8,12},{12,16},{16,20},{20,24},{24,28},{28,32},{32,36}... | collective-permute-start | bytes 61448 | tf_op jit(solution)/shard_map/ppermute | solution.py:234
  100.9 1.9 %collective-permute-start.6 = (bf16[80,128]{1,0:T(8,128)(2,1)S(1)}, bf16[80,128]{1,0:T(8,128)(2,1)S(1)}, u32[]{:S(2)}, u32[]{:S(2)}) collective-permute-start(bf16[80,128]{1,0:T(8,128)(2,1)S(1)} %pad_maximum_fusion.3), channel_id=1, source_target_pairs={{4,0},{8,4},{12,8},{16,12},{20,16},{24,20},{28,24},{32,28},{36,32}... | collective-permute-start | bytes 61448 | tf_op jit(solution)/shard_map/ppermute | solution.py:234
  103.5 2.8 %collective-permute-done.6.from_bm = bf16[80,128]{1,0:T(8,128)(2,1)S(1)} collective-permute-done((bf16[80,128]{1,0:T(8,128)(2,1)S(1)}, bf16[80,128]{1,0:T(8,128)(2,1)S(1)}, u32[]{:S(2)}, u32[]{:S(2)}) %collective-permute-start.6) | collective-permute-done | bytes 20512 | tf_op jit(solution)/shard_map/ppermute | solution.py:234
  107.7 1.0 all-to-all-done.4
  (43 shorter events, 6.8 us)
Async XLA Ops:
  2.6 5.0 %copy-start.3 = (s32[2,16]{1,0:T(2,128)S(1)}, s32[2,16]{1,0:T(2,128)}, u32[]{:S(2)}) copy-start(s32[2,16]{1,0:T(2,128)} %param.7) | copy-start | bytes 388
  2.6 11.9 %copy-start = (bf16[27,32,128]{2,1,0:T(8,128)(2,1)S(1)}, bf16[27,32,128]{2,1,0:T(8,128)(2,1)}, u32[]{:S(2)}) copy-start(bf16[27,32,128]{2,1,0:T(8,128)(2,1)} %own_weights.1) | copy-start | bytes 663556
  2.6 11.9 %all-to-all-start = ((bf16[4,2,2,32,512]{4,3,2,1,0:T(8,128)(2,1)}), bf16[4,2,2,32,512]{4,3,2,1,0:T(8,128)(2,1)S(1)}, u32[]{:S(2)}, u32[]{:S(2)}) async-start(bf16[4,2,2,32,512]{4,3,2,1,0:T(8,128)(2,1)} %broadcast_in_dim.4), calls=%async_computation | async-start | bytes 1048576 | tf_op jit(solution)/shard_map/all_to_all | solution.py:263
  15.5 26.4 %all-to-all-start.1 = ((bf16[4,27,32,128]{3,2,1,0:T(8,128)(2,1)}), bf16[4,27,32,128]{3,2,1,0:T(8,128)(2,1)S(1)}, u32[]{:S(2)}, u32[]{:S(2)}) async-start(bf16[4,27,32,128]{3,2,1,0:T(8,128)(2,1)} %broadcast_in_dim.5), calls=%async_computation.1 | async-start | bytes 1769472 | tf_op jit(solution)/shard_map/all_to_all | solution.py:263
  19.0 0.7 copy-start.1
  20.5 9.9 %collective-permute-start = (bf16[80,128]{1,0:T(8,128)(2,1)S(1)}, bf16[80,128]{1,0:T(8,128)(2,1)S(1)}, u32[]{:S(2)}, u32[]{:S(2)}) collective-permute-start(bf16[80,128]{1,0:T(8,128)(2,1)S(1)} %get-tuple-element.28), channel_id=1, source_target_pairs={{0,4},{4,8},{8,12},{12,16},{16,20},{20,24},{24,28},{28,32},{32,36}... | collective-permute-start | bytes 61448 | tf_op jit(solution)/shard_map/ppermute | solution.py:234
  27.9 5.4 %collective-permute-start.1 = (bf16[80,128]{1,0:T(8,128)(2,1)S(1)}, bf16[80,128]{1,0:T(8,128)(2,1)S(1)}, u32[]{:S(2)}, u32[]{:S(2)}) collective-permute-start(bf16[80,128]{1,0:T(8,128)(2,1)S(1)} %get-tuple-element.27), channel_id=1, source_target_pairs={{4,0},{8,4},{12,8},{16,12},{20,16},{24,20},{28,24},{32,28},{36,32}... | collective-permute-start | bytes 61448 | tf_op jit(solution)/shard_map/ppermute | solution.py:234
  33.3 7.7 %collective-permute-start.3 = (bf16[80,128]{1,0:T(8,128)(2,1)S(1)}, bf16[80,128]{1,0:T(8,128)(2,1)S(1)}, u32[]{:S(2)}, u32[]{:S(2)}) collective-permute-start(bf16[80,128]{1,0:T(8,128)(2,1)S(1)} %pad_maximum_fusion.2), channel_id=1, source_target_pairs={{16,0},{20,4},{24,8},{28,12},{32,16},{36,20},{40,24},{44,28},{48,3... | collective-permute-start | bytes 61448 | tf_op jit(solution)/shard_map/ppermute | solution.py:234
  34.6 7.3 %collective-permute-start.2 = (bf16[80,128]{1,0:T(8,128)(2,1)S(1)}, bf16[80,128]{1,0:T(8,128)(2,1)S(1)}, u32[]{:S(2)}, u32[]{:S(2)}) collective-permute-start(bf16[80,128]{1,0:T(8,128)(2,1)S(1)} %pad_maximum_fusion.1), channel_id=1, source_target_pairs={{0,16},{4,20},{8,24},{12,28},{16,32},{20,36},{24,40},{28,44},{32,4... | collective-permute-start | bytes 61448 | tf_op jit(solution)/shard_map/ppermute | solution.py:234
  41.9 0.7 copy-start.2
  49.0 22.9 %all-to-all-start.2 = ((bf16[16,56,128]{2,1,0:T(8,128)(2,1)}), bf16[16,56,128]{2,1,0:T(8,128)(2,1)S(1)}, u32[]{:S(2)}, u32[]{:S(2)}) async-start(bf16[16,56,128]{2,1,0:T(8,128)(2,1)} %bitcast.16), calls=%async_computation.2 | async-start | bytes 458752 | tf_op jit(solution)/shard_map/all_to_all | solution.py:252
  60.8 20.3 %collective-permute-start.4 = (bf16[80,128]{1,0:T(8,128)(2,1)S(1)}, bf16[80,128]{1,0:T(8,128)(2,1)S(1)}, u32[]{:S(2)}, u32[]{:S(2)}) collective-permute-start(bf16[80,128]{1,0:T(8,128)(2,1)S(1)} %get-tuple-element.26), channel_id=1, source_target_pairs={{16,0},{20,4},{24,8},{28,12},{32,16},{36,20},{40,24},{44,28},{48,3... | collective-permute-start | bytes 61448 | tf_op jit(solution)/shard_map/ppermute | solution.py:234
  62.1 35.2 %collective-permute-start.5 = (bf16[80,128]{1,0:T(8,128)(2,1)S(1)}, bf16[80,128]{1,0:T(8,128)(2,1)S(1)}, u32[]{:S(2)}, u32[]{:S(2)}) collective-permute-start(bf16[80,128]{1,0:T(8,128)(2,1)S(1)} %get-tuple-element.25), channel_id=1, source_target_pairs={{0,16},{4,20},{8,24},{12,28},{16,32},{20,36},{24,40},{28,44},{32,4... | collective-permute-start | bytes 61448 | tf_op jit(solution)/shard_map/ppermute | solution.py:234
  72.6 20.2 %all-to-all-start.3 = ((f32[8,56,128]{2,1,0:T(8,128)}), f32[8,56,128]{2,1,0:T(8,128)S(1)}, u32[]{:S(2)}, u32[]{:S(2)}) async-start(f32[8,56,128]{2,1,0:T(8,128)} %tile.4), calls=%async_computation.3 | async-start | bytes 458752 | tf_op jit(solution)/shard_map/all_to_all | solution.py:252
  93.5 15.1 %all-to-all-start.4 = ((bf16[16,56,128]{2,1,0:T(8,128)(2,1)}), bf16[16,56,128]{2,1,0:T(8,128)(2,1)S(1)}, u32[]{:S(2)}, u32[]{:S(2)}) async-start(bf16[16,56,128]{2,1,0:T(8,128)(2,1)} %tile.5), calls=%async_computation.4 | async-start | bytes 458752 | tf_op jit(solution)/shard_map/all_to_all | solution.py:252
  97.3 6.2 %collective-permute-start.7 = (bf16[80,128]{1,0:T(8,128)(2,1)S(1)}, bf16[80,128]{1,0:T(8,128)(2,1)S(1)}, u32[]{:S(2)}, u32[]{:S(2)}) collective-permute-start(bf16[80,128]{1,0:T(8,128)(2,1)S(1)} %pad_maximum_fusion.4), channel_id=1, source_target_pairs={{0,4},{4,8},{8,12},{12,16},{16,20},{20,24},{24,28},{28,32},{32,36}... | collective-permute-start | bytes 61448 | tf_op jit(solution)/shard_map/ppermute | solution.py:234
  100.9 5.4 %collective-permute-start.6 = (bf16[80,128]{1,0:T(8,128)(2,1)S(1)}, bf16[80,128]{1,0:T(8,128)(2,1)S(1)}, u32[]{:S(2)}, u32[]{:S(2)}) collective-permute-start(bf16[80,128]{1,0:T(8,128)(2,1)S(1)} %pad_maximum_fusion.3), channel_id=1, source_target_pairs={{4,0},{8,4},{12,8},{16,12},{20,16},{24,20},{28,24},{32,28},{36,32}... | collective-permute-start | bytes 61448 | tf_op jit(solution)/shard_map/ppermute | solution.py:234

commit v3 on v2

--- a/solution.py
+++ b/solution.py
@@ -1,3 +1,4 @@
+import functools
 import math
 
 import jax
@@ -13,7 +14,10 @@
 RIM = {-1: slice(0, 1), 0: slice(1, 9), 1: slice(9, 10)}
 PLANAR = [(a, b) for a in (-1, 0, 1) for b in (-1, 0, 1)]
 MOVES = [m for m in PLANAR if m != (0, 0)]
-DW_ROWS = 28 * 32
+STEPS = {(a, b): 4 * a + b for a, b in MOVES}
+GROUP = 16
+PART = 64
+SENT = PART + 16
 
 
 def slot_of(dx, dy, dz):
@@ -28,6 +32,27 @@
 def tiles(ref_or_value, dx, dy):
     part = ref_or_value[SIDE[dx], SIDE[dy]]
     return part.reshape(-1, 8, 128)
+
+
+def packed(rim):
+    if rim.shape[0] == 1:
+        return jnp.concatenate([rim[0], jnp.zeros((8, 128), F32)], axis=0)
+    lane = lax.broadcasted_iota(jnp.int32, (8, 128), 1)
+    halves = []
+    for first in (0, 4):
+        value = rim[first]
+        for j in (1, 2, 3):
+            value = jnp.where(lane < 32 * j, value, pltpu.roll(rim[first + j], 32 * j, 1))
+        halves.append(value)
+    return jnp.concatenate(halves, axis=0)
+
+
+def unpacked(rows, count):
+    pieces = []
+    for i in range(count):
+        value = rows[8 * (i // 4) : 8 * (i // 4) + 8]
+        pieces.append(pltpu.roll(value, 128 - 32 * (i % 4), 1) if i % 4 else value)
+    return jnp.stack(pieces)
 
 
 def rims_kernel(send, mask, gathered, local, to_b, face_a):
@@ -48,8 +73,8 @@
 
 
 def main_kernel(
-    near, chan, mask, local, from_bm, from_bp, from_am, from_ap, gathered, weights, own_weights,
-    act_out, dw_out, own_out, ret_a, ret_b,
+    near, chan, place, mask, local, from_bm, from_bp, from_am, from_ap, gathered, weights, own_weights,
+    act_out, sent, own_out,
     blocks, grads, own_block, act_all, terms,
 ):
     z = lax.broadcasted_iota(jnp.int32, (1, 8, 128), 1)
@@ -133,8 +158,15 @@
     for i, (dx, dy) in enumerate(PLANAR):
         window = own_block[dx + 1 : dx + 9, dy + 1 : dy + 9].reshape(1024, 128)
         product = jnp.dot(back_t, window, preferred_element_type=F32)
-        dw_out[96 * i : 96 * i + 96] = product.T[0:96].astype(BF)
-    dw_out[864:896] = jnp.zeros((32, 128), BF)
+        product = product.T[0:96].astype(BF)
+        for dz in range(3):
+            j, half = divmod(3 * i + dz, 2)
+            sent[j, 32 * half : 32 * half + 32] = product[32 * dz : 32 * dz + 32]
+    sent[13, 32:64] = jnp.zeros((32, 128), BF)
+    for j in range(14, GROUP):
+        sent[j, 0:PART] = jnp.zeros((PART, 128), BF)
+    for j in range(GROUP):
+        sent[j, PART:SENT] = jnp.zeros((16, 128), BF)
 
     spread = jnp.zeros((1600, 128), F32)
     for dx in (-1, 0, 1):
@@ -165,7 +197,6 @@
         terms[2, brick] = jnp.where(z == 0, down, 0.0).reshape(10, 10, 8, 128)
     for brick in range(2):
         own_out[brick] = terms[1, brick, 1:9, 1:9]
-    edges = {}
     for dx, dy in PLANAR:
         pieces = [
             (near[brick, slot], terms[i, brick, RIM[dx], RIM[dy]])
@@ -183,27 +214,59 @@
         for brick in range(2):
             own_out[brick, SIDE[dx], SIDE[dy]] += collected(brick)
         if (dx, dy) != (0, 0):
-            edges[dx, dy] = collected(2 + MOVES.index((dx, dy))).reshape(-1, 8, 128)
-    for i, a in enumerate((-1, 1)):
-        parts = [edges[a, 0], edges[a, -1], edges[a, 1]]
-        ret_a[i] = jnp.concatenate(parts, axis=0).reshape(80, 128).astype(BF)
-    for i, b in enumerate((-1, 1)):
-        ret_b[i] = edges[0, b].reshape(64, 128).astype(BF)
-
-
-def final_kernel(send, mask, own, from_am, from_ap, from_bm, from_bp, out, total):
+            rim = collected(2 + MOVES.index((dx, dy))).reshape(-1, 8, 128)
+            target = lax.rem(place[0] + STEPS[dx, dy] + GROUP, GROUP)
+            sent[target, PART:SENT] = packed(rim).astype(BF)
+
+
+def middle_kernel(place, arrived, sent):
+    total = arrived[0, 0:PART].astype(F32)
+    for j in range(1, GROUP):
+        total = total + arrived[j, 0:PART].astype(F32)
+    zero = jnp.zeros((16, 128), F32)
+    for j in range(sent.shape[0]):
+        sent[j, 0:PART] = total
+        sent[j, PART : PART + 16] = zero
+        sent[j, PART + 16 : PART + 32] = zero
+    for a in (-1, 1):
+        rims = [
+            arrived[lax.rem(place[0] - STEPS[a, b] + GROUP, GROUP), PART:SENT].astype(F32)
+            for b in (-1, 0, 1)
+        ]
+        target = place[1] + a
+
+        @pl.when((target >= 0) & (target < sent.shape[0]))
+        def _():
+            sent[target, PART : PART + 16] = rims[1]
+            sent[target, PART + 16 : PART + 24] = rims[0][0:8]
+            sent[target, PART + 24 : PART + 32] = rims[2][0:8]
+
+
+def sum_kernel(scale, arrived, sent):
+    total = arrived[0, 0:PART]
+    for j in range(1, arrived.shape[0]):
+        total = total + arrived[j, 0:PART]
+    total = (total * scale).astype(BF)
+    for j in range(GROUP):
+        sent[j] = total
+
+
+def final_kernel(send, place, mask, own, direct, onward, out, total):
     total[...] = own[...]
-    from_a = {-1: from_am, 1: from_ap}
-    from_b = {-1: from_bm, 1: from_bp}
+    inner, outer = place[0], place[1]
     for dx, dy in MOVES:
         s = send[MOVES.index((dx, dy))]
-        if dy == 0:
-            piece = from_a[dx][0:64].astype(F32).reshape(1, 8, 8, 128)
-        elif dx == 0:
-            piece = from_b[dy][0:64].astype(F32).reshape(8, 1, 8, 128)
-        else:
-            both = from_b[dy][64:80].astype(F32).reshape(2, 1, 1, 8, 128)
-            piece = both[0] if dx == -1 else both[1]
+        origin = inner - STEPS[dx, dy]
+        rows = direct[lax.rem(origin + GROUP, GROUP), PART:SENT].astype(F32)
+        if dx:
+            passer = jnp.clip(outer - dx, 0, onward.shape[0] - 1)
+            first = PART if dy == 0 else PART + 16 if dy == -1 else PART + 24
+            other = onward[passer, first : first + (16 if dy == 0 else 8)]
+            inside = (origin >= 0) & (origin < GROUP)
+            rows = jnp.where(inside, rows[0 : other.shape[0]], other)
+        piece = unpacked(rows, 1 if dx and dy else 8)
+        nx = 8 if dx == 0 else 1
+        piece = piece.reshape(nx, piece.shape[0] // nx, 8, 128)
         for brick in range(2):
             total[brick, SIDE[dx], SIDE[dy]] += jnp.where(s == brick, piece, 0.0)
     for brick in range(2):
@@ -231,6 +294,8 @@
 def passed_along(shard, by):
     count = lax.axis_size("space")
     pairs = [(i, i + by) for i in range(count) if 0 <= i + by < count]
+    if abs(by) == 1:
+        pairs = [(i, j) for i, j in pairs if i // 4 == j // 4]
     return lax.ppermute(shard, "space", pairs)
 
 
@@ -240,21 +305,13 @@
     return bits.reshape(packed.shape[0], packed.shape[1] * 32).astype(F32)
 
 
-def summed_over_space(part, scale):
+def exchanged(values, far):
     count = lax.axis_size("space")
-    inner = 16 if count == 128 else count // 2
-    outer = count // inner
-    near = [[j * inner + i for i in range(inner)] for j in range(outer)]
-    far = [[j * inner + i for j in range(outer)] for i in range(inner)]
-    rows = DW_ROWS // inner
-
-    def exchange(values, groups):
-        return lax.all_to_all(values, "space", 0, 0, tiled=True, axis_index_groups=groups)
-
-    mine = exchange(part, near).astype(F32).reshape(inner, rows, 128).sum(0)
-    mine = exchange(jnp.tile(mine, (outer, 1)), far).reshape(outer, rows, 128).sum(0)
-    mine = (mine * scale).astype(BF)
-    return exchange(jnp.tile(mine, (inner, 1)), near)
+    planes = count // GROUP
+    groups = [[j * GROUP + i for i in range(GROUP)] for j in range(planes)]
+    if far:
+        groups = [list(members) for members in zip(*groups)]
+    return lax.all_to_all(values, "space", 0, 0, tiled=True, axis_index_groups=groups)
 
 
 def from_all_chan(part):
@@ -266,6 +323,9 @@
 def on_device(features, mask_packed, neighbours, send_list, weights, cotangent):
     chan = lax.axis_index("chan").astype(jnp.int32).reshape(1)
     send = send_list.reshape(8)
+    where = lax.axis_index("space").astype(jnp.int32)
+    place = jnp.stack([where % GROUP, where // GROUP])
+    planes = lax.axis_size("space") // GROUP
     mask = unpack_mask(mask_packed)
     values = jnp.stack([features.transpose(1, 0, 2), cotangent.transpose(1, 0, 2)])
     all_weights = from_all_chan(weights)
@@ -278,12 +338,11 @@
     to_am = jnp.concatenate([face_a[0], from_bm[64:72], from_bp[64:72]], axis=0)
     to_ap = jnp.concatenate([face_a[1], from_bm[72:80], from_bp[72:80]], axis=0)
     from_am, from_ap = passed_along(to_am, 4), passed_along(to_ap, -4)
-    act, dw, own, ret_a, ret_b = call(
-        main_kernel, "conv", [neighbours, chan],
+    act, sent, own = call(
+        main_kernel, "conv", [neighbours, chan, place],
         [mask, local, from_bm, from_bp, from_am, from_ap, gathered, all_weights, weights],
         [
-            ((2, 32, 512), BF), ((DW_ROWS, 128), BF), ((2, 8, 8, 8, 128), F32),
-            ((2, 80, 128), BF), ((2, 64, 128), BF),
+            ((2, 32, 512), BF), ((GROUP, SENT, 128), BF), ((2, 8, 8, 8, 128), F32),
         ],
         [
             ((3, 10, 10, 16, 128), BF), ((12, 12, 16, 128), BF), ((10, 10, 16, 128), BF),
@@ -291,14 +350,19 @@
         ],
         40,
     )
-    back_am, back_ap = passed_along(ret_a[0], -4), passed_along(ret_a[1], 4)
-    to_bm = jnp.concatenate([ret_b[0], back_am[64:72], back_ap[64:72]], axis=0)
-    to_bp = jnp.concatenate([ret_b[1], back_am[72:80], back_ap[72:80]], axis=0)
-    back_bm, back_bp = passed_along(to_bm, -1), passed_along(to_bp, 1)
     scale = 1.0 / math.sqrt(2 * lax.axis_size("space") * 512)
-    grad_weights = summed_over_space(dw, scale)[:864].astype(F32).reshape(27, 32, 128)
+    direct = exchanged(sent, False)
+    (sent,) = call(
+        middle_kernel, "middle", [place], [direct], [((planes, PART + 32, 128), F32)], [], 16
+    )
+    onward = exchanged(sent, True)
+    (sent,) = call(
+        functools.partial(sum_kernel, scale), "sums", [], [onward], [((GROUP, PART, 128), BF)], [], 16
+    )
+    summed = exchanged(sent, False).reshape(GROUP * PART, 128)
+    grad_weights = summed[:864].astype(F32).reshape(27, 32, 128)
     (grad,) = call(
-        final_kernel, "grad", [send], [mask, own, back_am, back_ap, back_bm, back_bp],
+        final_kernel, "grad", [send, place], [mask, own, direct, onward],
         [((2, 32, 512), BF)], [((2, 8, 8, 8, 128), F32)], 16,
     )
     return act.transpose(1, 0, 2), grad.transpose(1, 0, 2), grad_weights

time: 110 us -> 112 us (1.018)
  blocking collectives: 0 us -> 43.1 us
  starting transfers between devices: 61.7 us -> 28.3 us
  waiting for transfers between devices: 30.7 us -> 23 us
    all_to_all x0 -> x2, blocking collectives: none -> 43.1 us  [exchanged(): lax.all_to_all(values, 'space', 0, 0, tiled=True, axis_index_groups=groups)]
    all_to_all x3 -> x1, starting transfers between devices: 24 us -> 3.73 us  [exchanged(): lax.all_to_all(values, 'space', 0, 0, tiled=True, axis_index_groups=groups)]
    ppermute x8 -> x4, starting transfers between devices: 29.2 us -> 16.1 us  [passed_along(): return lax.ppermute(shard, 'space', pairs)]
    all_to_all x3 -> x1, waiting for transfers between devices: 17.5 us -> 9.66 us  [exchanged(): lax.all_to_all(values, 'space', 0, 0, tiled=True, axis_index_groups=groups)]
    another operation x2 -> x0, local copies, waits for them, and re-layouts: 1.42 us -> none  [the longest x1 0.72 us: summed_over_space(): return exchange(jnp.tile(mine, (inner, 1)), near)]
    pallas_call x3 -> x5, Pallas kernels: 7.85 us -> 8.72 us  [call(): pl.pallas_call(kernel, out_shape=shapes, in_specs=[SMEM] * len(smem) + [V...]
    ppermute x8 -> x4, waiting for transfers between devices: 6.57 us -> 7.3 us  [passed_along(): return lax.ppermute(shard, 'space', pairs)]
  transfers between devices with their start and end apart: 13 -> 7, of which waited for: 7 -> 4; matrix products, arithmetic and copies ran while one was open for 3% -> 2% of each run, Pallas kernels for 1% -> 1%
where the time goes in v3:
time: 112 us; the launch traced here: 111 us
  blocking collectives  43.1 us (38%)
  starting transfers between devices  28.3 us (25%)
  waiting for transfers between devices  23 us (21%)
  Pallas kernels  8.72 us (8%)
  local copies, waits for them, and re-layouts  5.5 us (5%)
  other arithmetic  1.97 us (2%)
    all_to_all x2, blocking collectives, exchanged(): lax.all_to_all(values, 'space', 0, 0, tiled=True, axis_index_groups=groups)  43.1 us
    ppermute x4, starting transfers between devices, passed_along(): return lax.ppermute(shard, 'space', pairs)  16.1 us
    all_to_all x1, waiting for transfers between devices, exchanged(): lax.all_to_all(values, 'space', 0, 0, tiled=True, axis_index_groups=groups)  9.66 us
    pallas_call x5, Pallas kernels, call(): pl.pallas_call(kernel, out_shape=shapes, in_specs=[SMEM] * len(smem) + [V...  8.72 us
    all_to_all x2, starting transfers between devices, from_all_chan(): return lax.all_to_all(copies, 'chan', 0, 0, tiled=True)  8.48 us
    ppermute x4, waiting for transfers between devices, passed_along(): return lax.ppermute(shard, 'space', pairs)  7.3 us
    all_to_all x2, waiting for transfers between devices, from_all_chan(): return lax.all_to_all(copies, 'chan', 0, 0, tiled=True)  6.09 us
    all_to_all x1, starting transfers between devices, exchanged(): lax.all_to_all(values, 'space', 0, 0, tiled=True, axis_index_groups=groups)  3.73 us
  transfers between devices with their start and end apart: 7, of which 4 were waited for; matrix products, arithmetic and copies ran while one was open for 2% of the time, Pallas kernels for 1%

profile of v3, /device:TPU:1, one launch (start us, length us, event | category | flops | bytes accessed | tf_op | source)
XLA Modules:
  0.0 111.5 jit_solution(14469743539968918329)
XLA Ops:
  0.6 1.1 pad_maximum_fusion
  1.7 0.9 broadcast_in_dim.4
  2.6 5.0 %all-to-all-start = ((bf16[4,2,2,32,512]{4,3,2,1,0:T(8,128)(2,1)}), bf16[4,2,2,32,512]{4,3,2,1,0:T(8,128)(2,1)S(1)}, u32[]{:S(2)}, u32[]{:S(2)}) async-start(bf16[4,2,2,32,512]{4,3,2,1,0:T(8,128)(2,1)} %broadcast_in_dim.4), calls=%async_computation | async-start | bytes 1048576 | tf_op jit(solution)/shard_map/all_to_all | solution.py:320
  8.4 6.1 %all-to-all-done.gathered = bf16[4,2,2,32,512]{4,3,2,1,0:T(8,128)(2,1)S(1)} async-done(((bf16[4,2,2,32,512]{4,3,2,1,0:T(8,128)(2,1)}), bf16[4,2,2,32,512]{4,3,2,1,0:T(8,128)(2,1)S(1)}, u32[]{:S(2)}, u32[]{:S(2)}) %all-to-all-start) | async-done | bytes 524320 | tf_op jit(solution)/shard_map/all_to_all | solution.py:320
  14.5 1.0 broadcast_in_dim.5
  15.5 3.5 %all-to-all-start.1 = ((bf16[4,27,32,128]{3,2,1,0:T(8,128)(2,1)}), bf16[4,27,32,128]{3,2,1,0:T(8,128)(2,1)S(1)}, u32[]{:S(2)}, u32[]{:S(2)}) async-start(bf16[4,27,32,128]{3,2,1,0:T(8,128)(2,1)} %broadcast_in_dim.5), calls=%async_computation.1 | async-start | bytes 1769472 | tf_op jit(solution)/shard_map/all_to_all | solution.py:320
  19.7 0.7 rims.1
  20.4 8.5 %collective-permute-start.1 = (bf16[80,128]{1,0:T(8,128)(2,1)S(1)}, bf16[80,128]{1,0:T(8,128)(2,1)S(1)}, u32[]{:S(2)}, u32[]{:S(2)}) collective-permute-start(bf16[80,128]{1,0:T(8,128)(2,1)S(1)} %get-tuple-element.18), channel_id=1, source_target_pairs={{4,0},{8,4},{12,8},{20,16},{24,20},{28,24},{36,32},{40,36},{44,40}... | collective-permute-start | bytes 61448 | tf_op jit(solution)/shard_map/ppermute | solution.py:299
  29.0 1.9 %collective-permute-start = (bf16[80,128]{1,0:T(8,128)(2,1)S(1)}, bf16[80,128]{1,0:T(8,128)(2,1)S(1)}, u32[]{:S(2)}, u32[]{:S(2)}) collective-permute-start(bf16[80,128]{1,0:T(8,128)(2,1)S(1)} %get-tuple-element.19), channel_id=1, source_target_pairs={{0,4},{4,8},{8,12},{16,20},{20,24},{24,28},{32,36},{36,40},{40,44}... | collective-permute-start | bytes 61448 | tf_op jit(solution)/shard_map/ppermute | solution.py:299
  30.9 1.1 %collective-permute-done.from_bm = bf16[80,128]{1,0:T(8,128)(2,1)S(1)} collective-permute-done((bf16[80,128]{1,0:T(8,128)(2,1)S(1)}, bf16[80,128]{1,0:T(8,128)(2,1)S(1)}, u32[]{:S(2)}, u32[]{:S(2)}) %collective-permute-start) | collective-permute-done | bytes 20512 | tf_op jit(solution)/shard_map/ppermute | solution.py:299
  32.1 4.4 %collective-permute-start.2 = (bf16[80,128]{1,0:T(8,128)(2,1)S(1)}, bf16[80,128]{1,0:T(8,128)(2,1)S(1)}, u32[]{:S(2)}, u32[]{:S(2)}) collective-permute-start(bf16[80,128]{1,0:T(8,128)(2,1)S(1)} %pad_maximum_fusion.1), channel_id=1, source_target_pairs={{0,16},{4,20},{8,24},{12,28},{16,32},{20,36},{24,40},{28,44},{32,4... | collective-permute-start | bytes 61448 | tf_op jit(solution)/shard_map/ppermute | solution.py:299
  36.5 1.3 %collective-permute-start.3 = (bf16[80,128]{1,0:T(8,128)(2,1)S(1)}, bf16[80,128]{1,0:T(8,128)(2,1)S(1)}, u32[]{:S(2)}, u32[]{:S(2)}) collective-permute-start(bf16[80,128]{1,0:T(8,128)(2,1)S(1)} %pad_maximum_fusion.2), channel_id=1, source_target_pairs={{16,0},{20,4},{24,8},{28,12},{32,16},{36,20},{40,24},{44,28},{48,3... | collective-permute-start | bytes 61448 | tf_op jit(solution)/shard_map/ppermute | solution.py:299
  37.9 6.2 %collective-permute-done.3.from_ap = bf16[80,128]{1,0:T(8,128)(2,1)S(1)} collective-permute-done((bf16[80,128]{1,0:T(8,128)(2,1)S(1)}, bf16[80,128]{1,0:T(8,128)(2,1)S(1)}, u32[]{:S(2)}, u32[]{:S(2)}) %collective-permute-start.3) | collective-permute-done | bytes 20512 | tf_op jit(solution)/shard_map/ppermute | solution.py:299
  44.0 0.7 copy-done.2
  44.7 5.9 %conv.1 = (bf16[2,32,512]{2,1,0:T(8,128)(2,1)S(1)}, bf16[16,80,128]{2,1,0:T(8,128)(2,1)S(1)}, f32[2,8,8,8,128]{4,3,2,1,0:T(8,128)S(1)}) custom-call(s32[2,26]{1,0:T(2,128)S(1)} %copy-done.2, s32[1]{0:T(128)} %bitcast.chan, s32[2]{0:T(128)S(1)} %pad_add_fusion.place, f32[2,512]{1,0:T(2,128)S(1)} %and_convert_fusion.mask, ...), custom_call_target="tpu_custom_call" | custom-call | tf_op jit(solution)/shard_map/conv/pallas_call | solution.py:283
  50.6 21.3 %all_to_all.25.arrived.direct = bf16[16,80,128]{2,1,0:T(8,128)(2,1)S(1)} all-to-all(bf16[16,80,128]{2,1,0:T(8,128)(2,1)S(1)} %get-tuple-element.14), channel_id=1, replica_groups={{0,4,8,12,16,20,24,28,32,36,40,44,48,52,56,60},{64,68,72,76,80,84,88,92..., dimensions={0} | all-to-all | bytes 655360 | tf_op jit(solution)/shard_map/all_to_all | solution.py:314
  72.5 21.9 %all_to_all.26.onward.arrived = f32[8,96,128]{2,1,0:T(8,128)S(1)} all-to-all(f32[8,96,128]{2,1,0:T(8,128)S(1)} %middle.1), channel_id=1, replica_groups={{0,64,128,192,256,320,384,448},{4,68,132,196,260,324,388,452},{8,72,136..., dimensions={0} | all-to-all | bytes 786432 | tf_op jit(solution)/shard_map/all_to_all | solution.py:314
  94.3 0.7 sums.1
  95.1 3.7 %all-to-all-start.4 = ((bf16[16,64,128]{2,1,0:T(8,128)(2,1)}), bf16[16,64,128]{2,1,0:T(8,128)(2,1)S(1)}, u32[]{:S(2)}, u32[]{:S(2)}) async-start(bf16[16,64,128]{2,1,0:T(8,128)(2,1)} %sums.1), calls=%async_computation.4 | async-start | bytes 524288 | tf_op jit(solution)/shard_map/all_to_all | solution.py:314
  98.8 0.7 copy.10
  99.5 0.8 grad.1
  100.3 0.7 copy.11
  101.0 9.7 %all-to-all-done.4 = bf16[16,64,128]{2,1,0:T(8,128)(2,1)S(1)} async-done(((bf16[16,64,128]{2,1,0:T(8,128)(2,1)}), bf16[16,64,128]{2,1,0:T(8,128)(2,1)S(1)}, u32[]{:S(2)}, u32[]{:S(2)}) %all-to-all-start.4) | async-done | bytes 262176 | tf_op jit(solution)/shard_map/all_to_all | solution.py:314
  110.7 0.8 convert.1
  (25 shorter events, 2.2 us)
Async XLA Ops:
  2.6 11.9 %copy-start = (bf16[27,32,128]{2,1,0:T(8,128)(2,1)S(1)}, bf16[27,32,128]{2,1,0:T(8,128)(2,1)}, u32[]{:S(2)}) copy-start(bf16[27,32,128]{2,1,0:T(8,128)(2,1)} %own_weights.1) | copy-start | bytes 663556
  2.6 11.9 %all-to-all-start = ((bf16[4,2,2,32,512]{4,3,2,1,0:T(8,128)(2,1)}), bf16[4,2,2,32,512]{4,3,2,1,0:T(8,128)(2,1)S(1)}, u32[]{:S(2)}, u32[]{:S(2)}) async-start(bf16[4,2,2,32,512]{4,3,2,1,0:T(8,128)(2,1)} %broadcast_in_dim.4), calls=%async_computation | async-start | bytes 1048576 | tf_op jit(solution)/shard_map/all_to_all | solution.py:320
  7.6 0.7 copy-start.3
  15.5 28.5 %all-to-all-start.1 = ((bf16[4,27,32,128]{3,2,1,0:T(8,128)(2,1)}), bf16[4,27,32,128]{3,2,1,0:T(8,128)(2,1)S(1)}, u32[]{:S(2)}, u32[]{:S(2)}) async-start(bf16[4,27,32,128]{3,2,1,0:T(8,128)(2,1)} %broadcast_in_dim.5), calls=%async_computation.1 | async-start | bytes 1769472 | tf_op jit(solution)/shard_map/all_to_all | solution.py:320
  19.0 0.7 copy-start.1
  20.4 10.5 %collective-permute-start.1 = (bf16[80,128]{1,0:T(8,128)(2,1)S(1)}, bf16[80,128]{1,0:T(8,128)(2,1)S(1)}, u32[]{:S(2)}, u32[]{:S(2)}) collective-permute-start(bf16[80,128]{1,0:T(8,128)(2,1)S(1)} %get-tuple-element.18), channel_id=1, source_target_pairs={{4,0},{8,4},{12,8},{20,16},{24,20},{28,24},{36,32},{40,36},{44,40}... | collective-permute-start | bytes 61448 | tf_op jit(solution)/shard_map/ppermute | solution.py:299
  29.0 3.1 %collective-permute-start = (bf16[80,128]{1,0:T(8,128)(2,1)S(1)}, bf16[80,128]{1,0:T(8,128)(2,1)S(1)}, u32[]{:S(2)}, u32[]{:S(2)}) collective-permute-start(bf16[80,128]{1,0:T(8,128)(2,1)S(1)} %get-tuple-element.19), channel_id=1, source_target_pairs={{0,4},{4,8},{8,12},{16,20},{20,24},{24,28},{32,36},{36,40},{40,44}... | collective-permute-start | bytes 61448 | tf_op jit(solution)/shard_map/ppermute | solution.py:299
  32.1 5.8 %collective-permute-start.2 = (bf16[80,128]{1,0:T(8,128)(2,1)S(1)}, bf16[80,128]{1,0:T(8,128)(2,1)S(1)}, u32[]{:S(2)}, u32[]{:S(2)}) collective-permute-start(bf16[80,128]{1,0:T(8,128)(2,1)S(1)} %pad_maximum_fusion.1), channel_id=1, source_target_pairs={{0,16},{4,20},{8,24},{12,28},{16,32},{20,36},{24,40},{28,44},{32,4... | collective-permute-start | bytes 61448 | tf_op jit(solution)/shard_map/ppermute | solution.py:299
  36.5 7.5 %collective-permute-start.3 = (bf16[80,128]{1,0:T(8,128)(2,1)S(1)}, bf16[80,128]{1,0:T(8,128)(2,1)S(1)}, u32[]{:S(2)}, u32[]{:S(2)}) collective-permute-start(bf16[80,128]{1,0:T(8,128)(2,1)S(1)} %pad_maximum_fusion.2), channel_id=1, source_target_pairs={{16,0},{20,4},{24,8},{28,12},{32,16},{36,20},{40,24},{44,28},{48,3... | collective-permute-start | bytes 61448 | tf_op jit(solution)/shard_map/ppermute | solution.py:299
  44.0 0.7 copy-start.2
  95.1 15.6 %all-to-all-start.4 = ((bf16[16,64,128]{2,1,0:T(8,128)(2,1)}), bf16[16,64,128]{2,1,0:T(8,128)(2,1)S(1)}, u32[]{:S(2)}, u32[]{:S(2)}) async-start(bf16[16,64,128]{2,1,0:T(8,128)(2,1)} %sums.1), calls=%async_computation.4 | async-start | bytes 524288 | tf_op jit(solution)/shard_map/all_to_all | solution.py:314

commit v4 on v3

--- a/solution.py
+++ b/solution.py
@@ -16,8 +16,9 @@
 MOVES = [m for m in PLANAR if m != (0, 0)]
 STEPS = {(a, b): 4 * a + b for a, b in MOVES}
 GROUP = 16
-PART = 64
+PART = 56
 SENT = PART + 16
+ONWARD = PART + 24
 
 
 def slot_of(dx, dy, dz):
@@ -55,6 +56,10 @@
     return jnp.stack(pieces)
 
 
+def rows_of(index, stride, first, count):
+    return pl.ds(pl.multiple_of(index * stride + first, 8), count)
+
+
 def rims_kernel(send, mask, gathered, local, to_b, face_a):
     for brick in range(2):
         rows = gathered[:, 0, brick].reshape(128, 512).astype(F32) * mask[brick : brick + 1, :]
@@ -75,7 +80,7 @@
 def main_kernel(
     near, chan, place, mask, local, from_bm, from_bp, from_am, from_ap, gathered, weights, own_weights,
     act_out, sent, own_out,
-    blocks, grads, own_block, act_all, terms,
+    blocks, grads, own_block, act_all, terms, stage,
 ):
     z = lax.broadcasted_iota(jnp.int32, (1, 8, 128), 1)
     from_b = {-1: from_bm, 1: from_bp}
@@ -155,18 +160,21 @@
     own_block[...] = (
         jnp.dot(stacked, select, preferred_element_type=F32).astype(BF).reshape(10, 10, 16, 128)
     )
+
+    def put_part(tile, value):
+        first = tile // 7 * SENT + tile % 7 * 8
+        stage[first : first + 8] = value
+
     for i, (dx, dy) in enumerate(PLANAR):
         window = own_block[dx + 1 : dx + 9, dy + 1 : dy + 9].reshape(1024, 128)
         product = jnp.dot(back_t, window, preferred_element_type=F32)
-        product = product.T[0:96].astype(BF)
-        for dz in range(3):
-            j, half = divmod(3 * i + dz, 2)
-            sent[j, 32 * half : 32 * half + 32] = product[32 * dz : 32 * dz + 32]
-    sent[13, 32:64] = jnp.zeros((32, 128), BF)
-    for j in range(14, GROUP):
-        sent[j, 0:PART] = jnp.zeros((PART, 128), BF)
+        product = product.T
+        for tile in range(12):
+            put_part(12 * i + tile, product[8 * tile : 8 * tile + 8])
+    for tile in range(108, 112):
+        put_part(tile, jnp.zeros((8, 128), F32))
     for j in range(GROUP):
-        sent[j, PART:SENT] = jnp.zeros((16, 128), BF)
+        stage[j * SENT + PART : (j + 1) * SENT] = jnp.zeros((16, 128), F32)
 
     spread = jnp.zeros((1600, 128), F32)
     for dx in (-1, 0, 1):
@@ -216,54 +224,59 @@
         if (dx, dy) != (0, 0):
             rim = collected(2 + MOVES.index((dx, dy))).reshape(-1, 8, 128)
             target = lax.rem(place[0] + STEPS[dx, dy] + GROUP, GROUP)
-            sent[target, PART:SENT] = packed(rim).astype(BF)
-
-
-def middle_kernel(place, arrived, sent):
-    total = arrived[0, 0:PART].astype(F32)
+            stage[rows_of(target, SENT, PART, 16)] = packed(rim)
+    sent[...] = stage[...].astype(BF)
+
+
+def middle_kernel(place, arrived, sent, held, stage):
+    held[...] = arrived[...].astype(F32)
+    total = held[0:PART]
     for j in range(1, GROUP):
-        total = total + arrived[j, 0:PART].astype(F32)
-    zero = jnp.zeros((16, 128), F32)
-    for j in range(sent.shape[0]):
-        sent[j, 0:PART] = total
-        sent[j, PART : PART + 16] = zero
-        sent[j, PART + 16 : PART + 32] = zero
+        total = total + held[j * SENT : j * SENT + PART]
+    planes = stage.shape[0] // ONWARD
+    for j in range(planes):
+        stage[j * ONWARD : j * ONWARD + PART] = total
+        stage[j * ONWARD + PART : (j + 1) * ONWARD] = jnp.zeros((24, 128), F32)
+    lane = lax.broadcasted_iota(jnp.int32, (8, 128), 1)
     for a in (-1, 1):
-        rims = [
-            arrived[lax.rem(place[0] - STEPS[a, b] + GROUP, GROUP), PART:SENT].astype(F32)
+        rims = {
+            b: held[rows_of(lax.rem(place[0] - STEPS[a, b] + GROUP, GROUP), SENT, PART, 16 if b == 0 else 8)]
             for b in (-1, 0, 1)
-        ]
+        }
+        edges = jnp.where(lane < 32, rims[-1], pltpu.roll(rims[1], 32, 1))
         target = place[1] + a
 
-        @pl.when((target >= 0) & (target < sent.shape[0]))
+        @pl.when((target >= 0) & (target < planes))
         def _():
-            sent[target, PART : PART + 16] = rims[1]
-            sent[target, PART + 16 : PART + 24] = rims[0][0:8]
-            sent[target, PART + 24 : PART + 32] = rims[2][0:8]
+            stage[rows_of(target, ONWARD, PART, 24)] = jnp.concatenate([rims[0], edges], axis=0)
+
+    sent[...] = stage[...].astype(BF)
 
 
 def sum_kernel(scale, arrived, sent):
-    total = arrived[0, 0:PART]
-    for j in range(1, arrived.shape[0]):
-        total = total + arrived[j, 0:PART]
-    total = (total * scale).astype(BF)
-    for j in range(GROUP):
-        sent[j] = total
-
-
-def final_kernel(send, place, mask, own, direct, onward, out, total):
+    values = arrived[...].astype(F32)
+    total = values[0:PART]
+    for j in range(1, values.shape[0] // ONWARD):
+        total = total + values[j * ONWARD : j * ONWARD + PART]
+    sent[...] = jnp.concatenate([total * scale] * GROUP, axis=0).astype(BF)
+
+
+def final_kernel(send, place, mask, own, direct, onward, out, total, held, passed):
     total[...] = own[...]
+    held[...] = direct[...].astype(F32)
+    passed[...] = onward[...].astype(F32)
     inner, outer = place[0], place[1]
     for dx, dy in MOVES:
         s = send[MOVES.index((dx, dy))]
         origin = inner - STEPS[dx, dy]
-        rows = direct[lax.rem(origin + GROUP, GROUP), PART:SENT].astype(F32)
+        size = 8 if dx and dy else 16
+        rows = held[rows_of(lax.rem(origin + GROUP, GROUP), SENT, PART, size)]
         if dx:
-            passer = jnp.clip(outer - dx, 0, onward.shape[0] - 1)
-            first = PART if dy == 0 else PART + 16 if dy == -1 else PART + 24
-            other = onward[passer, first : first + (16 if dy == 0 else 8)]
-            inside = (origin >= 0) & (origin < GROUP)
-            rows = jnp.where(inside, rows[0 : other.shape[0]], other)
+            passer = jnp.clip(outer - dx, 0, passed.shape[0] // ONWARD - 1)
+            other = passed[rows_of(passer, ONWARD, PART + 16 if dy else PART, size)]
+            if dy == 1:
+                other = pltpu.roll(other, 96, 1)
+            rows = jnp.where((origin >= 0) & (origin < GROUP), rows, other)
         piece = unpacked(rows, 1 if dx and dy else 8)
         nx = 8 if dx == 0 else 1
         piece = piece.reshape(nx, piece.shape[0] // nx, 8, 128)
@@ -342,28 +355,30 @@
         main_kernel, "conv", [neighbours, chan, place],
         [mask, local, from_bm, from_bp, from_am, from_ap, gathered, all_weights, weights],
         [
-            ((2, 32, 512), BF), ((GROUP, SENT, 128), BF), ((2, 8, 8, 8, 128), F32),
+            ((2, 32, 512), BF), ((GROUP * SENT, 128), BF), ((2, 8, 8, 8, 128), F32),
         ],
         [
             ((3, 10, 10, 16, 128), BF), ((12, 12, 16, 128), BF), ((10, 10, 16, 128), BF),
-            ((2, 128, 512), BF), ((3, 2, 10, 10, 8, 128), F32),
+            ((2, 128, 512), BF), ((3, 2, 10, 10, 8, 128), F32), ((GROUP * SENT, 128), F32),
         ],
         40,
     )
     scale = 1.0 / math.sqrt(2 * lax.axis_size("space") * 512)
     direct = exchanged(sent, False)
     (sent,) = call(
-        middle_kernel, "middle", [place], [direct], [((planes, PART + 32, 128), F32)], [], 16
+        middle_kernel, "middle", [place], [direct], [((planes * ONWARD, 128), BF)],
+        [((GROUP * SENT, 128), F32), ((planes * ONWARD, 128), F32)], 16,
     )
     onward = exchanged(sent, True)
     (sent,) = call(
-        functools.partial(sum_kernel, scale), "sums", [], [onward], [((GROUP, PART, 128), BF)], [], 16
-    )
-    summed = exchanged(sent, False).reshape(GROUP * PART, 128)
+        functools.partial(sum_kernel, scale), "sums", [], [onward], [((GROUP * PART, 128), BF)], [], 16
+    )
+    summed = exchanged(sent, False)
     grad_weights = summed[:864].astype(F32).reshape(27, 32, 128)
     (grad,) = call(
         final_kernel, "grad", [send, place], [mask, own, direct, onward],
-        [((2, 32, 512), BF)], [((2, 8, 8, 8, 128), F32)], 16,
+        [((2, 32, 512), BF)],
+        [((2, 8, 8, 8, 128), F32), ((GROUP * SENT, 128), F32), ((planes * ONWARD, 128), F32)], 16,
     )
     return act.transpose(1, 0, 2), grad.transpose(1, 0, 2), grad_weights
 

time: 112 us -> 106 us (0.946)
  blocking collectives: 43.1 us -> 37.5 us
    all_to_all x2, blocking collectives: 43.1 us -> 37.5 us  [exchanged(): lax.all_to_all(values, 'space', 0, 0, tiled=True, axis_index_groups=groups)]
  transfers between devices with their start and end apart: 7 -> 7, of which waited for: 4 -> 4; matrix products, arithmetic and copies ran while one was open for 2% -> 2% of each run, Pallas kernels for 1% -> 2%
where the time goes in v4:
time: 106 us; the launch traced here: 105 us
  blocking collectives  37.5 us (35%)
  starting transfers between devices  28.3 us (27%)
  waiting for transfers between devices  22.3 us (21%)
  Pallas kernels  8.92 us (8%)
  local copies, waits for them, and re-layouts  5.5 us (5%)
  other arithmetic  1.97 us (2%)
    all_to_all x2, blocking collectives, exchanged(): lax.all_to_all(values, 'space', 0, 0, tiled=True, axis_index_groups=groups)  37.5 us
    ppermute x4, starting transfers between devices, passed_along(): return lax.ppermute(shard, 'space', pairs)  16.1 us
    pallas_call x5, Pallas kernels, call(): pl.pallas_call(kernel, out_shape=shapes, in_specs=[SMEM] * len(smem) + [V...  8.92 us
    all_to_all x1, waiting for transfers between devices, exchanged(): lax.all_to_all(values, 'space', 0, 0, tiled=True, axis_index_groups=groups)  8.9 us
    all_to_all x2, starting transfers between devices, from_all_chan(): return lax.all_to_all(copies, 'chan', 0, 0, tiled=True)  8.48 us
    ppermute x4, waiting for transfers between devices, passed_along(): return lax.ppermute(shard, 'space', pairs)  7.3 us
    all_to_all x2, waiting for transfers between devices, from_all_chan(): return lax.all_to_all(copies, 'chan', 0, 0, tiled=True)  6.09 us
    all_to_all x1, starting transfers between devices, exchanged(): lax.all_to_all(values, 'space', 0, 0, tiled=True, axis_index_groups=groups)  3.73 us
  transfers between devices with their start and end apart: 7, of which 4 were waited for; matrix products, arithmetic and copies ran while one was open for 2% of the time, Pallas kernels for 2%

profile of v4, /device:TPU:1, one launch (start us, length us, event | category | flops | bytes accessed | tf_op | source)
XLA Modules:
  0.0 105.3 jit_solution(4389647109389499007)
XLA Ops:
  0.6 1.1 %pad_maximum_fusion = bf16[2,2,32,512]{3,1,2,0:T(2,128)(2,1)S(1)} fusion(bf16[1,2,32,512]{3,1,2,0:T(2,128)(2,1)} %bitcast.40, bf16[1,2,32,512]{3,1,2,0:T(2,128)(2,1)} %bitcast.41), kind=kLoop, calls=%fused_computation | loop fusion | flops 65536 | bytes 262144 | tf_op jit(solution)/shard_map/stack | solution.py:343
  1.7 0.9 broadcast_in_dim.4
  2.6 5.0 %all-to-all-start = ((bf16[4,2,2,32,512]{4,3,2,1,0:T(8,128)(2,1)}), bf16[4,2,2,32,512]{4,3,2,1,0:T(8,128)(2,1)S(1)}, u32[]{:S(2)}, u32[]{:S(2)}) async-start(bf16[4,2,2,32,512]{4,3,2,1,0:T(8,128)(2,1)} %broadcast_in_dim.4), calls=%async_computation | async-start | bytes 1048576 | tf_op jit(solution)/shard_map/all_to_all | solution.py:333
  8.4 6.1 %all-to-all-done.gathered = bf16[4,2,2,32,512]{4,3,2,1,0:T(8,128)(2,1)S(1)} async-done(((bf16[4,2,2,32,512]{4,3,2,1,0:T(8,128)(2,1)}), bf16[4,2,2,32,512]{4,3,2,1,0:T(8,128)(2,1)S(1)}, u32[]{:S(2)}, u32[]{:S(2)}) %all-to-all-start) | async-done | bytes 524320 | tf_op jit(solution)/shard_map/all_to_all | solution.py:333
  14.5 1.0 broadcast_in_dim.5
  15.5 3.5 %all-to-all-start.1 = ((bf16[4,27,32,128]{3,2,1,0:T(8,128)(2,1)}), bf16[4,27,32,128]{3,2,1,0:T(8,128)(2,1)S(1)}, u32[]{:S(2)}, u32[]{:S(2)}) async-start(bf16[4,27,32,128]{3,2,1,0:T(8,128)(2,1)} %broadcast_in_dim.5), calls=%async_computation.1 | async-start | bytes 1769472 | tf_op jit(solution)/shard_map/all_to_all | solution.py:333
  19.7 0.7 rims.1
  20.4 8.5 %collective-permute-start.1 = (bf16[80,128]{1,0:T(8,128)(2,1)S(1)}, bf16[80,128]{1,0:T(8,128)(2,1)S(1)}, u32[]{:S(2)}, u32[]{:S(2)}) collective-permute-start(bf16[80,128]{1,0:T(8,128)(2,1)S(1)} %get-tuple-element.18), channel_id=1, source_target_pairs={{4,0},{8,4},{12,8},{20,16},{24,20},{28,24},{36,32},{40,36},{44,40}... | collective-permute-start | bytes 61448 | tf_op jit(solution)/shard_map/ppermute | solution.py:312
  29.0 1.9 %collective-permute-start = (bf16[80,128]{1,0:T(8,128)(2,1)S(1)}, bf16[80,128]{1,0:T(8,128)(2,1)S(1)}, u32[]{:S(2)}, u32[]{:S(2)}) collective-permute-start(bf16[80,128]{1,0:T(8,128)(2,1)S(1)} %get-tuple-element.19), channel_id=1, source_target_pairs={{0,4},{4,8},{8,12},{16,20},{20,24},{24,28},{32,36},{36,40},{40,44}... | collective-permute-start | bytes 61448 | tf_op jit(solution)/shard_map/ppermute | solution.py:312
  30.9 1.1 %collective-permute-done.from_bm = bf16[80,128]{1,0:T(8,128)(2,1)S(1)} collective-permute-done((bf16[80,128]{1,0:T(8,128)(2,1)S(1)}, bf16[80,128]{1,0:T(8,128)(2,1)S(1)}, u32[]{:S(2)}, u32[]{:S(2)}) %collective-permute-start) | collective-permute-done | bytes 20512 | tf_op jit(solution)/shard_map/ppermute | solution.py:312
  32.1 4.4 %collective-permute-start.2 = (bf16[80,128]{1,0:T(8,128)(2,1)S(1)}, bf16[80,128]{1,0:T(8,128)(2,1)S(1)}, u32[]{:S(2)}, u32[]{:S(2)}) collective-permute-start(bf16[80,128]{1,0:T(8,128)(2,1)S(1)} %pad_maximum_fusion.1), channel_id=1, source_target_pairs={{0,16},{4,20},{8,24},{12,28},{16,32},{20,36},{24,40},{28,44},{32,4... | collective-permute-start | bytes 61448 | tf_op jit(solution)/shard_map/ppermute | solution.py:312
  36.5 1.3 %collective-permute-start.3 = (bf16[80,128]{1,0:T(8,128)(2,1)S(1)}, bf16[80,128]{1,0:T(8,128)(2,1)S(1)}, u32[]{:S(2)}, u32[]{:S(2)}) collective-permute-start(bf16[80,128]{1,0:T(8,128)(2,1)S(1)} %pad_maximum_fusion.2), channel_id=1, source_target_pairs={{16,0},{20,4},{24,8},{28,12},{32,16},{36,20},{40,24},{44,28},{48,3... | collective-permute-start | bytes 61448 | tf_op jit(solution)/shard_map/ppermute | solution.py:312
  37.9 6.2 %collective-permute-done.3.from_ap = bf16[80,128]{1,0:T(8,128)(2,1)S(1)} collective-permute-done((bf16[80,128]{1,0:T(8,128)(2,1)S(1)}, bf16[80,128]{1,0:T(8,128)(2,1)S(1)}, u32[]{:S(2)}, u32[]{:S(2)}) %collective-permute-start.3) | collective-permute-done | bytes 20512 | tf_op jit(solution)/shard_map/ppermute | solution.py:312
  44.7 5.9 %conv.1 = (bf16[2,32,512]{2,1,0:T(8,128)(2,1)S(1)}, bf16[1152,128]{1,0:T(8,128)(2,1)S(1)}, f32[2,8,8,8,128]{4,3,2,1,0:T(8,128)S(1)}) custom-call(s32[2,26]{1,0:T(2,128)S(1)} %copy-done.2, s32[1]{0:T(128)} %bitcast.chan, s32[2]{0:T(128)S(1)} %pad_add_fusion.place, f32[2,512]{1,0:T(2,128)S(1)} %and_convert_fusion.mask, ...), custom_call_target="tpu_custom_call" | custom-call | tf_op jit(solution)/shard_map/conv/pallas_call | solution.py:296
  50.6 20.6 %all_to_all.44 = bf16[16,72,128]{2,1,0:T(8,128)(2,1)S(1)} all-to-all(bf16[16,72,128]{2,1,0:T(8,128)(2,1)S(1)} %bitcast.33), channel_id=1, replica_groups={{0,4,8,12,16,20,24,28,32,36,40,44,48,52,56,60},{64,68,72,76,80,84,88,92..., dimensions={0} | all-to-all | bytes 589824 | tf_op jit(solution)/shard_map/all_to_all | solution.py:327
  71.2 0.8 middle.1
  71.9 16.9 %all_to_all.45 = bf16[8,80,128]{2,1,0:T(8,128)(2,1)S(1)} all-to-all(bf16[8,80,128]{2,1,0:T(8,128)(2,1)S(1)} %bitcast.32), channel_id=1, replica_groups={{0,64,128,192,256,320,384,448},{4,68,132,196,260,324,388,452},{8,72,136..., dimensions={0} | all-to-all | bytes 327680 | tf_op jit(solution)/shard_map/all_to_all | solution.py:327
  88.9 0.7 sums.1
  89.6 3.7 %all-to-all-start.4 = ((bf16[16,56,128]{2,1,0:T(8,128)(2,1)}), bf16[16,56,128]{2,1,0:T(8,128)(2,1)S(1)}, u32[]{:S(2)}, u32[]{:S(2)}) async-start(bf16[16,56,128]{2,1,0:T(8,128)(2,1)} %bitcast.18), calls=%async_computation.4 | async-start | bytes 458752 | tf_op jit(solution)/shard_map/all_to_all | solution.py:327
  93.3 0.7 copy.10
  94.0 0.9 grad.1
  94.9 0.7 copy.11
  95.6 8.9 %all-to-all-done.4 = bf16[16,56,128]{2,1,0:T(8,128)(2,1)S(1)} async-done(((bf16[16,56,128]{2,1,0:T(8,128)(2,1)}), bf16[16,56,128]{2,1,0:T(8,128)(2,1)S(1)}, u32[]{:S(2)}, u32[]{:S(2)}) %all-to-all-start.4) | async-done | bytes 229408 | tf_op jit(solution)/shard_map/all_to_all | solution.py:327
  104.5 0.8 convert.1
  (25 shorter events, 2.3 us)
Async XLA Ops:
  2.6 11.9 %copy-start = (bf16[27,32,128]{2,1,0:T(8,128)(2,1)S(1)}, bf16[27,32,128]{2,1,0:T(8,128)(2,1)}, u32[]{:S(2)}) copy-start(bf16[27,32,128]{2,1,0:T(8,128)(2,1)} %own_weights.1) | copy-start | bytes 663556
  2.6 11.9 %all-to-all-start = ((bf16[4,2,2,32,512]{4,3,2,1,0:T(8,128)(2,1)}), bf16[4,2,2,32,512]{4,3,2,1,0:T(8,128)(2,1)S(1)}, u32[]{:S(2)}, u32[]{:S(2)}) async-start(bf16[4,2,2,32,512]{4,3,2,1,0:T(8,128)(2,1)} %broadcast_in_dim.4), calls=%async_computation | async-start | bytes 1048576 | tf_op jit(solution)/shard_map/all_to_all | solution.py:333
  7.6 0.7 copy-start.3
  15.5 28.5 %all-to-all-start.1 = ((bf16[4,27,32,128]{3,2,1,0:T(8,128)(2,1)}), bf16[4,27,32,128]{3,2,1,0:T(8,128)(2,1)S(1)}, u32[]{:S(2)}, u32[]{:S(2)}) async-start(bf16[4,27,32,128]{3,2,1,0:T(8,128)(2,1)} %broadcast_in_dim.5), calls=%async_computation.1 | async-start | bytes 1769472 | tf_op jit(solution)/shard_map/all_to_all | solution.py:333
  19.0 0.7 copy-start.1
  20.4 10.5 %collective-permute-start.1 = (bf16[80,128]{1,0:T(8,128)(2,1)S(1)}, bf16[80,128]{1,0:T(8,128)(2,1)S(1)}, u32[]{:S(2)}, u32[]{:S(2)}) collective-permute-start(bf16[80,128]{1,0:T(8,128)(2,1)S(1)} %get-tuple-element.18), channel_id=1, source_target_pairs={{4,0},{8,4},{12,8},{20,16},{24,20},{28,24},{36,32},{40,36},{44,40}... | collective-permute-start | bytes 61448 | tf_op jit(solution)/shard_map/ppermute | solution.py:312
  29.0 3.1 %collective-permute-start = (bf16[80,128]{1,0:T(8,128)(2,1)S(1)}, bf16[80,128]{1,0:T(8,128)(2,1)S(1)}, u32[]{:S(2)}, u32[]{:S(2)}) collective-permute-start(bf16[80,128]{1,0:T(8,128)(2,1)S(1)} %get-tuple-element.19), channel_id=1, source_target_pairs={{0,4},{4,8},{8,12},{16,20},{20,24},{24,28},{32,36},{36,40},{40,44}... | collective-permute-start | bytes 61448 | tf_op jit(solution)/shard_map/ppermute | solution.py:312
  32.1 5.8 %collective-permute-start.2 = (bf16[80,128]{1,0:T(8,128)(2,1)S(1)}, bf16[80,128]{1,0:T(8,128)(2,1)S(1)}, u32[]{:S(2)}, u32[]{:S(2)}) collective-permute-start(bf16[80,128]{1,0:T(8,128)(2,1)S(1)} %pad_maximum_fusion.1), channel_id=1, source_target_pairs={{0,16},{4,20},{8,24},{12,28},{16,32},{20,36},{24,40},{28,44},{32,4... | collective-permute-start | bytes 61448 | tf_op jit(solution)/shard_map/ppermute | solution.py:312
  36.5 7.5 %collective-permute-start.3 = (bf16[80,128]{1,0:T(8,128)(2,1)S(1)}, bf16[80,128]{1,0:T(8,128)(2,1)S(1)}, u32[]{:S(2)}, u32[]{:S(2)}) collective-permute-start(bf16[80,128]{1,0:T(8,128)(2,1)S(1)} %pad_maximum_fusion.2), channel_id=1, source_target_pairs={{16,0},{20,4},{24,8},{28,12},{32,16},{36,20},{40,24},{44,28},{48,3... | collective-permute-start | bytes 61448 | tf_op jit(solution)/shard_map/ppermute | solution.py:312
  44.0 0.7 copy-start.2
  89.6 14.9 %all-to-all-start.4 = ((bf16[16,56,128]{2,1,0:T(8,128)(2,1)}), bf16[16,56,128]{2,1,0:T(8,128)(2,1)S(1)}, u32[]{:S(2)}, u32[]{:S(2)}) async-start(bf16[16,56,128]{2,1,0:T(8,128)(2,1)} %bitcast.18), calls=%async_computation.4 | async-start | bytes 458752 | tf_op jit(solution)/shard_map/all_to_all | solution.py:327

commit v5 on v4

--- a/solution.py
+++ b/solution.py
@@ -62,7 +62,7 @@
 
 def rims_kernel(send, mask, gathered, local, to_b, face_a):
     for brick in range(2):
-        rows = gathered[:, 0, brick].reshape(128, 512).astype(F32) * mask[brick : brick + 1, :]
+        rows = gathered[:, brick].reshape(128, 512).astype(F32) * mask[brick : brick + 1, :]
         local[brick] = rows.T.reshape(8, 8, 8, 128)
 
     def chosen(move):
@@ -78,13 +78,16 @@
 
 
 def main_kernel(
-    near, chan, place, mask, local, from_bm, from_bp, from_am, from_ap, gathered, weights, own_weights,
+    near, chan, place, mask, local, from_bm, from_bp, from_am, from_ap, extra0, extra1, extra2, extra3,
     act_out, sent, own_out,
-    blocks, grads, own_block, act_all, terms, stage,
+    blocks, grads, own_block, act_all, terms, stage, extra,
 ):
     z = lax.broadcasted_iota(jnp.int32, (1, 8, 128), 1)
     from_b = {-1: from_bm, 1: from_bp}
     from_a = {-1: from_am, 1: from_ap}
+    own_weights = extra0
+    for by, part in enumerate((extra0, extra1, extra2, extra3)):
+        extra[lax.rem(chan[0] - by + 4, 4)] = part[...]
 
     def arrived(dx, dy):
         if dx == 0:
@@ -131,7 +134,7 @@
             ],
             axis=1,
         )
-        right = jnp.concatenate([weights[:, 9 * dx + o].reshape(128, 128) for o in range(9)], axis=0)
+        right = jnp.concatenate([extra[:, 9 * dx + o].reshape(128, 128) for o in range(9)], axis=0)
         pre = pre + jnp.dot(left, right, preferred_element_type=F32)
     pre = pre.reshape(64, 2, 8, 128)
 
@@ -141,7 +144,9 @@
         pre_act = pre[:, brick].reshape(512, 128).T * on
         gate = jax.nn.sigmoid(pre_act)
         act_all[brick] = (pre_act * gate).astype(BF)
-        cotangent = gathered[:, 1, brick].reshape(128, 512).astype(F32)
+        cotangent = jnp.concatenate(
+            [extra[:, 27 + 4 * brick + i].reshape(128, 128).astype(F32) for i in range(4)], axis=1
+        )
         grad = cotangent * on * gate * (1.0 + pre_act * (1.0 - gate))
         back.append(grad.T.reshape(64, 8, 128))
     start = pl.multiple_of(chan[0] * 32, 32)
@@ -327,6 +332,11 @@
     return lax.all_to_all(values, "space", 0, 0, tiled=True, axis_index_groups=groups)
 
 
+def round_chan(shard, by):
+    count = lax.axis_size("chan")
+    return lax.ppermute(shard, "chan", [(i, (i + by) % count) for i in range(count)])
+
+
 def from_all_chan(part):
     count = lax.axis_size("chan")
     copies = jnp.broadcast_to(part[None], (count,) + part.shape)
@@ -340,9 +350,10 @@
     place = jnp.stack([where % GROUP, where // GROUP])
     planes = lax.axis_size("space") // GROUP
     mask = unpack_mask(mask_packed)
-    values = jnp.stack([features.transpose(1, 0, 2), cotangent.transpose(1, 0, 2)])
-    all_weights = from_all_chan(weights)
-    gathered = from_all_chan(values)
+    gathered = from_all_chan(features.transpose(1, 0, 2))
+    by_lanes = cotangent.reshape(32, 8, 128).transpose(1, 0, 2)
+    extra = jnp.concatenate([weights, by_lanes], axis=0)
+    extras = [extra] + [round_chan(extra, by) for by in (1, 2, 3)]
     local, to_b, face_a = call(
         rims_kernel, "rims", [send], [mask, gathered],
         [((2, 8, 8, 8, 128), F32), ((2, 80, 128), BF), ((2, 64, 128), BF)], [], 16,
@@ -353,13 +364,14 @@
     from_am, from_ap = passed_along(to_am, 4), passed_along(to_ap, -4)
     act, sent, own = call(
         main_kernel, "conv", [neighbours, chan, place],
-        [mask, local, from_bm, from_bp, from_am, from_ap, gathered, all_weights, weights],
+        [mask, local, from_bm, from_bp, from_am, from_ap, *extras],
         [
             ((2, 32, 512), BF), ((GROUP * SENT, 128), BF), ((2, 8, 8, 8, 128), F32),
         ],
         [
             ((3, 10, 10, 16, 128), BF), ((12, 12, 16, 128), BF), ((10, 10, 16, 128), BF),
             ((2, 128, 512), BF), ((3, 2, 10, 10, 8, 128), F32), ((GROUP * SENT, 128), F32),
+            ((4, 35, 32, 128), BF),
         ],
         40,
     )

time: 106 us -> 111 us (1.047)
  starting transfers between devices: 28.3 us -> 33.9 us
  waiting for transfers between devices: 22.3 us -> 23.8 us
    ppermute x0 -> x3, starting transfers between devices: none -> 10.2 us  [round_chan(): lax.ppermute(shard, 'chan', [(i, (i + by) % count) for i in range(count)])]
    all_to_all x2 -> x1, starting transfers between devices: 8.48 us -> 3.41 us  [from_all_chan(): return lax.all_to_all(copies, 'chan', 0, 0, tiled=True)]
    all_to_all x2 -> x1, waiting for transfers between devices: 6.09 us -> 7.88 us  [from_all_chan(): return lax.all_to_all(copies, 'chan', 0, 0, tiled=True)]
    broadcast_in_dim x2 -> x1, local copies, waits for them, and re-layouts: 1.88 us -> 0.72 us  [from_all_chan(): copies = jnp.broadcast_to(part[None], (count,) + part.shape)]
    unnamed x10 -> x12, local copies, waits for them, and re-layouts: 3.34 us -> 2.69 us
  transfers between devices with their start and end apart: 7 -> 9, of which waited for: 4 -> 4; matrix products, arithmetic and copies ran while one was open for 2% -> 2% of each run, Pallas kernels for 2% -> 1%
where the time goes in v5:
time: 111 us
  blocking collectives  37.5 us (34%)
  starting transfers between devices  33.9 us (31%)
  waiting for transfers between devices  23.8 us (21%)
  Pallas kernels  8.95 us (8%)
  local copies, waits for them, and re-layouts  4.63 us (4%)
    all_to_all x2, blocking collectives, exchanged(): lax.all_to_all(values, 'space', 0, 0, tiled=True, axis_index_groups=groups)  37.5 us
    ppermute x4, starting transfers between devices, passed_along(): return lax.ppermute(shard, 'space', pairs)  16.6 us
    ppermute x3, starting transfers between devices, round_chan(): lax.ppermute(shard, 'chan', [(i, (i + by) % count) for i in range(count)])  10.2 us
    pallas_call x5, Pallas kernels, call(): pl.pallas_call(kernel, out_shape=shapes, in_specs=[SMEM] * len(smem) + [V...  8.95 us
    all_to_all x1, waiting for transfers between devices, exchanged(): lax.all_to_all(values, 'space', 0, 0, tiled=True, axis_index_groups=groups)  8.9 us
    all_to_all x1, waiting for transfers between devices, from_all_chan(): return lax.all_to_all(copies, 'chan', 0, 0, tiled=True)  7.88 us
    ppermute x4, waiting for transfers between devices, passed_along(): return lax.ppermute(shard, 'space', pairs)  7.03 us
    all_to_all x1, starting transfers between devices, exchanged(): lax.all_to_all(values, 'space', 0, 0, tiled=True, axis_index_groups=groups)  3.73 us
  transfers between devices with their start and end apart: 9, of which 4 were waited for; matrix products, arithmetic and copies ran while one was open for 2% of the time, Pallas kernels for 1%

profile of v5, /device:TPU:1, one launch (start us, length us, event | category | flops | bytes accessed | tf_op | source)
XLA Modules:
  0.0 110.7 jit_solution(9655585038056223640)
XLA Ops:
  0.6 0.9 reshape.34
  1.6 5.2 %collective-permute-start.6 = (bf16[35,32,128]{2,1,0:T(8,128)(2,1)S(1)}, bf16[35,32,128]{2,1,0:T(8,128)(2,1)S(1)}, u32[]{:S(2)}, u32[]{:S(2)}) collective-permute-start(bf16[35,32,128]{2,1,0:T(8,128)(2,1)S(1)} %pad_maximum_fusion.extra0), channel_id=1, source_target_pairs={{0,3},{1,0},{2,1},{3,2},{4,7},{5,4},{6,5},{7,6},{8,11},{9,8},{10,9... | collective-permute-start | bytes 860168 | tf_op jit(solution)/shard_map/ppermute | solution.py:337
  6.9 2.4 %collective-permute-start.5 = (bf16[35,32,128]{2,1,0:T(8,128)(2,1)S(1)}, bf16[35,32,128]{2,1,0:T(8,128)(2,1)S(1)}, u32[]{:S(2)}, u32[]{:S(2)}) collective-permute-start(bf16[35,32,128]{2,1,0:T(8,128)(2,1)S(1)} %pad_maximum_fusion.extra0), channel_id=1, source_target_pairs={{0,2},{1,3},{2,0},{3,1},{4,6},{5,7},{6,4},{7,5},{8,10},{9,11},{10,... | collective-permute-start | bytes 860168 | tf_op jit(solution)/shard_map/ppermute | solution.py:337
  9.3 2.5 %collective-permute-start.4 = (bf16[35,32,128]{2,1,0:T(8,128)(2,1)S(1)}, bf16[35,32,128]{2,1,0:T(8,128)(2,1)S(1)}, u32[]{:S(2)}, u32[]{:S(2)}) collective-permute-start(bf16[35,32,128]{2,1,0:T(8,128)(2,1)S(1)} %pad_maximum_fusion.extra0), channel_id=1, source_target_pairs={{0,1},{1,2},{2,3},{3,0},{4,5},{5,6},{6,7},{7,4},{8,9},{9,10},{10,1... | collective-permute-start | bytes 860168 | tf_op jit(solution)/shard_map/ppermute | solution.py:337
  11.9 0.7 broadcast_in_dim.2
  12.6 3.4 %all-to-all-start = ((bf16[4,2,32,512]{3,2,1,0:T(8,128)(2,1)}), bf16[4,2,32,512]{3,2,1,0:T(8,128)(2,1)S(1)}, u32[]{:S(2)}, u32[]{:S(2)}) async-start(bf16[4,2,32,512]{3,2,1,0:T(8,128)(2,1)} %broadcast_in_dim.2), calls=%async_computation | async-start | bytes 524288 | tf_op jit(solution)/shard_map/all_to_all | solution.py:343
  16.9 7.9 %all-to-all-done.gathered = bf16[4,2,32,512]{3,2,1,0:T(8,128)(2,1)S(1)} async-done(((bf16[4,2,32,512]{3,2,1,0:T(8,128)(2,1)}), bf16[4,2,32,512]{3,2,1,0:T(8,128)(2,1)S(1)}, u32[]{:S(2)}, u32[]{:S(2)}) %all-to-all-start) | async-done | bytes 262176 | tf_op jit(solution)/shard_map/all_to_all | solution.py:343
  24.8 0.7 rims.1
  25.5 6.3 %collective-permute-start.1 = (bf16[80,128]{1,0:T(8,128)(2,1)S(1)}, bf16[80,128]{1,0:T(8,128)(2,1)S(1)}, u32[]{:S(2)}, u32[]{:S(2)}) collective-permute-start(bf16[80,128]{1,0:T(8,128)(2,1)S(1)} %get-tuple-element.21), channel_id=1, source_target_pairs={{4,0},{8,4},{12,8},{20,16},{24,20},{28,24},{36,32},{40,36},{44,40}... | collective-permute-start | bytes 61448 | tf_op jit(solution)/shard_map/ppermute | solution.py:317
  31.8 3.3 %collective-permute-start = (bf16[80,128]{1,0:T(8,128)(2,1)S(1)}, bf16[80,128]{1,0:T(8,128)(2,1)S(1)}, u32[]{:S(2)}, u32[]{:S(2)}) collective-permute-start(bf16[80,128]{1,0:T(8,128)(2,1)S(1)} %get-tuple-element.22), channel_id=1, source_target_pairs={{0,4},{4,8},{8,12},{16,20},{20,24},{24,28},{32,36},{36,40},{40,44}... | collective-permute-start | bytes 61448 | tf_op jit(solution)/shard_map/ppermute | solution.py:317
  35.1 0.9 collective-permute-done.from_bm
  36.0 5.8 %collective-permute-start.2 = (bf16[80,128]{1,0:T(8,128)(2,1)S(1)}, bf16[80,128]{1,0:T(8,128)(2,1)S(1)}, u32[]{:S(2)}, u32[]{:S(2)}) collective-permute-start(bf16[80,128]{1,0:T(8,128)(2,1)S(1)} %pad_maximum_fusion.1), channel_id=1, source_target_pairs={{0,16},{4,20},{8,24},{12,28},{16,32},{20,36},{24,40},{28,44},{32,4... | collective-permute-start | bytes 61448 | tf_op jit(solution)/shard_map/ppermute | solution.py:317
  41.8 1.3 %collective-permute-start.3 = (bf16[80,128]{1,0:T(8,128)(2,1)S(1)}, bf16[80,128]{1,0:T(8,128)(2,1)S(1)}, u32[]{:S(2)}, u32[]{:S(2)}) collective-permute-start(bf16[80,128]{1,0:T(8,128)(2,1)S(1)} %pad_maximum_fusion.2), channel_id=1, source_target_pairs={{16,0},{20,4},{24,8},{28,12},{32,16},{36,20},{40,24},{44,28},{48,3... | collective-permute-start | bytes 61448 | tf_op jit(solution)/shard_map/ppermute | solution.py:317
  43.2 6.2 %collective-permute-done.3.from_ap = bf16[80,128]{1,0:T(8,128)(2,1)S(1)} collective-permute-done((bf16[80,128]{1,0:T(8,128)(2,1)S(1)}, bf16[80,128]{1,0:T(8,128)(2,1)S(1)}, u32[]{:S(2)}, u32[]{:S(2)}) %collective-permute-start.3) | collective-permute-done | bytes 20512 | tf_op jit(solution)/shard_map/ppermute | solution.py:317
  50.1 5.9 %conv.1 = (bf16[2,32,512]{2,1,0:T(8,128)(2,1)S(1)}, bf16[1152,128]{1,0:T(8,128)(2,1)S(1)}, f32[2,8,8,8,128]{4,3,2,1,0:T(8,128)S(1)}) custom-call(s32[2,26]{1,0:T(2,128)S(1)} %copy-done.1, s32[1]{0:T(128)} %bitcast.chan, s32[2]{0:T(128)S(1)} %pad_add_fusion.place, f32[2,512]{1,0:T(2,128)S(1)} %and_convert_fusion.mask, ...), custom_call_target="tpu_custom_call" | custom-call | tf_op jit(solution)/shard_map/conv/pallas_call | solution.py:301
  56.0 20.6 %all_to_all.39 = bf16[16,72,128]{2,1,0:T(8,128)(2,1)S(1)} all-to-all(bf16[16,72,128]{2,1,0:T(8,128)(2,1)S(1)} %bitcast.31), channel_id=1, replica_groups={{0,4,8,12,16,20,24,28,32,36,40,44,48,52,56,60},{64,68,72,76,80,84,88,92..., dimensions={0} | all-to-all | bytes 589824 | tf_op jit(solution)/shard_map/all_to_all | solution.py:332
  76.6 0.8 middle.1
  77.3 16.9 %all_to_all.40 = bf16[8,80,128]{2,1,0:T(8,128)(2,1)S(1)} all-to-all(bf16[8,80,128]{2,1,0:T(8,128)(2,1)S(1)} %bitcast.30), channel_id=1, replica_groups={{0,64,128,192,256,320,384,448},{4,68,132,196,260,324,388,452},{8,72,136..., dimensions={0} | all-to-all | bytes 327680 | tf_op jit(solution)/shard_map/all_to_all | solution.py:332
  94.2 0.7 sums.1
  95.0 3.7 %all-to-all-start.3 = ((bf16[16,56,128]{2,1,0:T(8,128)(2,1)}), bf16[16,56,128]{2,1,0:T(8,128)(2,1)S(1)}, u32[]{:S(2)}, u32[]{:S(2)}) async-start(bf16[16,56,128]{2,1,0:T(8,128)(2,1)} %bitcast.16), calls=%async_computation.3 | async-start | bytes 458752 | tf_op jit(solution)/shard_map/all_to_all | solution.py:332
  99.4 0.9 grad.1
  100.2 0.7 copy.15
  101.0 8.9 %all-to-all-done.3 = bf16[16,56,128]{2,1,0:T(8,128)(2,1)S(1)} async-done(((bf16[16,56,128]{2,1,0:T(8,128)(2,1)}), bf16[16,56,128]{2,1,0:T(8,128)(2,1)S(1)}, u32[]{:S(2)}, u32[]{:S(2)}) %all-to-all-start.3) | async-done | bytes 229408 | tf_op jit(solution)/shard_map/all_to_all | solution.py:332
  109.9 0.8 convert.1
  (32 shorter events, 2.4 us)
Async XLA Ops:
  0.6 1.0 copy-start.2
  1.6 10.2 %copy-start.3 = (bf16[32,2,512]{2,1,0:T(2,128)(2,1)S(1)}, bf16[32,2,512]{2,1,0:T(2,128)(2,1)}, u32[]{:S(2)}) copy-start(bf16[32,2,512]{2,1,0:T(2,128)(2,1)} %param.6) | copy-start | bytes 196612
  1.6 47.7 %collective-permute-start.6 = (bf16[35,32,128]{2,1,0:T(8,128)(2,1)S(1)}, bf16[35,32,128]{2,1,0:T(8,128)(2,1)S(1)}, u32[]{:S(2)}, u32[]{:S(2)}) collective-permute-start(bf16[35,32,128]{2,1,0:T(8,128)(2,1)S(1)} %pad_maximum_fusion.extra0), channel_id=1, source_target_pairs={{0,3},{1,0},{2,1},{3,2},{4,7},{5,4},{6,5},{7,6},{8,11},{9,8},{10,9... | collective-permute-start | bytes 860168 | tf_op jit(solution)/shard_map/ppermute | solution.py:337
  6.9 42.5 %collective-permute-start.5 = (bf16[35,32,128]{2,1,0:T(8,128)(2,1)S(1)}, bf16[35,32,128]{2,1,0:T(8,128)(2,1)S(1)}, u32[]{:S(2)}, u32[]{:S(2)}) collective-permute-start(bf16[35,32,128]{2,1,0:T(8,128)(2,1)S(1)} %pad_maximum_fusion.extra0), channel_id=1, source_target_pairs={{0,2},{1,3},{2,0},{3,1},{4,6},{5,7},{6,4},{7,5},{8,10},{9,11},{10,... | collective-permute-start | bytes 860168 | tf_op jit(solution)/shard_map/ppermute | solution.py:337
  9.3 40.1 %collective-permute-start.4 = (bf16[35,32,128]{2,1,0:T(8,128)(2,1)S(1)}, bf16[35,32,128]{2,1,0:T(8,128)(2,1)S(1)}, u32[]{:S(2)}, u32[]{:S(2)}) collective-permute-start(bf16[35,32,128]{2,1,0:T(8,128)(2,1)S(1)} %pad_maximum_fusion.extra0), channel_id=1, source_target_pairs={{0,1},{1,2},{2,3},{3,0},{4,5},{5,6},{6,7},{7,4},{8,9},{9,10},{10,1... | collective-permute-start | bytes 860168 | tf_op jit(solution)/shard_map/ppermute | solution.py:337
  12.6 12.2 %all-to-all-start = ((bf16[4,2,32,512]{3,2,1,0:T(8,128)(2,1)}), bf16[4,2,32,512]{3,2,1,0:T(8,128)(2,1)S(1)}, u32[]{:S(2)}, u32[]{:S(2)}) async-start(bf16[4,2,32,512]{3,2,1,0:T(8,128)(2,1)} %broadcast_in_dim.2), calls=%async_computation | async-start | bytes 524288 | tf_op jit(solution)/shard_map/all_to_all | solution.py:343
  16.0 0.7 copy-start.4
  16.9 7.9 %copy-start = (s32[1,8,1]{1,2,0:T(1,128)S(1)}, s32[1,8,1]{1,2,0:T(1,128)}, u32[]{:S(2)}) copy-start(s32[1,8,1]{1,2,0:T(1,128)} %param.9) | copy-start | bytes 100
  25.5 9.6 %collective-permute-start.1 = (bf16[80,128]{1,0:T(8,128)(2,1)S(1)}, bf16[80,128]{1,0:T(8,128)(2,1)S(1)}, u32[]{:S(2)}, u32[]{:S(2)}) collective-permute-start(bf16[80,128]{1,0:T(8,128)(2,1)S(1)} %get-tuple-element.21), channel_id=1, source_target_pairs={{4,0},{8,4},{12,8},{20,16},{24,20},{28,24},{36,32},{40,36},{44,40}... | collective-permute-start | bytes 61448 | tf_op jit(solution)/shard_map/ppermute | solution.py:317
  31.8 4.2 %collective-permute-start = (bf16[80,128]{1,0:T(8,128)(2,1)S(1)}, bf16[80,128]{1,0:T(8,128)(2,1)S(1)}, u32[]{:S(2)}, u32[]{:S(2)}) collective-permute-start(bf16[80,128]{1,0:T(8,128)(2,1)S(1)} %get-tuple-element.22), channel_id=1, source_target_pairs={{0,4},{4,8},{8,12},{16,20},{20,24},{24,28},{32,36},{36,40},{40,44}... | collective-permute-start | bytes 61448 | tf_op jit(solution)/shard_map/ppermute | solution.py:317
  36.0 7.2 %collective-permute-start.2 = (bf16[80,128]{1,0:T(8,128)(2,1)S(1)}, bf16[80,128]{1,0:T(8,128)(2,1)S(1)}, u32[]{:S(2)}, u32[]{:S(2)}) collective-permute-start(bf16[80,128]{1,0:T(8,128)(2,1)S(1)} %pad_maximum_fusion.1), channel_id=1, source_target_pairs={{0,16},{4,20},{8,24},{12,28},{16,32},{20,36},{24,40},{28,44},{32,4... | collective-permute-start | bytes 61448 | tf_op jit(solution)/shard_map/ppermute | solution.py:317
  41.8 7.5 %collective-permute-start.3 = (bf16[80,128]{1,0:T(8,128)(2,1)S(1)}, bf16[80,128]{1,0:T(8,128)(2,1)S(1)}, u32[]{:S(2)}, u32[]{:S(2)}) collective-permute-start(bf16[80,128]{1,0:T(8,128)(2,1)S(1)} %pad_maximum_fusion.2), channel_id=1, source_target_pairs={{16,0},{20,4},{24,8},{28,12},{32,16},{36,20},{40,24},{44,28},{48,3... | collective-permute-start | bytes 61448 | tf_op jit(solution)/shard_map/ppermute | solution.py:317
  49.4 0.7 copy-start.1
  95.0 14.9 %all-to-all-start.3 = ((bf16[16,56,128]{2,1,0:T(8,128)(2,1)}), bf16[16,56,128]{2,1,0:T(8,128)(2,1)S(1)}, u32[]{:S(2)}, u32[]{:S(2)}) async-start(bf16[16,56,128]{2,1,0:T(8,128)(2,1)} %bitcast.16), calls=%async_computation.3 | async-start | bytes 458752 | tf_op jit(solution)/shard_map/all_to_all | solution.py:332

commit v6 on v5

--- a/solution.py
+++ b/solution.py
@@ -78,16 +78,13 @@
 
 
 def main_kernel(
-    near, chan, place, mask, local, from_bm, from_bp, from_am, from_ap, extra0, extra1, extra2, extra3,
+    near, chan, place, mask, local, from_bm, from_bp, from_am, from_ap, extra, own_weights,
     act_out, sent, own_out,
-    blocks, grads, own_block, act_all, terms, stage, extra,
+    blocks, grads, own_block, act_all, terms, stage,
 ):
     z = lax.broadcasted_iota(jnp.int32, (1, 8, 128), 1)
     from_b = {-1: from_bm, 1: from_bp}
     from_a = {-1: from_am, 1: from_ap}
-    own_weights = extra0
-    for by, part in enumerate((extra0, extra1, extra2, extra3)):
-        extra[lax.rem(chan[0] - by + 4, 4)] = part[...]
 
     def arrived(dx, dy):
         if dx == 0:
@@ -332,11 +329,6 @@
     return lax.all_to_all(values, "space", 0, 0, tiled=True, axis_index_groups=groups)
 
 
-def round_chan(shard, by):
-    count = lax.axis_size("chan")
-    return lax.ppermute(shard, "chan", [(i, (i + by) % count) for i in range(count)])
-
-
 def from_all_chan(part):
     count = lax.axis_size("chan")
     copies = jnp.broadcast_to(part[None], (count,) + part.shape)
@@ -353,7 +345,7 @@
     gathered = from_all_chan(features.transpose(1, 0, 2))
     by_lanes = cotangent.reshape(32, 8, 128).transpose(1, 0, 2)
     extra = jnp.concatenate([weights, by_lanes], axis=0)
-    extras = [extra] + [round_chan(extra, by) for by in (1, 2, 3)]
+    extra = from_all_chan(extra)
     local, to_b, face_a = call(
         rims_kernel, "rims", [send], [mask, gathered],
         [((2, 8, 8, 8, 128), F32), ((2, 80, 128), BF), ((2, 64, 128), BF)], [], 16,
@@ -364,14 +356,13 @@
     from_am, from_ap = passed_along(to_am, 4), passed_along(to_ap, -4)
     act, sent, own = call(
         main_kernel, "conv", [neighbours, chan, place],
-        [mask, local, from_bm, from_bp, from_am, from_ap, *extras],
+        [mask, local, from_bm, from_bp, from_am, from_ap, extra, weights],
         [
             ((2, 32, 512), BF), ((GROUP * SENT, 128), BF), ((2, 8, 8, 8, 128), F32),
         ],
         [
             ((3, 10, 10, 16, 128), BF), ((12, 12, 16, 128), BF), ((10, 10, 16, 128), BF),
             ((2, 128, 512), BF), ((3, 2, 10, 10, 8, 128), F32), ((GROUP * SENT, 128), F32),
-            ((4, 35, 32, 128), BF),
         ],
         40,
     )

time: 111 us -> 102 us (0.919)
  starting transfers between devices: 33.9 us -> 27 us
  waiting for transfers between devices: 23.8 us -> 19.8 us
  local copies, waits for them, and re-layouts: 4.63 us -> 6.04 us
    ppermute x3 -> x0, starting transfers between devices: 10.2 us -> none  [round_chan(): lax.ppermute(shard, 'chan', [(i, (i + by) % count) for i in range(count)])]
    all_to_all x1 -> x2, starting transfers between devices: 3.41 us -> 8.5 us  [from_all_chan(): return lax.all_to_all(copies, 'chan', 0, 0, tiled=True)]
    all_to_all x1 -> x2, waiting for transfers between devices: 7.88 us -> 3.63 us  [from_all_chan(): return lax.all_to_all(copies, 'chan', 0, 0, tiled=True)]
    ppermute x4, starting transfers between devices: 16.6 us -> 14.7 us  [passed_along(): return lax.ppermute(shard, 'space', pairs)]
    unnamed x12 -> x8, local copies, waits for them, and re-layouts: 2.69 us -> 1.41 us
    broadcast_in_dim x1 -> x2, local copies, waits for them, and re-layouts: 0.72 us -> 1.89 us  [from_all_chan(): copies = jnp.broadcast_to(part[None], (count,) + part.shape)]
  transfers between devices with their start and end apart: 9 -> 7, of which waited for: 4 -> 4; matrix products, arithmetic and copies ran while one was open for 2% -> 3% of each run, Pallas kernels for 1% -> 2%
where the time goes in v6:
time: 102 us; the launch traced here: 101 us
  blocking collectives  37.5 us (37%)
  starting transfers between devices  27 us (26%)
  waiting for transfers between devices  19.8 us (19%)
  Pallas kernels  8.94 us (9%)
  local copies, waits for them, and re-layouts  6.04 us (6%)
    all_to_all x2, blocking collectives, exchanged(): lax.all_to_all(values, 'space', 0, 0, tiled=True, axis_index_groups=groups)  37.5 us
    ppermute x4, starting transfers between devices, passed_along(): return lax.ppermute(shard, 'space', pairs)  14.7 us
    pallas_call x5, Pallas kernels, call(): pl.pallas_call(kernel, out_shape=shapes, in_specs=[SMEM] * len(smem) + [V...  8.94 us
    all_to_all x1, waiting for transfers between devices, exchanged(): lax.all_to_all(values, 'space', 0, 0, tiled=True, axis_index_groups=groups)  8.9 us
    all_to_all x2, starting transfers between devices, from_all_chan(): return lax.all_to_all(copies, 'chan', 0, 0, tiled=True)  8.5 us
    ppermute x4, waiting for transfers between devices, passed_along(): return lax.ppermute(shard, 'space', pairs)  7.3 us
    all_to_all x1, starting transfers between devices, exchanged(): lax.all_to_all(values, 'space', 0, 0, tiled=True, axis_index_groups=groups)  3.73 us
    all_to_all x2, waiting for transfers between devices, from_all_chan(): return lax.all_to_all(copies, 'chan', 0, 0, tiled=True)  3.63 us
  transfers between devices with their start and end apart: 7, of which 4 were waited for; matrix products, arithmetic and copies ran while one was open for 3% of the time, Pallas kernels for 2%

profile of v6, /device:TPU:1, one launch (start us, length us, event | category | flops | bytes accessed | tf_op | source)
XLA Modules:
  0.0 101.0 jit_solution(12868872711192008293)
XLA Ops:
  0.6 0.9 copy.9
  1.5 0.7 broadcast_in_dim.4
  2.3 4.8 %all-to-all-start = ((bf16[4,2,32,512]{3,2,1,0:T(8,128)(2,1)}), bf16[4,2,32,512]{3,2,1,0:T(8,128)(2,1)S(1)}, u32[]{:S(2)}, u32[]{:S(2)}) async-start(bf16[4,2,32,512]{3,2,1,0:T(8,128)(2,1)} %broadcast_in_dim.4), calls=%async_computation | async-start | bytes 524288 | tf_op jit(solution)/shard_map/all_to_all | solution.py:335
  7.2 0.7 shift_right_logical.20
  8.0 0.9 reshape.35
  9.0 3.6 %all-to-all-done.gathered = bf16[4,2,32,512]{3,2,1,0:T(8,128)(2,1)S(1)} async-done(((bf16[4,2,32,512]{3,2,1,0:T(8,128)(2,1)}), bf16[4,2,32,512]{3,2,1,0:T(8,128)(2,1)S(1)}, u32[]{:S(2)}, u32[]{:S(2)}) %all-to-all-start) | async-done | bytes 262176 | tf_op jit(solution)/shard_map/all_to_all | solution.py:335
  12.6 1.2 %broadcast_in_dim.5 = bf16[4,35,32,128]{3,2,1,0:T(8,128)(2,1)} broadcast(bf16[35,32,128]{2,1,0:T(8,128)(2,1)S(1)} %pad_maximum_fusion), dimensions={1,2,3} | broadcast | bytes 1433600 | tf_op jit(solution)/shard_map/broadcast_in_dim | solution.py:334
  13.8 3.7 %all-to-all-start.1 = ((bf16[4,35,32,128]{3,2,1,0:T(8,128)(2,1)}), bf16[4,35,32,128]{3,2,1,0:T(8,128)(2,1)S(1)}, u32[]{:S(2)}, u32[]{:S(2)}) async-start(bf16[4,35,32,128]{3,2,1,0:T(8,128)(2,1)} %broadcast_in_dim.5), calls=%async_computation.1 | async-start | bytes 2293760 | tf_op jit(solution)/shard_map/all_to_all | solution.py:335
  17.5 0.7 rims.1
  18.2 8.5 %collective-permute-start.1 = (bf16[80,128]{1,0:T(8,128)(2,1)S(1)}, bf16[80,128]{1,0:T(8,128)(2,1)S(1)}, u32[]{:S(2)}, u32[]{:S(2)}) collective-permute-start(bf16[80,128]{1,0:T(8,128)(2,1)S(1)} %get-tuple-element.18), channel_id=1, source_target_pairs={{4,0},{8,4},{12,8},{20,16},{24,20},{28,24},{36,32},{40,36},{44,40}... | collective-permute-start | bytes 61448 | tf_op jit(solution)/shard_map/ppermute | solution.py:314
  26.7 1.9 %collective-permute-start = (bf16[80,128]{1,0:T(8,128)(2,1)S(1)}, bf16[80,128]{1,0:T(8,128)(2,1)S(1)}, u32[]{:S(2)}, u32[]{:S(2)}) collective-permute-start(bf16[80,128]{1,0:T(8,128)(2,1)S(1)} %get-tuple-element.19), channel_id=1, source_target_pairs={{0,4},{4,8},{8,12},{16,20},{20,24},{24,28},{32,36},{36,40},{40,44}... | collective-permute-start | bytes 61448 | tf_op jit(solution)/shard_map/ppermute | solution.py:314
  28.7 1.1 %collective-permute-done.from_bm = bf16[80,128]{1,0:T(8,128)(2,1)S(1)} collective-permute-done((bf16[80,128]{1,0:T(8,128)(2,1)S(1)}, bf16[80,128]{1,0:T(8,128)(2,1)S(1)}, u32[]{:S(2)}, u32[]{:S(2)}) %collective-permute-start) | collective-permute-done | bytes 20512 | tf_op jit(solution)/shard_map/ppermute | solution.py:314
  29.8 3.0 %collective-permute-start.2 = (bf16[80,128]{1,0:T(8,128)(2,1)S(1)}, bf16[80,128]{1,0:T(8,128)(2,1)S(1)}, u32[]{:S(2)}, u32[]{:S(2)}) collective-permute-start(bf16[80,128]{1,0:T(8,128)(2,1)S(1)} %pad_maximum_fusion.1), channel_id=1, source_target_pairs={{0,16},{4,20},{8,24},{12,28},{16,32},{20,36},{24,40},{28,44},{32,4... | collective-permute-start | bytes 61448 | tf_op jit(solution)/shard_map/ppermute | solution.py:314
  32.9 1.3 %collective-permute-start.3 = (bf16[80,128]{1,0:T(8,128)(2,1)S(1)}, bf16[80,128]{1,0:T(8,128)(2,1)S(1)}, u32[]{:S(2)}, u32[]{:S(2)}) collective-permute-start(bf16[80,128]{1,0:T(8,128)(2,1)S(1)} %pad_maximum_fusion.2), channel_id=1, source_target_pairs={{16,0},{20,4},{24,8},{28,12},{32,16},{36,20},{40,24},{44,28},{48,3... | collective-permute-start | bytes 61448 | tf_op jit(solution)/shard_map/ppermute | solution.py:314
  34.3 6.2 %collective-permute-done.3.from_ap = bf16[80,128]{1,0:T(8,128)(2,1)S(1)} collective-permute-done((bf16[80,128]{1,0:T(8,128)(2,1)S(1)}, bf16[80,128]{1,0:T(8,128)(2,1)S(1)}, u32[]{:S(2)}, u32[]{:S(2)}) %collective-permute-start.3) | collective-permute-done | bytes 20512 | tf_op jit(solution)/shard_map/ppermute | solution.py:314
  40.4 5.9 %conv.1 = (bf16[2,32,512]{2,1,0:T(8,128)(2,1)S(1)}, bf16[1152,128]{1,0:T(8,128)(2,1)S(1)}, f32[2,8,8,8,128]{4,3,2,1,0:T(8,128)S(1)}) custom-call(s32[2,26]{1,0:T(2,128)S(1)} %copy-done.2, s32[1]{0:T(128)} %bitcast.chan, s32[2]{0:T(128)S(1)} %pad_add_fusion.place, f32[2,512]{1,0:T(2,128)S(1)} %and_convert_fusion.mask, ...), custom_call_target="tpu_custom_call" | custom-call | tf_op jit(solution)/shard_map/conv/pallas_call | solution.py:298
  46.3 20.6 %all_to_all.44 = bf16[16,72,128]{2,1,0:T(8,128)(2,1)S(1)} all-to-all(bf16[16,72,128]{2,1,0:T(8,128)(2,1)S(1)} %bitcast.31), channel_id=1, replica_groups={{0,4,8,12,16,20,24,28,32,36,40,44,48,52,56,60},{64,68,72,76,80,84,88,92..., dimensions={0} | all-to-all | bytes 589824 | tf_op jit(solution)/shard_map/all_to_all | solution.py:329
  66.9 0.8 middle.1
  67.7 16.9 %all_to_all.45 = bf16[8,80,128]{2,1,0:T(8,128)(2,1)S(1)} all-to-all(bf16[8,80,128]{2,1,0:T(8,128)(2,1)S(1)} %bitcast.30), channel_id=1, replica_groups={{0,64,128,192,256,320,384,448},{4,68,132,196,260,324,388,452},{8,72,136..., dimensions={0} | all-to-all | bytes 327680 | tf_op jit(solution)/shard_map/all_to_all | solution.py:329
  84.6 0.7 sums.1
  85.3 3.7 %all-to-all-start.4 = ((bf16[16,56,128]{2,1,0:T(8,128)(2,1)}), bf16[16,56,128]{2,1,0:T(8,128)(2,1)S(1)}, u32[]{:S(2)}, u32[]{:S(2)}) async-start(bf16[16,56,128]{2,1,0:T(8,128)(2,1)} %bitcast.16), calls=%async_computation.4 | async-start | bytes 458752 | tf_op jit(solution)/shard_map/all_to_all | solution.py:329
  89.8 0.9 grad.1
  91.3 8.9 %all-to-all-done.4 = bf16[16,56,128]{2,1,0:T(8,128)(2,1)S(1)} async-done(((bf16[16,56,128]{2,1,0:T(8,128)(2,1)}), bf16[16,56,128]{2,1,0:T(8,128)(2,1)S(1)}, u32[]{:S(2)}, u32[]{:S(2)}) %all-to-all-start.4) | async-done | bytes 229408 | tf_op jit(solution)/shard_map/all_to_all | solution.py:329
  100.2 0.8 convert.1
  (25 shorter events, 1.8 us)
Async XLA Ops:
  0.6 8.3 %copy-start = (bf16[27,32,128]{2,1,0:T(8,128)(2,1)S(1)}, bf16[27,32,128]{2,1,0:T(8,128)(2,1)}, u32[]{:S(2)}) copy-start(bf16[27,32,128]{2,1,0:T(8,128)(2,1)} %own_weights.1) | copy-start | bytes 663556
  2.3 10.4 %all-to-all-start = ((bf16[4,2,32,512]{3,2,1,0:T(8,128)(2,1)}), bf16[4,2,32,512]{3,2,1,0:T(8,128)(2,1)S(1)}, u32[]{:S(2)}, u32[]{:S(2)}) async-start(bf16[4,2,32,512]{3,2,1,0:T(8,128)(2,1)} %broadcast_in_dim.4), calls=%async_computation | async-start | bytes 524288 | tf_op jit(solution)/shard_map/all_to_all | solution.py:335
  13.8 3.7 %copy-start.1 = (s32[1,8,1]{1,2,0:T(1,128)S(1)}, s32[1,8,1]{1,2,0:T(1,128)}, u32[]{:S(2)}) copy-start(s32[1,8,1]{1,2,0:T(1,128)} %param.9) | copy-start | bytes 100
  13.8 26.6 %copy-start.2 = (s32[2,26]{1,0:T(2,128)S(1)}, s32[2,26]{1,0:T(2,128)}, u32[]{:S(2)}) copy-start(s32[2,26]{1,0:T(2,128)} %near.1) | copy-start | bytes 628
  13.8 26.6 %all-to-all-start.1 = ((bf16[4,35,32,128]{3,2,1,0:T(8,128)(2,1)}), bf16[4,35,32,128]{3,2,1,0:T(8,128)(2,1)S(1)}, u32[]{:S(2)}, u32[]{:S(2)}) async-start(bf16[4,35,32,128]{3,2,1,0:T(8,128)(2,1)} %broadcast_in_dim.5), calls=%async_computation.1 | async-start | bytes 2293760 | tf_op jit(solution)/shard_map/all_to_all | solution.py:335
  18.2 10.4 %collective-permute-start.1 = (bf16[80,128]{1,0:T(8,128)(2,1)S(1)}, bf16[80,128]{1,0:T(8,128)(2,1)S(1)}, u32[]{:S(2)}, u32[]{:S(2)}) collective-permute-start(bf16[80,128]{1,0:T(8,128)(2,1)S(1)} %get-tuple-element.18), channel_id=1, source_target_pairs={{4,0},{8,4},{12,8},{20,16},{24,20},{28,24},{36,32},{40,36},{44,40}... | collective-permute-start | bytes 61448 | tf_op jit(solution)/shard_map/ppermute | solution.py:314
  26.7 3.1 %collective-permute-start = (bf16[80,128]{1,0:T(8,128)(2,1)S(1)}, bf16[80,128]{1,0:T(8,128)(2,1)S(1)}, u32[]{:S(2)}, u32[]{:S(2)}) collective-permute-start(bf16[80,128]{1,0:T(8,128)(2,1)S(1)} %get-tuple-element.19), channel_id=1, source_target_pairs={{0,4},{4,8},{8,12},{16,20},{20,24},{24,28},{32,36},{36,40},{40,44}... | collective-permute-start | bytes 61448 | tf_op jit(solution)/shard_map/ppermute | solution.py:314
  29.8 4.4 %collective-permute-start.2 = (bf16[80,128]{1,0:T(8,128)(2,1)S(1)}, bf16[80,128]{1,0:T(8,128)(2,1)S(1)}, u32[]{:S(2)}, u32[]{:S(2)}) collective-permute-start(bf16[80,128]{1,0:T(8,128)(2,1)S(1)} %pad_maximum_fusion.1), channel_id=1, source_target_pairs={{0,16},{4,20},{8,24},{12,28},{16,32},{20,36},{24,40},{28,44},{32,4... | collective-permute-start | bytes 61448 | tf_op jit(solution)/shard_map/ppermute | solution.py:314
  32.9 7.5 %collective-permute-start.3 = (bf16[80,128]{1,0:T(8,128)(2,1)S(1)}, bf16[80,128]{1,0:T(8,128)(2,1)S(1)}, u32[]{:S(2)}, u32[]{:S(2)}) collective-permute-start(bf16[80,128]{1,0:T(8,128)(2,1)S(1)} %pad_maximum_fusion.2), channel_id=1, source_target_pairs={{16,0},{20,4},{24,8},{28,12},{32,16},{36,20},{40,24},{44,28},{48,3... | collective-permute-start | bytes 61448 | tf_op jit(solution)/shard_map/ppermute | solution.py:314
  85.3 14.9 %all-to-all-start.4 = ((bf16[16,56,128]{2,1,0:T(8,128)(2,1)}), bf16[16,56,128]{2,1,0:T(8,128)(2,1)S(1)}, u32[]{:S(2)}, u32[]{:S(2)}) async-start(bf16[16,56,128]{2,1,0:T(8,128)(2,1)} %bitcast.16), calls=%async_computation.4 | async-start | bytes 458752 | tf_op jit(solution)/shard_map/all_to_all | solution.py:329

commit v7 on v6

--- a/solution.py
+++ b/solution.py
@@ -345,7 +345,7 @@
     gathered = from_all_chan(features.transpose(1, 0, 2))
     by_lanes = cotangent.reshape(32, 8, 128).transpose(1, 0, 2)
     extra = jnp.concatenate([weights, by_lanes], axis=0)
-    extra = from_all_chan(extra)
+    extra = lax.all_gather(extra, "chan", axis=0)
     local, to_b, face_a = call(
         rims_kernel, "rims", [send], [mask, gathered],
         [((2, 8, 8, 8, 128), F32), ((2, 80, 128), BF), ((2, 64, 128), BF)], [], 16,

time: 102 us -> 114 us (1.12)
  between operations: 0.82 us -> 14.2 us
  starting transfers between devices: 27 us -> 23.3 us
  waiting for transfers between devices: 19.8 us -> 22.4 us
  other arithmetic: 0.94 us -> 2.63 us
  local copies, waits for them, and re-layouts: 6.04 us -> 4.59 us
    all_to_all x2 -> x1, starting transfers between devices: 8.5 us -> 4.84 us  [from_all_chan(): return lax.all_to_all(copies, 'chan', 0, 0, tiled=True)]
    concatenate x1, other arithmetic: 0.03 us -> 1.72 us  [on_device(): extra = jnp.concatenate([weights, by_lanes], axis=0)]
    all_to_all x2 -> x1, waiting for transfers between devices: 3.63 us -> 5.28 us  [from_all_chan(): return lax.all_to_all(copies, 'chan', 0, 0, tiled=True)]
    unnamed x8 -> x14, local copies, waits for them, and re-layouts: 1.41 us -> 2.69 us
    broadcast_in_dim x2 -> x1, local copies, waits for them, and re-layouts: 1.89 us -> 0.73 us  [from_all_chan(): copies = jnp.broadcast_to(part[None], (count,) + part.shape)]
  transfers between devices with their start and end apart: 7 -> 7, of which waited for: 4 -> 5; matrix products, arithmetic and copies ran while one was open for 3% -> 2% of each run, Pallas kernels for 2% -> 1%
where the time goes in v7:
time: 114 us
  blocking collectives  37.7 us (33%)
  starting transfers between devices  23.3 us (20%)
  waiting for transfers between devices  22.4 us (20%)
  between operations  14.2 us (12%)
  Pallas kernels  8.93 us (8%)
  local copies, waits for them, and re-layouts  4.59 us (4%)
  other arithmetic  2.63 us (2%)
    all_to_all x2, blocking collectives, exchanged(): lax.all_to_all(values, 'space', 0, 0, tiled=True, axis_index_groups=groups)  37.7 us
    ppermute x4, starting transfers between devices, passed_along(): return lax.ppermute(shard, 'space', pairs)  14.7 us
    pallas_call x5, Pallas kernels, call(): pl.pallas_call(kernel, out_shape=shapes, in_specs=[SMEM] * len(smem) + [V...  8.93 us
    all_to_all x1, waiting for transfers between devices, exchanged(): lax.all_to_all(values, 'space', 0, 0, tiled=True, axis_index_groups=groups)  8.9 us
    ppermute x4, waiting for transfers between devices, passed_along(): return lax.ppermute(shard, 'space', pairs)  7.7 us
    all_to_all x1, waiting for transfers between devices, from_all_chan(): return lax.all_to_all(copies, 'chan', 0, 0, tiled=True)  5.28 us
    all_to_all x1, starting transfers between devices, from_all_chan(): return lax.all_to_all(copies, 'chan', 0, 0, tiled=True)  4.84 us
    all_to_all x1, starting transfers between devices, exchanged(): lax.all_to_all(values, 'space', 0, 0, tiled=True, axis_index_groups=groups)  3.73 us
  transfers between devices with their start and end apart: 7, of which 5 were waited for; matrix products, arithmetic and copies ran while one was open for 2% of the time, Pallas kernels for 1%

profile of v7, /device:TPU:1, one launch (start us, length us, event | category | flops | bytes accessed | tf_op | source)
XLA Modules:
  0.0 113.8 jit_solution(2286130183153442597)
XLA Ops:
  7.2 0.9 reshape.34
  8.2 1.7 %pad_maximum_fusion = bf16[35,32,128]{2,1,0:T(8,128)(2,1)} fusion(bf16[8,32,128]{2,1,0:T(8,128)(2,1)S(1)} %copy.17, bf16[27,32,128]{2,1,0:T(8,128)(2,1)} %own_weights.1), kind=kLoop, calls=%fused_computation | loop fusion | flops 143360 | bytes 573440 | tf_op jit(solution)/shard_map/concatenate | solution.py:347
  10.0 0.7 broadcast_in_dim.2
  10.7 4.8 %all-to-all-start = ((bf16[4,2,32,512]{3,2,1,0:T(8,128)(2,1)}), bf16[4,2,32,512]{3,2,1,0:T(8,128)(2,1)S(1)}, u32[]{:S(2)}, u32[]{:S(2)}) async-start(bf16[4,2,32,512]{3,2,1,0:T(8,128)(2,1)} %broadcast_in_dim.2), calls=%async_computation | async-start | bytes 524288 | tf_op jit(solution)/shard_map/all_to_all | solution.py:335
  15.8 5.3 %all-to-all-done.gathered = bf16[4,2,32,512]{3,2,1,0:T(8,128)(2,1)S(1)} async-done(((bf16[4,2,32,512]{3,2,1,0:T(8,128)(2,1)}), bf16[4,2,32,512]{3,2,1,0:T(8,128)(2,1)S(1)}, u32[]{:S(2)}, u32[]{:S(2)}) %all-to-all-start) | async-done | bytes 262176 | tf_op jit(solution)/shard_map/all_to_all | solution.py:335
  21.1 0.7 rims.1
  21.8 8.5 %collective-permute-start.1 = (bf16[80,128]{1,0:T(8,128)(2,1)S(1)}, bf16[80,128]{1,0:T(8,128)(2,1)S(1)}, u32[]{:S(2)}, u32[]{:S(2)}) collective-permute-start(bf16[80,128]{1,0:T(8,128)(2,1)S(1)} %get-tuple-element.24), channel_id=1, source_target_pairs={{4,0},{8,4},{12,8},{20,16},{24,20},{28,24},{36,32},{40,36},{44,40}... | collective-permute-start | bytes 61448 | tf_op jit(solution)/shard_map/ppermute | solution.py:314
  30.3 1.9 %collective-permute-start = (bf16[80,128]{1,0:T(8,128)(2,1)S(1)}, bf16[80,128]{1,0:T(8,128)(2,1)S(1)}, u32[]{:S(2)}, u32[]{:S(2)}) collective-permute-start(bf16[80,128]{1,0:T(8,128)(2,1)S(1)} %get-tuple-element.25), channel_id=1, source_target_pairs={{0,4},{4,8},{8,12},{16,20},{20,24},{24,28},{32,36},{36,40},{40,44}... | collective-permute-start | bytes 61448 | tf_op jit(solution)/shard_map/ppermute | solution.py:314
  32.3 1.1 collective-permute-done.from_bm
  33.4 3.0 %collective-permute-start.2 = (bf16[80,128]{1,0:T(8,128)(2,1)S(1)}, bf16[80,128]{1,0:T(8,128)(2,1)S(1)}, u32[]{:S(2)}, u32[]{:S(2)}) collective-permute-start(bf16[80,128]{1,0:T(8,128)(2,1)S(1)} %pad_maximum_fusion.1), channel_id=1, source_target_pairs={{0,16},{4,20},{8,24},{12,28},{16,32},{20,36},{24,40},{28,44},{32,4... | collective-permute-start | bytes 61448 | tf_op jit(solution)/shard_map/ppermute | solution.py:314
  36.5 1.3 %collective-permute-start.3 = (bf16[80,128]{1,0:T(8,128)(2,1)S(1)}, bf16[80,128]{1,0:T(8,128)(2,1)S(1)}, u32[]{:S(2)}, u32[]{:S(2)}) collective-permute-start(bf16[80,128]{1,0:T(8,128)(2,1)S(1)} %pad_maximum_fusion.2), channel_id=1, source_target_pairs={{16,0},{20,4},{24,8},{28,12},{32,16},{36,20},{40,24},{44,28},{48,3... | collective-permute-start | bytes 61448 | tf_op jit(solution)/shard_map/ppermute | solution.py:314
  37.8 6.6 %collective-permute-done.3.from_ap = bf16[80,128]{1,0:T(8,128)(2,1)S(1)} collective-permute-done((bf16[80,128]{1,0:T(8,128)(2,1)S(1)}, bf16[80,128]{1,0:T(8,128)(2,1)S(1)}, u32[]{:S(2)}, u32[]{:S(2)}) %collective-permute-start.3) | collective-permute-done | bytes 20512 | tf_op jit(solution)/shard_map/ppermute | solution.py:314
  44.9 1.3 %copy-done = bf16[140,32,128]{2,1,0:T(8,128)(2,1)S(1)} copy-done((bf16[140,32,128]{2,1,0:T(8,128)(2,1)S(1)}, bf16[140,32,128]{2,1,0:T(8,128)(2,1)}, u32[]{:S(2)}) %copy-start) | copy-done | bytes 1146904
  46.2 5.9 %conv.1 = (bf16[2,32,512]{2,1,0:T(8,128)(2,1)S(1)}, bf16[1152,128]{1,0:T(8,128)(2,1)S(1)}, f32[2,8,8,8,128]{4,3,2,1,0:T(8,128)S(1)}) custom-call(s32[2,26]{1,0:T(2,128)S(1)} %copy-done.3, s32[1]{0:T(128)} %bitcast.chan, s32[2]{0:T(128)S(1)} %pad_add_fusion.place, f32[2,512]{1,0:T(2,128)S(1)} %and_convert_fusion.mask, ...), custom_call_target="tpu_custom_call" | custom-call | tf_op jit(solution)/shard_map/conv/pallas_call | solution.py:298
  52.0 21.2 %all_to_all.39 = bf16[16,72,128]{2,1,0:T(8,128)(2,1)S(1)} all-to-all(bf16[16,72,128]{2,1,0:T(8,128)(2,1)S(1)} %bitcast.31), channel_id=1, replica_groups={{0,4,8,12,16,20,24,28,32,36,40,44,48,52,56,60},{64,68,72,76,80,84,88,92..., dimensions={0} | all-to-all | bytes 589824 | tf_op jit(solution)/shard_map/all_to_all | solution.py:329
  73.2 0.8 middle.1
  73.9 16.6 %all_to_all.40 = bf16[8,80,128]{2,1,0:T(8,128)(2,1)S(1)} all-to-all(bf16[8,80,128]{2,1,0:T(8,128)(2,1)S(1)} %bitcast.30), channel_id=1, replica_groups={{0,64,128,192,256,320,384,448},{4,68,132,196,260,324,388,452},{8,72,136..., dimensions={0} | all-to-all | bytes 327680 | tf_op jit(solution)/shard_map/all_to_all | solution.py:329
  90.5 0.7 sums.1
  91.2 3.7 %all-to-all-start.3 = ((bf16[16,56,128]{2,1,0:T(8,128)(2,1)}), bf16[16,56,128]{2,1,0:T(8,128)(2,1)S(1)}, u32[]{:S(2)}, u32[]{:S(2)}) async-start(bf16[16,56,128]{2,1,0:T(8,128)(2,1)} %bitcast.17), calls=%async_computation.3 | async-start | bytes 458752 | tf_op jit(solution)/shard_map/all_to_all | solution.py:329
  95.0 0.7 copy.18
  95.7 0.9 grad.1
  96.5 0.7 copy.19
  97.2 8.9 %all-to-all-done.3 = bf16[16,56,128]{2,1,0:T(8,128)(2,1)S(1)} async-done(((bf16[16,56,128]{2,1,0:T(8,128)(2,1)}), bf16[16,56,128]{2,1,0:T(8,128)(2,1)S(1)}, u32[]{:S(2)}, u32[]{:S(2)}) %all-to-all-start.3) | async-done | bytes 229408 | tf_op jit(solution)/shard_map/all_to_all | solution.py:329
  106.1 0.8 convert.1
  (31 shorter events, 1.0 us)
Async XLA Ops:
  7.2 2.8 %copy-start.4 = (bf16[32,2,512]{2,1,0:T(2,128)(2,1)S(1)}, bf16[32,2,512]{2,1,0:T(2,128)(2,1)}, u32[]{:S(2)}) copy-start(bf16[32,2,512]{2,1,0:T(2,128)(2,1)} %param.6) | copy-start | bytes 196612
  7.2 8.4 %copy-start.5 = (s32[2,16]{1,0:T(2,128)S(1)}, s32[2,16]{1,0:T(2,128)}, u32[]{:S(2)}) copy-start(s32[2,16]{1,0:T(2,128)} %param.7) | copy-start | bytes 388
  7.2 13.9 %copy-start.2 = (s32[1,8,1]{1,2,0:T(1,128)S(1)}, s32[1,8,1]{1,2,0:T(1,128)}, u32[]{:S(2)}) copy-start(s32[1,8,1]{1,2,0:T(1,128)} %param.9) | copy-start | bytes 100
  7.2 37.7 %all-gather.3.cloned.1.call-start = ((), (), s32[]{:S(2)}) async-start(), calls=%async_computation.4 | async-start | bytes 1433600 | tf_op jit(solution)/shard_map/all_gather | solution.py:348
  8.1 36.7 %copy-start.1 = (bf16[27,32,128]{2,1,0:T(8,128)(2,1)S(1)}, bf16[27,32,128]{2,1,0:T(8,128)(2,1)}, u32[]{:S(2)}) copy-start(bf16[27,32,128]{2,1,0:T(8,128)(2,1)} %own_weights.1) | copy-start | bytes 663556
  8.2 36.7 %copy-start.3 = (s32[2,26]{1,0:T(2,128)S(1)}, s32[2,26]{1,0:T(2,128)}, u32[]{:S(2)}) copy-start(s32[2,26]{1,0:T(2,128)} %near.1) | copy-start | bytes 628
  10.7 10.4 %all-to-all-start = ((bf16[4,2,32,512]{3,2,1,0:T(8,128)(2,1)}), bf16[4,2,32,512]{3,2,1,0:T(8,128)(2,1)S(1)}, u32[]{:S(2)}, u32[]{:S(2)}) async-start(bf16[4,2,32,512]{3,2,1,0:T(8,128)(2,1)} %broadcast_in_dim.2), calls=%async_computation | async-start | bytes 524288 | tf_op jit(solution)/shard_map/all_to_all | solution.py:335
  21.8 10.4 %collective-permute-start.1 = (bf16[80,128]{1,0:T(8,128)(2,1)S(1)}, bf16[80,128]{1,0:T(8,128)(2,1)S(1)}, u32[]{:S(2)}, u32[]{:S(2)}) collective-permute-start(bf16[80,128]{1,0:T(8,128)(2,1)S(1)} %get-tuple-element.24), channel_id=1, source_target_pairs={{4,0},{8,4},{12,8},{20,16},{24,20},{28,24},{36,32},{40,36},{44,40}... | collective-permute-start | bytes 61448 | tf_op jit(solution)/shard_map/ppermute | solution.py:314
  30.3 3.1 %collective-permute-start = (bf16[80,128]{1,0:T(8,128)(2,1)S(1)}, bf16[80,128]{1,0:T(8,128)(2,1)S(1)}, u32[]{:S(2)}, u32[]{:S(2)}) collective-permute-start(bf16[80,128]{1,0:T(8,128)(2,1)S(1)} %get-tuple-element.25), channel_id=1, source_target_pairs={{0,4},{4,8},{8,12},{16,20},{20,24},{24,28},{32,36},{36,40},{40,44}... | collective-permute-start | bytes 61448 | tf_op jit(solution)/shard_map/ppermute | solution.py:314
  33.4 4.4 %collective-permute-start.2 = (bf16[80,128]{1,0:T(8,128)(2,1)S(1)}, bf16[80,128]{1,0:T(8,128)(2,1)S(1)}, u32[]{:S(2)}, u32[]{:S(2)}) collective-permute-start(bf16[80,128]{1,0:T(8,128)(2,1)S(1)} %pad_maximum_fusion.1), channel_id=1, source_target_pairs={{0,16},{4,20},{8,24},{12,28},{16,32},{20,36},{24,40},{28,44},{32,4... | collective-permute-start | bytes 61448 | tf_op jit(solution)/shard_map/ppermute | solution.py:314
  36.5 7.9 %collective-permute-start.3 = (bf16[80,128]{1,0:T(8,128)(2,1)S(1)}, bf16[80,128]{1,0:T(8,128)(2,1)S(1)}, u32[]{:S(2)}, u32[]{:S(2)}) collective-permute-start(bf16[80,128]{1,0:T(8,128)(2,1)S(1)} %pad_maximum_fusion.2), channel_id=1, source_target_pairs={{16,0},{20,4},{24,8},{28,12},{32,16},{36,20},{40,24},{44,28},{48,3... | collective-permute-start | bytes 61448 | tf_op jit(solution)/shard_map/ppermute | solution.py:314
  44.9 1.3 %copy-start = (bf16[140,32,128]{2,1,0:T(8,128)(2,1)S(1)}, bf16[140,32,128]{2,1,0:T(8,128)(2,1)}, u32[]{:S(2)}) copy-start(bf16[140,32,128]{2,1,0:T(8,128)(2,1)} %all-gather.3.cloned.1.call-done) | copy-start | bytes 3440644
  91.2 14.9 %all-to-all-start.3 = ((bf16[16,56,128]{2,1,0:T(8,128)(2,1)}), bf16[16,56,128]{2,1,0:T(8,128)(2,1)S(1)}, u32[]{:S(2)}, u32[]{:S(2)}) async-start(bf16[16,56,128]{2,1,0:T(8,128)(2,1)} %bitcast.17), calls=%async_computation.3 | async-start | bytes 458752 | tf_op jit(solution)/shard_map/all_to_all | solution.py:329
Sparse Core Ops, SparseCore 0:
  10.7 34.1 all-gather.2

commit v8 on v6

--- a/solution.py
+++ b/solution.py
@@ -121,18 +121,30 @@
             nx = 8 if dx == 0 else 1
             blocks[i, RIM[dx], RIM[dy]] = both.reshape(nx, count // nx, 16, 128).astype(BF)
 
-    pre = jnp.zeros((1024, 128), F32)
-    for dx in range(3):
-        left = jnp.concatenate(
+    def lefts(first, count):
+        return jnp.concatenate(
             [
-                blocks[dz, dx : dx + 8, dy : dy + 8].reshape(1024, 128)
-                for dy in range(3)
+                blocks[dz, dx : dx + 8, first : first + count].reshape(128 * count, 128)
+                for dx in range(3)
                 for dz in range(3)
             ],
             axis=1,
         )
-        right = jnp.concatenate([extra[:, 9 * dx + o].reshape(128, 128) for o in range(9)], axis=0)
-        pre = pre + jnp.dot(left, right, preferred_element_type=F32)
+
+    def rights(dy):
+        return jnp.concatenate(
+            [
+                extra[:, 9 * dx + 3 * dy + dz].reshape(128, 128)
+                for dx in range(3)
+                for dz in range(3)
+            ],
+            axis=0,
+        )
+
+    pair = jnp.concatenate([rights(0), rights(1)], axis=1)
+    pair = jnp.dot(lefts(0, 9), pair, preferred_element_type=F32).reshape(8, 9, 16, 256)
+    pre = jnp.dot(lefts(2, 8), rights(2), preferred_element_type=F32).reshape(8, 8, 16, 128)
+    pre = pre + pair[:, 0:8, :, 0:128] + pair[:, 1:9, :, 128:256]
     pre = pre.reshape(64, 2, 8, 128)
 
     back = []
@@ -167,33 +179,44 @@
         first = tile // 7 * SENT + tile % 7 * 8
         stage[first : first + 8] = value
 
-    for i, (dx, dy) in enumerate(PLANAR):
-        window = own_block[dx + 1 : dx + 9, dy + 1 : dy + 9].reshape(1024, 128)
-        product = jnp.dot(back_t, window, preferred_element_type=F32)
-        product = product.T
-        for tile in range(12):
-            put_part(12 * i + tile, product[8 * tile : 8 * tile + 8])
+    for first in range(0, 9, 2):
+        windows = [
+            own_block[dx + 1 : dx + 9, dy + 1 : dy + 9].reshape(1024, 128)
+            for dx, dy in PLANAR[first : first + 2]
+        ]
+        product = jnp.dot(back_t, jnp.concatenate(windows, axis=1), preferred_element_type=F32)
+        for i in range(len(windows)):
+            turned = product[:, 128 * i : 128 * i + 128].T
+            for tile in range(12):
+                put_part(12 * (first + i) + tile, turned[8 * tile : 8 * tile + 8])
     for tile in range(108, 112):
         put_part(tile, jnp.zeros((8, 128), F32))
     for j in range(GROUP):
         stage[j * SENT + PART : (j + 1) * SENT] = jnp.zeros((16, 128), F32)
 
-    spread = jnp.zeros((1600, 128), F32)
-    for dx in (-1, 0, 1):
-        left = jnp.concatenate(
+    def grad_lefts(first, count):
+        return jnp.concatenate(
             [
-                grads[1 - dx : 11 - dx, 1 - dy : 11 - dy].reshape(1600, 128)
-                for dy in (-1, 0, 1)
+                grads[1 - dx : 11 - dx, first : first + count].reshape(160 * count, 128)
+                for dx in (-1, 0, 1)
             ],
             axis=1,
         )
-        rights = []
-        for dy in (-1, 0, 1):
+
+    def grad_rights(dy):
+        pieces = []
+        for dx in (-1, 0, 1):
             first = (dx + 1) * 9 + (dy + 1) * 3
             piece = own_weights[first : first + 3].reshape(96, 128).astype(F32)
             piece = jnp.concatenate([piece, jnp.zeros((32, 128), F32)], axis=0)
-            rights.append(piece.T.astype(BF))
-        spread = spread + jnp.dot(left, jnp.concatenate(rights, axis=0), preferred_element_type=F32)
+            pieces.append(piece.T.astype(BF))
+        return jnp.concatenate(pieces, axis=0)
+
+    pair = jnp.concatenate([grad_rights(1), grad_rights(0)], axis=1)
+    pair = jnp.dot(grad_lefts(0, 11), pair, preferred_element_type=F32).reshape(10, 11, 16, 256)
+    spread = jnp.dot(grad_lefts(2, 10), grad_rights(-1), preferred_element_type=F32)
+    spread = spread.reshape(10, 10, 16, 128)
+    spread = spread + pair[:, 0:10, :, 0:128] + pair[:, 1:11, :, 128:256]
     spread = spread.reshape(100, 2, 8, 128)
     for brick in range(2):
         part = spread[:, brick]

time: 102 us -> 100 us (0.980)
  Pallas kernels: 8.94 us -> 7.73 us
    pallas_call x5, Pallas kernels: 8.94 us -> 7.73 us  [call(): pl.pallas_call(kernel, out_shape=shapes, in_specs=[SMEM] * len(smem) + [V...]
where the time goes in v8:
time: 100 us; the launch traced here: 99.8 us
  blocking collectives  37.5 us (38%)
  starting transfers between devices  27 us (27%)
  waiting for transfers between devices  19.8 us (20%)
  Pallas kernels  7.73 us (8%)
  local copies, waits for them, and re-layouts  6.04 us (6%)
    all_to_all x2, blocking collectives, exchanged(): lax.all_to_all(values, 'space', 0, 0, tiled=True, axis_index_groups=groups)  37.5 us
    ppermute x4, starting transfers between devices, passed_along(): return lax.ppermute(shard, 'space', pairs)  14.7 us
    all_to_all x1, waiting for transfers between devices, exchanged(): lax.all_to_all(values, 'space', 0, 0, tiled=True, axis_index_groups=groups)  8.9 us
    all_to_all x2, starting transfers between devices, from_all_chan(): return lax.all_to_all(copies, 'chan', 0, 0, tiled=True)  8.5 us
    pallas_call x5, Pallas kernels, call(): pl.pallas_call(kernel, out_shape=shapes, in_specs=[SMEM] * len(smem) + [V...  7.73 us
    ppermute x4, waiting for transfers between devices, passed_along(): return lax.ppermute(shard, 'space', pairs)  7.3 us
    all_to_all x1, starting transfers between devices, exchanged(): lax.all_to_all(values, 'space', 0, 0, tiled=True, axis_index_groups=groups)  3.73 us
    all_to_all x2, waiting for transfers between devices, from_all_chan(): return lax.all_to_all(copies, 'chan', 0, 0, tiled=True)  3.63 us
  transfers between devices with their start and end apart: 7, of which 4 were waited for; matrix products, arithmetic and copies ran while one was open for 3% of the time, Pallas kernels for 2%

profile of v8, /device:TPU:1, one launch (start us, length us, event | category | flops | bytes accessed | tf_op | source)
XLA Modules:
  0.0 99.8 jit_solution(15577952293839944708)
XLA Ops:
  0.6 0.9 copy.9
  1.5 0.7 broadcast_in_dim.4
  2.3 4.8 %all-to-all-start = ((bf16[4,2,32,512]{3,2,1,0:T(8,128)(2,1)}), bf16[4,2,32,512]{3,2,1,0:T(8,128)(2,1)S(1)}, u32[]{:S(2)}, u32[]{:S(2)}) async-start(bf16[4,2,32,512]{3,2,1,0:T(8,128)(2,1)} %broadcast_in_dim.4), calls=%async_computation | async-start | bytes 524288 | tf_op jit(solution)/shard_map/all_to_all | solution.py:358
  7.2 0.7 shift_right_logical.20
  8.0 0.9 reshape.35
  9.0 3.6 %all-to-all-done.gathered = bf16[4,2,32,512]{3,2,1,0:T(8,128)(2,1)S(1)} async-done(((bf16[4,2,32,512]{3,2,1,0:T(8,128)(2,1)}), bf16[4,2,32,512]{3,2,1,0:T(8,128)(2,1)S(1)}, u32[]{:S(2)}, u32[]{:S(2)}) %all-to-all-start) | async-done | bytes 262176 | tf_op jit(solution)/shard_map/all_to_all | solution.py:358
  12.6 1.2 %broadcast_in_dim.5 = bf16[4,35,32,128]{3,2,1,0:T(8,128)(2,1)} broadcast(bf16[35,32,128]{2,1,0:T(8,128)(2,1)S(1)} %pad_maximum_fusion), dimensions={1,2,3} | broadcast | bytes 1433600 | tf_op jit(solution)/shard_map/broadcast_in_dim | solution.py:357
  13.8 3.7 %all-to-all-start.1 = ((bf16[4,35,32,128]{3,2,1,0:T(8,128)(2,1)}), bf16[4,35,32,128]{3,2,1,0:T(8,128)(2,1)S(1)}, u32[]{:S(2)}, u32[]{:S(2)}) async-start(bf16[4,35,32,128]{3,2,1,0:T(8,128)(2,1)} %broadcast_in_dim.5), calls=%async_computation.1 | async-start | bytes 2293760 | tf_op jit(solution)/shard_map/all_to_all | solution.py:358
  17.5 0.7 rims.1
  18.2 8.5 %collective-permute-start.1 = (bf16[80,128]{1,0:T(8,128)(2,1)S(1)}, bf16[80,128]{1,0:T(8,128)(2,1)S(1)}, u32[]{:S(2)}, u32[]{:S(2)}) collective-permute-start(bf16[80,128]{1,0:T(8,128)(2,1)S(1)} %get-tuple-element.18), channel_id=1, source_target_pairs={{4,0},{8,4},{12,8},{20,16},{24,20},{28,24},{36,32},{40,36},{44,40}... | collective-permute-start | bytes 61448 | tf_op jit(solution)/shard_map/ppermute | solution.py:337
  26.7 1.9 %collective-permute-start = (bf16[80,128]{1,0:T(8,128)(2,1)S(1)}, bf16[80,128]{1,0:T(8,128)(2,1)S(1)}, u32[]{:S(2)}, u32[]{:S(2)}) collective-permute-start(bf16[80,128]{1,0:T(8,128)(2,1)S(1)} %get-tuple-element.19), channel_id=1, source_target_pairs={{0,4},{4,8},{8,12},{16,20},{20,24},{24,28},{32,36},{36,40},{40,44}... | collective-permute-start | bytes 61448 | tf_op jit(solution)/shard_map/ppermute | solution.py:337
  28.7 1.1 %collective-permute-done.from_bm = bf16[80,128]{1,0:T(8,128)(2,1)S(1)} collective-permute-done((bf16[80,128]{1,0:T(8,128)(2,1)S(1)}, bf16[80,128]{1,0:T(8,128)(2,1)S(1)}, u32[]{:S(2)}, u32[]{:S(2)}) %collective-permute-start) | collective-permute-done | bytes 20512 | tf_op jit(solution)/shard_map/ppermute | solution.py:337
  29.8 3.0 %collective-permute-start.2 = (bf16[80,128]{1,0:T(8,128)(2,1)S(1)}, bf16[80,128]{1,0:T(8,128)(2,1)S(1)}, u32[]{:S(2)}, u32[]{:S(2)}) collective-permute-start(bf16[80,128]{1,0:T(8,128)(2,1)S(1)} %pad_maximum_fusion.1), channel_id=1, source_target_pairs={{0,16},{4,20},{8,24},{12,28},{16,32},{20,36},{24,40},{28,44},{32,4... | collective-permute-start | bytes 61448 | tf_op jit(solution)/shard_map/ppermute | solution.py:337
  32.9 1.3 %collective-permute-start.3 = (bf16[80,128]{1,0:T(8,128)(2,1)S(1)}, bf16[80,128]{1,0:T(8,128)(2,1)S(1)}, u32[]{:S(2)}, u32[]{:S(2)}) collective-permute-start(bf16[80,128]{1,0:T(8,128)(2,1)S(1)} %pad_maximum_fusion.2), channel_id=1, source_target_pairs={{16,0},{20,4},{24,8},{28,12},{32,16},{36,20},{40,24},{44,28},{48,3... | collective-permute-start | bytes 61448 | tf_op jit(solution)/shard_map/ppermute | solution.py:337
  34.3 6.2 %collective-permute-done.3.from_ap = bf16[80,128]{1,0:T(8,128)(2,1)S(1)} collective-permute-done((bf16[80,128]{1,0:T(8,128)(2,1)S(1)}, bf16[80,128]{1,0:T(8,128)(2,1)S(1)}, u32[]{:S(2)}, u32[]{:S(2)}) %collective-permute-start.3) | collective-permute-done | bytes 20512 | tf_op jit(solution)/shard_map/ppermute | solution.py:337
  40.4 4.7 %conv.1 = (bf16[2,32,512]{2,1,0:T(8,128)(2,1)S(1)}, bf16[1152,128]{1,0:T(8,128)(2,1)S(1)}, f32[2,8,8,8,128]{4,3,2,1,0:T(8,128)S(1)}) custom-call(s32[2,26]{1,0:T(2,128)S(1)} %copy-done.2, s32[1]{0:T(128)} %bitcast.chan, s32[2]{0:T(128)S(1)} %pad_add_fusion.place, f32[2,512]{1,0:T(2,128)S(1)} %and_convert_fusion.mask, ...), custom_call_target="tpu_custom_call" | custom-call | tf_op jit(solution)/shard_map/conv/pallas_call | solution.py:321
  45.1 20.6 %all_to_all.44 = bf16[16,72,128]{2,1,0:T(8,128)(2,1)S(1)} all-to-all(bf16[16,72,128]{2,1,0:T(8,128)(2,1)S(1)} %bitcast.31), channel_id=1, replica_groups={{0,4,8,12,16,20,24,28,32,36,40,44,48,52,56,60},{64,68,72,76,80,84,88,92..., dimensions={0} | all-to-all | bytes 589824 | tf_op jit(solution)/shard_map/all_to_all | solution.py:352
  65.7 0.8 middle.1
  66.5 16.9 %all_to_all.45 = bf16[8,80,128]{2,1,0:T(8,128)(2,1)S(1)} all-to-all(bf16[8,80,128]{2,1,0:T(8,128)(2,1)S(1)} %bitcast.30), channel_id=1, replica_groups={{0,64,128,192,256,320,384,448},{4,68,132,196,260,324,388,452},{8,72,136..., dimensions={0} | all-to-all | bytes 327680 | tf_op jit(solution)/shard_map/all_to_all | solution.py:352
  83.4 0.7 sums.1
  84.1 3.7 %all-to-all-start.4 = ((bf16[16,56,128]{2,1,0:T(8,128)(2,1)}), bf16[16,56,128]{2,1,0:T(8,128)(2,1)S(1)}, u32[]{:S(2)}, u32[]{:S(2)}) async-start(bf16[16,56,128]{2,1,0:T(8,128)(2,1)} %bitcast.16), calls=%async_computation.4 | async-start | bytes 458752 | tf_op jit(solution)/shard_map/all_to_all | solution.py:352
  88.5 0.9 grad.1
  90.1 8.9 %all-to-all-done.4 = bf16[16,56,128]{2,1,0:T(8,128)(2,1)S(1)} async-done(((bf16[16,56,128]{2,1,0:T(8,128)(2,1)}), bf16[16,56,128]{2,1,0:T(8,128)(2,1)S(1)}, u32[]{:S(2)}, u32[]{:S(2)}) %all-to-all-start.4) | async-done | bytes 229408 | tf_op jit(solution)/shard_map/all_to_all | solution.py:352
  99.0 0.8 convert.1
  (25 shorter events, 1.8 us)
Async XLA Ops:
  0.6 8.3 %copy-start = (bf16[27,32,128]{2,1,0:T(8,128)(2,1)S(1)}, bf16[27,32,128]{2,1,0:T(8,128)(2,1)}, u32[]{:S(2)}) copy-start(bf16[27,32,128]{2,1,0:T(8,128)(2,1)} %own_weights.1) | copy-start | bytes 663556
  2.3 10.4 %all-to-all-start = ((bf16[4,2,32,512]{3,2,1,0:T(8,128)(2,1)}), bf16[4,2,32,512]{3,2,1,0:T(8,128)(2,1)S(1)}, u32[]{:S(2)}, u32[]{:S(2)}) async-start(bf16[4,2,32,512]{3,2,1,0:T(8,128)(2,1)} %broadcast_in_dim.4), calls=%async_computation | async-start | bytes 524288 | tf_op jit(solution)/shard_map/all_to_all | solution.py:358
  13.8 3.7 %copy-start.1 = (s32[1,8,1]{1,2,0:T(1,128)S(1)}, s32[1,8,1]{1,2,0:T(1,128)}, u32[]{:S(2)}) copy-start(s32[1,8,1]{1,2,0:T(1,128)} %param.9) | copy-start | bytes 100
  13.8 26.6 %copy-start.2 = (s32[2,26]{1,0:T(2,128)S(1)}, s32[2,26]{1,0:T(2,128)}, u32[]{:S(2)}) copy-start(s32[2,26]{1,0:T(2,128)} %near.1) | copy-start | bytes 628
  13.8 26.6 %all-to-all-start.1 = ((bf16[4,35,32,128]{3,2,1,0:T(8,128)(2,1)}), bf16[4,35,32,128]{3,2,1,0:T(8,128)(2,1)S(1)}, u32[]{:S(2)}, u32[]{:S(2)}) async-start(bf16[4,35,32,128]{3,2,1,0:T(8,128)(2,1)} %broadcast_in_dim.5), calls=%async_computation.1 | async-start | bytes 2293760 | tf_op jit(solution)/shard_map/all_to_all | solution.py:358
  18.2 10.4 %collective-permute-start.1 = (bf16[80,128]{1,0:T(8,128)(2,1)S(1)}, bf16[80,128]{1,0:T(8,128)(2,1)S(1)}, u32[]{:S(2)}, u32[]{:S(2)}) collective-permute-start(bf16[80,128]{1,0:T(8,128)(2,1)S(1)} %get-tuple-element.18), channel_id=1, source_target_pairs={{4,0},{8,4},{12,8},{20,16},{24,20},{28,24},{36,32},{40,36},{44,40}... | collective-permute-start | bytes 61448 | tf_op jit(solution)/shard_map/ppermute | solution.py:337
  26.7 3.1 %collective-permute-start = (bf16[80,128]{1,0:T(8,128)(2,1)S(1)}, bf16[80,128]{1,0:T(8,128)(2,1)S(1)}, u32[]{:S(2)}, u32[]{:S(2)}) collective-permute-start(bf16[80,128]{1,0:T(8,128)(2,1)S(1)} %get-tuple-element.19), channel_id=1, source_target_pairs={{0,4},{4,8},{8,12},{16,20},{20,24},{24,28},{32,36},{36,40},{40,44}... | collective-permute-start | bytes 61448 | tf_op jit(solution)/shard_map/ppermute | solution.py:337
  29.8 4.4 %collective-permute-start.2 = (bf16[80,128]{1,0:T(8,128)(2,1)S(1)}, bf16[80,128]{1,0:T(8,128)(2,1)S(1)}, u32[]{:S(2)}, u32[]{:S(2)}) collective-permute-start(bf16[80,128]{1,0:T(8,128)(2,1)S(1)} %pad_maximum_fusion.1), channel_id=1, source_target_pairs={{0,16},{4,20},{8,24},{12,28},{16,32},{20,36},{24,40},{28,44},{32,4... | collective-permute-start | bytes 61448 | tf_op jit(solution)/shard_map/ppermute | solution.py:337
  32.9 7.5 %collective-permute-start.3 = (bf16[80,128]{1,0:T(8,128)(2,1)S(1)}, bf16[80,128]{1,0:T(8,128)(2,1)S(1)}, u32[]{:S(2)}, u32[]{:S(2)}) collective-permute-start(bf16[80,128]{1,0:T(8,128)(2,1)S(1)} %pad_maximum_fusion.2), channel_id=1, source_target_pairs={{16,0},{20,4},{24,8},{28,12},{32,16},{36,20},{40,24},{44,28},{48,3... | collective-permute-start | bytes 61448 | tf_op jit(solution)/shard_map/ppermute | solution.py:337
  84.1 14.9 %all-to-all-start.4 = ((bf16[16,56,128]{2,1,0:T(8,128)(2,1)}), bf16[16,56,128]{2,1,0:T(8,128)(2,1)S(1)}, u32[]{:S(2)}, u32[]{:S(2)}) async-start(bf16[16,56,128]{2,1,0:T(8,128)(2,1)} %bitcast.16), calls=%async_computation.4 | async-start | bytes 458752 | tf_op jit(solution)/shard_map/all_to_all | solution.py:352

commit v9 on v8

--- a/solution.py
+++ b/solution.py
@@ -77,49 +77,46 @@
         face_a[i] = chosen((a, 0)).reshape(64, 128).astype(BF)
 
 
-def main_kernel(
-    near, chan, place, mask, local, from_bm, from_bp, from_am, from_ap, extra, own_weights,
-    act_out, sent, own_out,
-    blocks, grads, own_block, act_all, terms, stage,
-):
+def block_tiles(near, local, arrived, dx, dy):
     z = lax.broadcasted_iota(jnp.int32, (1, 8, 128), 1)
-    from_b = {-1: from_bm, 1: from_bp}
-    from_a = {-1: from_am, 1: from_ap}
-
-    def arrived(dx, dy):
-        if dx == 0:
-            return from_b[dy][0:64].astype(F32).reshape(8, 8, 128)
-        if dy == 0:
-            return from_a[dx][0:64].astype(F32).reshape(8, 8, 128)
-        edges = from_a[dx][64:80].astype(F32).reshape(2, 8, 128)
-        return edges[0:1] if dy == -1 else edges[1:2]
-
-    for dx, dy in PLANAR:
-        options = [tiles(local[0], dx, dy), tiles(local[1], dx, dy)]
-        rows = [0, 1]
-        if (dx, dy) != (0, 0):
-            options.append(arrived(dx, dy))
-            rows.append(2 + MOVES.index((dx, dy)))
-
-        def pick(r):
-            value = 0.0
-            for row, option in zip(rows, options):
-                value = jnp.where(r == row, option, value)
-            return value
-
-        shifted = [[], [], []]
-        for brick in range(2):
-            below, level, above = planar_slots(dx, dy)
-            center = options[brick] if level is None else pick(near[brick, level])
-            under, over = pick(near[brick, below]), pick(near[brick, above])
-            shifted[0].append(pltpu.roll(jnp.where(z == 7, under, center), 1, 1))
-            shifted[1].append(center)
-            shifted[2].append(pltpu.roll(jnp.where(z == 0, over, center), 7, 1))
-        for i in range(3):
-            both = jnp.stack(shifted[i], axis=1)
-            count = both.shape[0]
-            nx = 8 if dx == 0 else 1
-            blocks[i, RIM[dx], RIM[dy]] = both.reshape(nx, count // nx, 16, 128).astype(BF)
+    options = [tiles(local[0], dx, dy), tiles(local[1], dx, dy)]
+    rows = [0, 1]
+    if (dx, dy) != (0, 0):
+        options.append(arrived)
+        rows.append(2 + MOVES.index((dx, dy)))
+
+    def pick(r):
+        value = 0.0
+        for row, option in zip(rows, options):
+            value = jnp.where(r == row, option, value)
+        return value
+
+    shifted = [[], [], []]
+    for brick in range(2):
+        below, level, above = planar_slots(dx, dy)
+        center = options[brick] if level is None else pick(near[brick, level])
+        under, over = pick(near[brick, below]), pick(near[brick, above])
+        shifted[0].append(pltpu.roll(jnp.where(z == 7, under, center), 1, 1))
+        shifted[1].append(center)
+        shifted[2].append(pltpu.roll(jnp.where(z == 0, over, center), 7, 1))
+    return [jnp.stack(pair, axis=1).reshape(-1, 16, 128).astype(BF) for pair in shifted]
+
+
+def selection(chan):
+    row = lax.broadcasted_iota(jnp.int32, (384, 128), 0)
+    column = lax.broadcasted_iota(jnp.int32, (384, 128), 1)
+    wanted = (row >> 7 == column >> 5) & ((row & 127) == chan * 32 + (column & 31))
+    return jnp.where(wanted, 1.0, 0.0).astype(BF)
+
+
+def center_kernel(near, chan, local, from_bm, from_bp, extra, pre_out, own_out, blocks):
+    for i in range(3):
+        for plane in (0, 9):
+            blocks[i, plane] = jnp.zeros((10, 16, 128), BF)
+    for dy, part in ((-1, from_bm), (0, None), (1, from_bp)):
+        arrived = None if part is None else part[0:64].astype(F32).reshape(8, 8, 128)
+        for i, value in enumerate(block_tiles(near, local, arrived, 0, dy)):
+            blocks[i, 1:9, RIM[dy]] = value.reshape(8, -1, 16, 128)
 
     def lefts(first, count):
         return jnp.concatenate(
@@ -144,7 +141,39 @@
     pair = jnp.concatenate([rights(0), rights(1)], axis=1)
     pair = jnp.dot(lefts(0, 9), pair, preferred_element_type=F32).reshape(8, 9, 16, 256)
     pre = jnp.dot(lefts(2, 8), rights(2), preferred_element_type=F32).reshape(8, 8, 16, 128)
-    pre = pre + pair[:, 0:8, :, 0:128] + pair[:, 1:9, :, 128:256]
+    pre_out[...] = pre + pair[:, 0:8, :, 0:128] + pair[:, 1:9, :, 128:256]
+    stacked = jnp.concatenate([blocks[dz, 1:9].reshape(1280, 128) for dz in range(3)], axis=1)
+    own = jnp.dot(stacked, selection(chan[0]), preferred_element_type=F32).astype(BF)
+    own_out[...] = own.reshape(8, 10, 16, 128)
+
+
+def main_kernel(
+    near, chan, place, mask, local, from_am, from_ap, center_pre, center_own, extra, own_weights,
+    act_out, sent, own_out,
+    rim, grads, own_block, act_all, terms, stage,
+):
+    z = lax.broadcasted_iota(jnp.int32, (1, 8, 128), 1)
+    own_block[1:9] = center_own[...]
+    edges = []
+    for side, (dx, part) in enumerate(((-1, from_am), (1, from_ap))):
+        corner = part[64:80].astype(F32).reshape(2, 8, 128)
+        face = part[0:64].astype(F32).reshape(8, 8, 128)
+        for dy, arrived in ((-1, corner[0:1]), (0, face), (1, corner[1:2])):
+            for i, value in enumerate(block_tiles(near, local, arrived, dx, dy)):
+                rim[side, i, RIM[dy]] = value
+        left = jnp.concatenate(
+            [rim[side, dz, dy : dy + 8].reshape(128, 128) for dy in range(3) for dz in range(3)],
+            axis=1,
+        )
+        right = jnp.concatenate(
+            [extra[:, 9 * (dx + 1) + o].reshape(128, 128) for o in range(9)], axis=0
+        )
+        edges.append(jnp.dot(left, right, preferred_element_type=F32).reshape(1, 8, 16, 128))
+        stacked = jnp.concatenate([rim[side, dz].reshape(160, 128) for dz in range(3)], axis=1)
+        own = jnp.dot(stacked, selection(chan[0]), preferred_element_type=F32).astype(BF)
+        own_block[9 * side] = own.reshape(10, 16, 128)
+    pre = center_pre[...]
+    pre = jnp.concatenate([pre[0:1] + edges[0], pre[1:7], pre[7:8] + edges[1]], axis=0)
     pre = pre.reshape(64, 2, 8, 128)
 
     back = []
@@ -165,15 +194,6 @@
     grads[...] = jnp.zeros(grads.shape, BF)
     grads[2:10, 2:10] = back.astype(BF).reshape(8, 8, 16, 128)
     back_t = back.T.astype(BF)
-
-    row = lax.broadcasted_iota(jnp.int32, (384, 128), 0)
-    column = lax.broadcasted_iota(jnp.int32, (384, 128), 1)
-    wanted = (row >> 7 == column >> 5) & ((row & 127) == chan[0] * 32 + (column & 31))
-    select = jnp.where(wanted, 1.0, 0.0).astype(BF)
-    stacked = jnp.concatenate([blocks[dz].reshape(1600, 128) for dz in range(3)], axis=1)
-    own_block[...] = (
-        jnp.dot(stacked, select, preferred_element_type=F32).astype(BF).reshape(10, 10, 16, 128)
-    )
 
     def put_part(tile, value):
         first = tile // 7 * SENT + tile % 7 * 8
@@ -316,7 +336,7 @@
 VMEM = pl.BlockSpec(memory_space=pltpu.VMEM)
 
 
-def call(kernel, name, smem, vmem, outs, scratch, limit):
+def call(kernel, name, smem, vmem, outs, scratch, limit, cost=None):
     shapes = [jax.ShapeDtypeStruct(s, d) for s, d in outs]
     return pl.pallas_call(
         kernel,
@@ -325,6 +345,7 @@
         out_specs=[VMEM] * len(outs),
         scratch_shapes=[pltpu.VMEM(s, d) for s, d in scratch],
         compiler_params=pltpu.CompilerParams(vmem_limit_bytes=limit << 20),
+        cost_estimate=cost,
         name=name,
     )(*smem, *vmem)
 
@@ -377,17 +398,22 @@
     to_am = jnp.concatenate([face_a[0], from_bm[64:72], from_bp[64:72]], axis=0)
     to_ap = jnp.concatenate([face_a[1], from_bm[72:80], from_bp[72:80]], axis=0)
     from_am, from_ap = passed_along(to_am, 4), passed_along(to_ap, -4)
+    center_pre, center_own = call(
+        center_kernel, "center", [neighbours, chan], [local, from_bm, from_bp, extra],
+        [((8, 8, 16, 128), F32), ((8, 10, 16, 128), BF)], [((3, 10, 10, 16, 128), BF)], 24,
+        pl.CostEstimate(flops=1 << 30, bytes_accessed=3 << 20, transcendentals=0),
+    )
     act, sent, own = call(
         main_kernel, "conv", [neighbours, chan, place],
-        [mask, local, from_bm, from_bp, from_am, from_ap, extra, weights],
+        [mask, local, from_am, from_ap, center_pre, center_own, extra, weights],
         [
             ((2, 32, 512), BF), ((GROUP * SENT, 128), BF), ((2, 8, 8, 8, 128), F32),
         ],
         [
-            ((3, 10, 10, 16, 128), BF), ((12, 12, 16, 128), BF), ((10, 10, 16, 128), BF),
+            ((2, 3, 10, 16, 128), BF), ((12, 12, 16, 128), BF), ((10, 10, 16, 128), BF),
             ((2, 128, 512), BF), ((3, 2, 10, 10, 8, 128), F32), ((GROUP * SENT, 128), F32),
         ],
-        40,
+        32,
     )
     scale = 1.0 / math.sqrt(2 * lax.axis_size("space") * 512)
     direct = exchanged(sent, False)

time: 100 us -> 99.2 us (level)
  blocking collectives: 37.5 us -> 35.1 us
  starting transfers between devices: 27 us -> 29.1 us
  waiting for transfers between devices: 19.8 us -> 17.8 us
    all_to_all x2, blocking collectives: 37.5 us -> 35.1 us  [exchanged(): lax.all_to_all(values, 'space', 0, 0, tiled=True, axis_index_groups=groups)]
    ppermute x4, starting transfers between devices: 14.7 us -> 16.9 us  [passed_along(): return lax.ppermute(shard, 'space', pairs)]
    ppermute x4, waiting for transfers between devices: 7.3 us -> 5.38 us  [passed_along(): return lax.ppermute(shard, 'space', pairs)]
    pallas_call x5 -> x6, Pallas kernels: 7.73 us -> 8.71 us  [call(): pl.pallas_call(kernel, out_shape=shapes, in_specs=[SMEM] * len(smem) + [V...]
  transfers between devices with their start and end apart: 7 -> 7, of which waited for: 4 -> 4; matrix products, arithmetic and copies ran while one was open for 3% -> 3% of each run, Pallas kernels for 2% -> 4%
where the time goes in v9:
time: 99.2 us; the launch traced here: 98.6 us
  blocking collectives  35.1 us (35%)
  starting transfers between devices  29.1 us (29%)
  waiting for transfers between devices  17.8 us (18%)
  Pallas kernels  8.71 us (9%)
  local copies, waits for them, and re-layouts  6.06 us (6%)
    all_to_all x2, blocking collectives, exchanged(): lax.all_to_all(values, 'space', 0, 0, tiled=True, axis_index_groups=groups)  35.1 us
    ppermute x4, starting transfers between devices, passed_along(): return lax.ppermute(shard, 'space', pairs)  16.9 us
    all_to_all x1, waiting for transfers between devices, exchanged(): lax.all_to_all(values, 'space', 0, 0, tiled=True, axis_index_groups=groups)  8.89 us
    pallas_call x6, Pallas kernels, call(): pl.pallas_call(kernel, out_shape=shapes, in_specs=[SMEM] * len(smem) + [V...  8.71 us
    all_to_all x2, starting transfers between devices, from_all_chan(): return lax.all_to_all(copies, 'chan', 0, 0, tiled=True)  8.5 us
    ppermute x4, waiting for transfers between devices, passed_along(): return lax.ppermute(shard, 'space', pairs)  5.38 us
    all_to_all x1, starting transfers between devices, exchanged(): lax.all_to_all(values, 'space', 0, 0, tiled=True, axis_index_groups=groups)  3.73 us
    all_to_all x2, waiting for transfers between devices, from_all_chan(): return lax.all_to_all(copies, 'chan', 0, 0, tiled=True)  3.57 us
  transfers between devices with their start and end apart: 7, of which 4 were waited for; matrix products, arithmetic and copies ran while one was open for 3% of the time, Pallas kernels for 4%

profile of v9, /device:TPU:1, one launch (start us, length us, event | category | flops | bytes accessed | tf_op | source)
XLA Modules:
  0.0 98.6 jit_solution(5222908059426816628)
XLA Ops:
  0.6 0.9 copy.9
  1.5 0.7 broadcast_in_dim.4
  2.3 4.8 %all-to-all-start = ((bf16[4,2,32,512]{3,2,1,0:T(8,128)(2,1)}), bf16[4,2,32,512]{3,2,1,0:T(8,128)(2,1)S(1)}, u32[]{:S(2)}, u32[]{:S(2)}) async-start(bf16[4,2,32,512]{3,2,1,0:T(8,128)(2,1)} %broadcast_in_dim.4), calls=%async_computation | async-start | bytes 524288 | tf_op jit(solution)/shard_map/all_to_all | solution.py:379
  7.2 0.7 shift_right_logical.20
  8.0 0.9 reshape.35
  9.1 3.6 %all-to-all-done.gathered = bf16[4,2,32,512]{3,2,1,0:T(8,128)(2,1)S(1)} async-done(((bf16[4,2,32,512]{3,2,1,0:T(8,128)(2,1)}), bf16[4,2,32,512]{3,2,1,0:T(8,128)(2,1)S(1)}, u32[]{:S(2)}, u32[]{:S(2)}) %all-to-all-start) | async-done | bytes 262176 | tf_op jit(solution)/shard_map/all_to_all | solution.py:379
  12.6 1.2 %broadcast_in_dim.5 = bf16[4,35,32,128]{3,2,1,0:T(8,128)(2,1)} broadcast(bf16[35,32,128]{2,1,0:T(8,128)(2,1)S(1)} %pad_maximum_fusion), dimensions={1,2,3} | broadcast | bytes 1433600 | tf_op jit(solution)/shard_map/broadcast_in_dim | solution.py:378
  13.8 3.7 %all-to-all-start.1 = ((bf16[4,35,32,128]{3,2,1,0:T(8,128)(2,1)}), bf16[4,35,32,128]{3,2,1,0:T(8,128)(2,1)S(1)}, u32[]{:S(2)}, u32[]{:S(2)}) async-start(bf16[4,35,32,128]{3,2,1,0:T(8,128)(2,1)} %broadcast_in_dim.5), calls=%async_computation.1 | async-start | bytes 2293760 | tf_op jit(solution)/shard_map/all_to_all | solution.py:379
  17.5 0.7 rims.1
  18.3 6.0 %collective-permute-start = (bf16[80,128]{1,0:T(8,128)(2,1)S(1)}, bf16[80,128]{1,0:T(8,128)(2,1)S(1)}, u32[]{:S(2)}, u32[]{:S(2)}) collective-permute-start(bf16[80,128]{1,0:T(8,128)(2,1)S(1)} %get-tuple-element.22), channel_id=1, source_target_pairs={{0,4},{4,8},{8,12},{16,20},{20,24},{24,28},{32,36},{36,40},{40,44}... | collective-permute-start | bytes 61448 | tf_op jit(solution)/shard_map/ppermute | solution.py:358
  24.3 3.8 %collective-permute-start.1 = (bf16[80,128]{1,0:T(8,128)(2,1)S(1)}, bf16[80,128]{1,0:T(8,128)(2,1)S(1)}, u32[]{:S(2)}, u32[]{:S(2)}) collective-permute-start(bf16[80,128]{1,0:T(8,128)(2,1)S(1)} %get-tuple-element.23), channel_id=1, source_target_pairs={{4,0},{8,4},{12,8},{20,16},{24,20},{28,24},{36,32},{40,36},{44,40}... | collective-permute-start | bytes 61448 | tf_op jit(solution)/shard_map/ppermute | solution.py:358
  28.1 1.6 %collective-permute-done.1.from_bp = bf16[80,128]{1,0:T(8,128)(2,1)S(1)} collective-permute-done((bf16[80,128]{1,0:T(8,128)(2,1)S(1)}, bf16[80,128]{1,0:T(8,128)(2,1)S(1)}, u32[]{:S(2)}, u32[]{:S(2)}) %collective-permute-start.1) | collective-permute-done | bytes 20512 | tf_op jit(solution)/shard_map/ppermute | solution.py:358
  29.7 5.8 %collective-permute-start.2 = (bf16[80,128]{1,0:T(8,128)(2,1)S(1)}, bf16[80,128]{1,0:T(8,128)(2,1)S(1)}, u32[]{:S(2)}, u32[]{:S(2)}) collective-permute-start(bf16[80,128]{1,0:T(8,128)(2,1)S(1)} %pad_maximum_fusion.1), channel_id=1, source_target_pairs={{0,16},{4,20},{8,24},{12,28},{16,32},{20,36},{24,40},{28,44},{32,4... | collective-permute-start | bytes 61448 | tf_op jit(solution)/shard_map/ppermute | solution.py:358
  35.5 1.3 %collective-permute-start.3 = (bf16[80,128]{1,0:T(8,128)(2,1)S(1)}, bf16[80,128]{1,0:T(8,128)(2,1)S(1)}, u32[]{:S(2)}, u32[]{:S(2)}) collective-permute-start(bf16[80,128]{1,0:T(8,128)(2,1)S(1)} %pad_maximum_fusion.2), channel_id=1, source_target_pairs={{16,0},{20,4},{24,8},{28,12},{32,16},{36,20},{40,24},{44,28},{48,3... | collective-permute-start | bytes 61448 | tf_op jit(solution)/shard_map/ppermute | solution.py:358
  36.8 2.4 %center.1 = (f32[8,8,16,128]{3,2,1,0:T(8,128)S(1)}, bf16[8,10,16,128]{3,2,1,0:T(8,128)(2,1)S(1)}) custom-call(s32[2,26]{1,0:T(2,128)S(1)} %copy-done.2, s32[1]{0:T(128)} %bitcast.chan, f32[2,8,8,8,128]{4,3,2,1,0:T(8,128)S(1)} %get-tuple-element.11.local, bf16[80,128]{1,0:T(8,128)(2,1)S(1)} %collective-permute-done.from_bm, ...), custom_call_target="tpu_custom_call" | custom-call | flops 1073741824 | bytes 3145728 | tf_op jit(solution)/shard_map/center/pallas_call | solution.py:341
  39.2 3.8 %collective-permute-done.3.from_ap = bf16[80,128]{1,0:T(8,128)(2,1)S(1)} collective-permute-done((bf16[80,128]{1,0:T(8,128)(2,1)S(1)}, bf16[80,128]{1,0:T(8,128)(2,1)S(1)}, u32[]{:S(2)}, u32[]{:S(2)}) %collective-permute-start.3) | collective-permute-done | bytes 20512 | tf_op jit(solution)/shard_map/ppermute | solution.py:358
  43.0 3.3 %conv.1 = (bf16[2,32,512]{2,1,0:T(8,128)(2,1)S(1)}, bf16[1152,128]{1,0:T(8,128)(2,1)S(1)}, f32[2,8,8,8,128]{4,3,2,1,0:T(8,128)S(1)}) custom-call(s32[2,26]{1,0:T(2,128)S(1)} %copy-done.2, s32[1]{0:T(128)} %bitcast.chan, s32[2]{0:T(128)S(1)} %pad_add_fusion.place, f32[2,512]{1,0:T(2,128)S(1)} %and_convert_fusion.mask, ...), custom_call_target="tpu_custom_call" | custom-call | tf_op jit(solution)/shard_map/conv/pallas_call | solution.py:341
  46.3 18.2 %all_to_all.44 = bf16[16,72,128]{2,1,0:T(8,128)(2,1)S(1)} all-to-all(bf16[16,72,128]{2,1,0:T(8,128)(2,1)S(1)} %bitcast.31), channel_id=1, replica_groups={{0,4,8,12,16,20,24,28,32,36,40,44,48,52,56,60},{64,68,72,76,80,84,88,92..., dimensions={0} | all-to-all | bytes 589824 | tf_op jit(solution)/shard_map/all_to_all | solution.py:373
  64.5 0.8 middle.1
  65.2 16.9 %all_to_all.45 = bf16[8,80,128]{2,1,0:T(8,128)(2,1)S(1)} all-to-all(bf16[8,80,128]{2,1,0:T(8,128)(2,1)S(1)} %bitcast.30), channel_id=1, replica_groups={{0,64,128,192,256,320,384,448},{4,68,132,196,260,324,388,452},{8,72,136..., dimensions={0} | all-to-all | bytes 327680 | tf_op jit(solution)/shard_map/all_to_all | solution.py:373
  82.9 3.7 %all-to-all-start.4 = ((bf16[16,56,128]{2,1,0:T(8,128)(2,1)}), bf16[16,56,128]{2,1,0:T(8,128)(2,1)S(1)}, u32[]{:S(2)}, u32[]{:S(2)}) async-start(bf16[16,56,128]{2,1,0:T(8,128)(2,1)} %bitcast.16), calls=%async_computation.4 | async-start | bytes 458752 | tf_op jit(solution)/shard_map/all_to_all | solution.py:373
  87.3 0.9 grad.1
  88.9 8.9 %all-to-all-done.4 = bf16[16,56,128]{2,1,0:T(8,128)(2,1)S(1)} async-done(((bf16[16,56,128]{2,1,0:T(8,128)(2,1)}), bf16[16,56,128]{2,1,0:T(8,128)(2,1)S(1)}, u32[]{:S(2)}, u32[]{:S(2)}) %all-to-all-start.4) | async-done | bytes 229408 | tf_op jit(solution)/shard_map/all_to_all | solution.py:373
  97.8 0.8 convert.1
  (26 shorter events, 2.5 us)
Async XLA Ops:
  0.6 8.4 %copy-start = (bf16[27,32,128]{2,1,0:T(8,128)(2,1)S(1)}, bf16[27,32,128]{2,1,0:T(8,128)(2,1)}, u32[]{:S(2)}) copy-start(bf16[27,32,128]{2,1,0:T(8,128)(2,1)} %own_weights.1) | copy-start | bytes 663556
  2.3 10.4 %all-to-all-start = ((bf16[4,2,32,512]{3,2,1,0:T(8,128)(2,1)}), bf16[4,2,32,512]{3,2,1,0:T(8,128)(2,1)S(1)}, u32[]{:S(2)}, u32[]{:S(2)}) async-start(bf16[4,2,32,512]{3,2,1,0:T(8,128)(2,1)} %broadcast_in_dim.4), calls=%async_computation | async-start | bytes 524288 | tf_op jit(solution)/shard_map/all_to_all | solution.py:379
  13.8 3.7 %copy-start.1 = (s32[1,8,1]{1,2,0:T(1,128)S(1)}, s32[1,8,1]{1,2,0:T(1,128)}, u32[]{:S(2)}) copy-start(s32[1,8,1]{1,2,0:T(1,128)} %param.9) | copy-start | bytes 100
  13.8 23.0 %copy-start.2 = (s32[2,26]{1,0:T(2,128)S(1)}, s32[2,26]{1,0:T(2,128)}, u32[]{:S(2)}) copy-start(s32[2,26]{1,0:T(2,128)} %near.3) | copy-start | bytes 628
  13.8 23.0 %all-to-all-start.1 = ((bf16[4,35,32,128]{3,2,1,0:T(8,128)(2,1)}), bf16[4,35,32,128]{3,2,1,0:T(8,128)(2,1)S(1)}, u32[]{:S(2)}, u32[]{:S(2)}) async-start(bf16[4,35,32,128]{3,2,1,0:T(8,128)(2,1)} %broadcast_in_dim.5), calls=%async_computation.1 | async-start | bytes 2293760 | tf_op jit(solution)/shard_map/all_to_all | solution.py:379
  18.3 9.8 %collective-permute-start = (bf16[80,128]{1,0:T(8,128)(2,1)S(1)}, bf16[80,128]{1,0:T(8,128)(2,1)S(1)}, u32[]{:S(2)}, u32[]{:S(2)}) collective-permute-start(bf16[80,128]{1,0:T(8,128)(2,1)S(1)} %get-tuple-element.22), channel_id=1, source_target_pairs={{0,4},{4,8},{8,12},{16,20},{20,24},{24,28},{32,36},{36,40},{40,44}... | collective-permute-start | bytes 61448 | tf_op jit(solution)/shard_map/ppermute | solution.py:358
  24.3 5.4 %collective-permute-start.1 = (bf16[80,128]{1,0:T(8,128)(2,1)S(1)}, bf16[80,128]{1,0:T(8,128)(2,1)S(1)}, u32[]{:S(2)}, u32[]{:S(2)}) collective-permute-start(bf16[80,128]{1,0:T(8,128)(2,1)S(1)} %get-tuple-element.23), channel_id=1, source_target_pairs={{4,0},{8,4},{12,8},{20,16},{24,20},{28,24},{36,32},{40,36},{44,40}... | collective-permute-start | bytes 61448 | tf_op jit(solution)/shard_map/ppermute | solution.py:358
  29.7 9.5 %collective-permute-start.2 = (bf16[80,128]{1,0:T(8,128)(2,1)S(1)}, bf16[80,128]{1,0:T(8,128)(2,1)S(1)}, u32[]{:S(2)}, u32[]{:S(2)}) collective-permute-start(bf16[80,128]{1,0:T(8,128)(2,1)S(1)} %pad_maximum_fusion.1), channel_id=1, source_target_pairs={{0,16},{4,20},{8,24},{12,28},{16,32},{20,36},{24,40},{28,44},{32,4... | collective-permute-start | bytes 61448 | tf_op jit(solution)/shard_map/ppermute | solution.py:358
  35.5 7.5 %collective-permute-start.3 = (bf16[80,128]{1,0:T(8,128)(2,1)S(1)}, bf16[80,128]{1,0:T(8,128)(2,1)S(1)}, u32[]{:S(2)}, u32[]{:S(2)}) collective-permute-start(bf16[80,128]{1,0:T(8,128)(2,1)S(1)} %pad_maximum_fusion.2), channel_id=1, source_target_pairs={{16,0},{20,4},{24,8},{28,12},{32,16},{36,20},{40,24},{44,28},{48,3... | collective-permute-start | bytes 61448 | tf_op jit(solution)/shard_map/ppermute | solution.py:358
  82.9 14.9 %all-to-all-start.4 = ((bf16[16,56,128]{2,1,0:T(8,128)(2,1)}), bf16[16,56,128]{2,1,0:T(8,128)(2,1)S(1)}, u32[]{:S(2)}, u32[]{:S(2)}) async-start(bf16[16,56,128]{2,1,0:T(8,128)(2,1)} %bitcast.16), calls=%async_computation.4 | async-start | bytes 458752 | tf_op jit(solution)/shard_map/all_to_all | solution.py:373

commit v10 on v9

--- a/solution.py
+++ b/solution.py
@@ -58,6 +58,12 @@
 
 def rows_of(index, stride, first, count):
     return pl.ds(pl.multiple_of(index * stride + first, 8), count)
+
+
+def copies_kernel(weights, by_lanes, out):
+    for i in range(out.shape[0]):
+        out[i, 0:27] = weights[...]
+        out[i, 27:35] = by_lanes[...]
 
 
 def rims_kernel(send, mask, gathered, local, to_b, face_a):
@@ -388,8 +394,11 @@
     mask = unpack_mask(mask_packed)
     gathered = from_all_chan(features.transpose(1, 0, 2))
     by_lanes = cotangent.reshape(32, 8, 128).transpose(1, 0, 2)
-    extra = jnp.concatenate([weights, by_lanes], axis=0)
-    extra = from_all_chan(extra)
+    (extra,) = call(
+        copies_kernel, "copies", [], [weights, by_lanes], [((4, 35, 32, 128), BF)], [], 16,
+        pl.CostEstimate(flops=0, bytes_accessed=8 << 20, transcendentals=0),
+    )
+    extra = lax.all_to_all(extra, "chan", 0, 0, tiled=True)
     local, to_b, face_a = call(
         rims_kernel, "rims", [send], [mask, gathered],
         [((2, 8, 8, 8, 128), F32), ((2, 80, 128), BF), ((2, 64, 128), BF)], [], 16,

time: 99.2 us -> 97.8 us (0.986)
  local copies, waits for them, and re-layouts: 6.06 us -> 4.87 us
  Pallas kernels: 8.71 us -> 9.89 us
  waiting for transfers between devices: 17.8 us -> 16.7 us
    all_to_all x2 -> x1, starting transfers between devices: 8.5 us -> 4.84 us  [from_all_chan(): return lax.all_to_all(copies, 'chan', 0, 0, tiled=True)]
    all_to_all x0 -> x1, starting transfers between devices: none -> 3.52 us  [on_device(): extra = lax.all_to_all(extra, 'chan', 0, 0, tiled=True)]
    broadcast_in_dim x2 -> x1, local copies, waits for them, and re-layouts: 1.91 us -> 0.72 us  [from_all_chan(): copies = jnp.broadcast_to(part[None], (count,) + part.shape)]
    pallas_call x6 -> x7, Pallas kernels: 8.71 us -> 9.89 us  [call(): pl.pallas_call(kernel, out_shape=shapes, in_specs=[SMEM] * len(smem) + [V...]
    all_to_all x2 -> x1, waiting for transfers between devices: 3.57 us -> 2.4 us  [from_all_chan(): return lax.all_to_all(copies, 'chan', 0, 0, tiled=True)]
  transfers between devices with their start and end apart: 7 -> 7, of which waited for: 4 -> 4; matrix products, arithmetic and copies ran while one was open for 3% -> 3% of each run, Pallas kernels for 4% -> 5%
where the time goes in v10:
time: 97.8 us; the launch traced here: 97.3 us
  blocking collectives  35.1 us (36%)
  starting transfers between devices  28.9 us (30%)
  waiting for transfers between devices  16.7 us (17%)
  Pallas kernels  9.89 us (10%)
  local copies, waits for them, and re-layouts  4.87 us (5%)
    all_to_all x2, blocking collectives, exchanged(): lax.all_to_all(values, 'space', 0, 0, tiled=True, axis_index_groups=groups)  35.1 us
    ppermute x4, starting transfers between devices, passed_along(): return lax.ppermute(shard, 'space', pairs)  16.9 us
    pallas_call x7, Pallas kernels, call(): pl.pallas_call(kernel, out_shape=shapes, in_specs=[SMEM] * len(smem) + [V...  9.89 us
    all_to_all x1, waiting for transfers between devices, exchanged(): lax.all_to_all(values, 'space', 0, 0, tiled=True, axis_index_groups=groups)  8.9 us
    ppermute x4, waiting for transfers between devices, passed_along(): return lax.ppermute(shard, 'space', pairs)  5.39 us
    all_to_all x1, starting transfers between devices, from_all_chan(): return lax.all_to_all(copies, 'chan', 0, 0, tiled=True)  4.84 us
    all_to_all x1, starting transfers between devices, exchanged(): lax.all_to_all(values, 'space', 0, 0, tiled=True, axis_index_groups=groups)  3.73 us
    all_to_all x1, starting transfers between devices, on_device(): extra = lax.all_to_all(extra, 'chan', 0, 0, tiled=True)  3.52 us
  transfers between devices with their start and end apart: 7, of which 4 were waited for; matrix products, arithmetic and copies ran while one was open for 3% of the time, Pallas kernels for 5%

profile of v10, /device:TPU:1, one launch (start us, length us, event | category | flops | bytes accessed | tf_op | source)
XLA Modules:
  0.0 97.3 jit_solution(15522732919770114062)
XLA Ops:
  0.6 0.9 copy.12
  1.5 0.7 broadcast_in_dim.2
  2.3 4.8 %all-to-all-start = ((bf16[4,2,32,512]{3,2,1,0:T(8,128)(2,1)}), bf16[4,2,32,512]{3,2,1,0:T(8,128)(2,1)S(1)}, u32[]{:S(2)}, u32[]{:S(2)}) async-start(bf16[4,2,32,512]{3,2,1,0:T(8,128)(2,1)} %broadcast_in_dim.2), calls=%async_computation | async-start | bytes 524288 | tf_op jit(solution)/shard_map/all_to_all | solution.py:385
  7.2 0.7 shift_right_logical.20
  8.0 0.9 reshape.34
  9.0 1.2 %copies.1 = bf16[4,35,32,128]{3,2,1,0:T(8,128)(2,1)} custom-call(bf16[27,32,128]{2,1,0:T(8,128)(2,1)S(1)} %copy-done, bf16[8,32,128]{2,1,0:T(8,128)(2,1)S(1)} %bitcast.32), custom_call_target="tpu_custom_call" | custom-call | bytes 8388608 | tf_op jit(solution)/shard_map/copies/pallas_call | solution.py:347
  10.2 2.4 %all-to-all-done.gathered = bf16[4,2,32,512]{3,2,1,0:T(8,128)(2,1)S(1)} async-done(((bf16[4,2,32,512]{3,2,1,0:T(8,128)(2,1)}), bf16[4,2,32,512]{3,2,1,0:T(8,128)(2,1)S(1)}, u32[]{:S(2)}, u32[]{:S(2)}) %all-to-all-start) | async-done | bytes 262176 | tf_op jit(solution)/shard_map/all_to_all | solution.py:385
  12.6 3.5 %all-to-all-start.1 = ((bf16[4,35,32,128]{3,2,1,0:T(8,128)(2,1)}), bf16[4,35,32,128]{3,2,1,0:T(8,128)(2,1)S(1)}, u32[]{:S(2)}, u32[]{:S(2)}) async-start(bf16[4,35,32,128]{3,2,1,0:T(8,128)(2,1)} %copies.1), calls=%async_computation.1 | async-start | bytes 2293760 | tf_op jit(solution)/shard_map/all_to_all | solution.py:401
  16.2 0.7 rims.1
  16.9 6.0 %collective-permute-start = (bf16[80,128]{1,0:T(8,128)(2,1)S(1)}, bf16[80,128]{1,0:T(8,128)(2,1)S(1)}, u32[]{:S(2)}, u32[]{:S(2)}) collective-permute-start(bf16[80,128]{1,0:T(8,128)(2,1)S(1)} %get-tuple-element.25), channel_id=1, source_target_pairs={{0,4},{4,8},{8,12},{16,20},{20,24},{24,28},{32,36},{36,40},{40,44}... | collective-permute-start | bytes 61448 | tf_op jit(solution)/shard_map/ppermute | solution.py:364
  22.9 3.8 %collective-permute-start.1 = (bf16[80,128]{1,0:T(8,128)(2,1)S(1)}, bf16[80,128]{1,0:T(8,128)(2,1)S(1)}, u32[]{:S(2)}, u32[]{:S(2)}) collective-permute-start(bf16[80,128]{1,0:T(8,128)(2,1)S(1)} %get-tuple-element.26), channel_id=1, source_target_pairs={{4,0},{8,4},{12,8},{20,16},{24,20},{28,24},{36,32},{40,36},{44,40}... | collective-permute-start | bytes 61448 | tf_op jit(solution)/shard_map/ppermute | solution.py:364
  26.8 1.6 %collective-permute-done.1.from_bp = bf16[80,128]{1,0:T(8,128)(2,1)S(1)} collective-permute-done((bf16[80,128]{1,0:T(8,128)(2,1)S(1)}, bf16[80,128]{1,0:T(8,128)(2,1)S(1)}, u32[]{:S(2)}, u32[]{:S(2)}) %collective-permute-start.1) | collective-permute-done | bytes 20512 | tf_op jit(solution)/shard_map/ppermute | solution.py:364
  28.4 5.8 %collective-permute-start.2 = (bf16[80,128]{1,0:T(8,128)(2,1)S(1)}, bf16[80,128]{1,0:T(8,128)(2,1)S(1)}, u32[]{:S(2)}, u32[]{:S(2)}) collective-permute-start(bf16[80,128]{1,0:T(8,128)(2,1)S(1)} %pad_maximum_fusion), channel_id=1, source_target_pairs={{0,16},{4,20},{8,24},{12,28},{16,32},{20,36},{24,40},{28,44},{32,4... | collective-permute-start | bytes 61448 | tf_op jit(solution)/shard_map/ppermute | solution.py:364
  34.2 1.3 %collective-permute-start.3 = (bf16[80,128]{1,0:T(8,128)(2,1)S(1)}, bf16[80,128]{1,0:T(8,128)(2,1)S(1)}, u32[]{:S(2)}, u32[]{:S(2)}) collective-permute-start(bf16[80,128]{1,0:T(8,128)(2,1)S(1)} %pad_maximum_fusion.1), channel_id=1, source_target_pairs={{16,0},{20,4},{24,8},{28,12},{32,16},{36,20},{40,24},{44,28},{48,3... | collective-permute-start | bytes 61448 | tf_op jit(solution)/shard_map/ppermute | solution.py:364
  35.5 2.4 %center.1 = (f32[8,8,16,128]{3,2,1,0:T(8,128)S(1)}, bf16[8,10,16,128]{3,2,1,0:T(8,128)(2,1)S(1)}) custom-call(s32[2,26]{1,0:T(2,128)S(1)} %copy-done.2, s32[1]{0:T(128)} %bitcast.chan, f32[2,8,8,8,128]{4,3,2,1,0:T(8,128)S(1)} %get-tuple-element.11.local, bf16[80,128]{1,0:T(8,128)(2,1)S(1)} %collective-permute-done.from_bm, ...), custom_call_target="tpu_custom_call" | custom-call | flops 1073741824 | bytes 3145728 | tf_op jit(solution)/shard_map/center/pallas_call | solution.py:347
  37.9 3.8 %collective-permute-done.3.from_ap = bf16[80,128]{1,0:T(8,128)(2,1)S(1)} collective-permute-done((bf16[80,128]{1,0:T(8,128)(2,1)S(1)}, bf16[80,128]{1,0:T(8,128)(2,1)S(1)}, u32[]{:S(2)}, u32[]{:S(2)}) %collective-permute-start.3) | collective-permute-done | bytes 20512 | tf_op jit(solution)/shard_map/ppermute | solution.py:364
  41.7 3.3 %conv.1 = (bf16[2,32,512]{2,1,0:T(8,128)(2,1)S(1)}, bf16[1152,128]{1,0:T(8,128)(2,1)S(1)}, f32[2,8,8,8,128]{4,3,2,1,0:T(8,128)S(1)}) custom-call(s32[2,26]{1,0:T(2,128)S(1)} %copy-done.2, s32[1]{0:T(128)} %bitcast.chan, s32[2]{0:T(128)S(1)} %pad_add_fusion.place, f32[2,512]{1,0:T(2,128)S(1)} %and_convert_fusion.mask, ...), custom_call_target="tpu_custom_call" | custom-call | tf_op jit(solution)/shard_map/conv/pallas_call | solution.py:347
  44.9 18.2 %all_to_all.44 = bf16[16,72,128]{2,1,0:T(8,128)(2,1)S(1)} all-to-all(bf16[16,72,128]{2,1,0:T(8,128)(2,1)S(1)} %bitcast.31), channel_id=1, replica_groups={{0,4,8,12,16,20,24,28,32,36,40,44,48,52,56,60},{64,68,72,76,80,84,88,92..., dimensions={0} | all-to-all | bytes 589824 | tf_op jit(solution)/shard_map/all_to_all | solution.py:379
  63.1 0.8 middle.1
  63.9 16.9 %all_to_all.45 = bf16[8,80,128]{2,1,0:T(8,128)(2,1)S(1)} all-to-all(bf16[8,80,128]{2,1,0:T(8,128)(2,1)S(1)} %bitcast.30), channel_id=1, replica_groups={{0,64,128,192,256,320,384,448},{4,68,132,196,260,324,388,452},{8,72,136..., dimensions={0} | all-to-all | bytes 327680 | tf_op jit(solution)/shard_map/all_to_all | solution.py:379
  81.5 3.7 %all-to-all-start.4 = ((bf16[16,56,128]{2,1,0:T(8,128)(2,1)}), bf16[16,56,128]{2,1,0:T(8,128)(2,1)S(1)}, u32[]{:S(2)}, u32[]{:S(2)}) async-start(bf16[16,56,128]{2,1,0:T(8,128)(2,1)} %bitcast.16), calls=%async_computation.4 | async-start | bytes 458752 | tf_op jit(solution)/shard_map/all_to_all | solution.py:379
  86.0 0.9 grad.1
  87.5 8.9 %all-to-all-done.4 = bf16[16,56,128]{2,1,0:T(8,128)(2,1)S(1)} async-done(((bf16[16,56,128]{2,1,0:T(8,128)(2,1)}), bf16[16,56,128]{2,1,0:T(8,128)(2,1)S(1)}, u32[]{:S(2)}, u32[]{:S(2)}) %all-to-all-start.4) | async-done | bytes 229408 | tf_op jit(solution)/shard_map/all_to_all | solution.py:379
  96.4 0.8 convert.1
  (25 shorter events, 2.4 us)
Async XLA Ops:
  0.6 8.4 %copy-start = (bf16[27,32,128]{2,1,0:T(8,128)(2,1)S(1)}, bf16[27,32,128]{2,1,0:T(8,128)(2,1)}, u32[]{:S(2)}) copy-start(bf16[27,32,128]{2,1,0:T(8,128)(2,1)} %own_weights.1) | copy-start | bytes 663556
  2.3 10.4 %all-to-all-start = ((bf16[4,2,32,512]{3,2,1,0:T(8,128)(2,1)}), bf16[4,2,32,512]{3,2,1,0:T(8,128)(2,1)S(1)}, u32[]{:S(2)}, u32[]{:S(2)}) async-start(bf16[4,2,32,512]{3,2,1,0:T(8,128)(2,1)} %broadcast_in_dim.2), calls=%async_computation | async-start | bytes 524288 | tf_op jit(solution)/shard_map/all_to_all | solution.py:385
  10.2 6.0 %copy-start.1 = (s32[1,8,1]{1,2,0:T(1,128)S(1)}, s32[1,8,1]{1,2,0:T(1,128)}, u32[]{:S(2)}) copy-start(s32[1,8,1]{1,2,0:T(1,128)} %param.9) | copy-start | bytes 100
  10.2 25.3 %copy-start.2 = (s32[2,26]{1,0:T(2,128)S(1)}, s32[2,26]{1,0:T(2,128)}, u32[]{:S(2)}) copy-start(s32[2,26]{1,0:T(2,128)} %near.3) | copy-start | bytes 628
  12.6 22.8 %all-to-all-start.1 = ((bf16[4,35,32,128]{3,2,1,0:T(8,128)(2,1)}), bf16[4,35,32,128]{3,2,1,0:T(8,128)(2,1)S(1)}, u32[]{:S(2)}, u32[]{:S(2)}) async-start(bf16[4,35,32,128]{3,2,1,0:T(8,128)(2,1)} %copies.1), calls=%async_computation.1 | async-start | bytes 2293760 | tf_op jit(solution)/shard_map/all_to_all | solution.py:401
  16.9 9.8 %collective-permute-start = (bf16[80,128]{1,0:T(8,128)(2,1)S(1)}, bf16[80,128]{1,0:T(8,128)(2,1)S(1)}, u32[]{:S(2)}, u32[]{:S(2)}) collective-permute-start(bf16[80,128]{1,0:T(8,128)(2,1)S(1)} %get-tuple-element.25), channel_id=1, source_target_pairs={{0,4},{4,8},{8,12},{16,20},{20,24},{24,28},{32,36},{36,40},{40,44}... | collective-permute-start | bytes 61448 | tf_op jit(solution)/shard_map/ppermute | solution.py:364
  22.9 5.4 %collective-permute-start.1 = (bf16[80,128]{1,0:T(8,128)(2,1)S(1)}, bf16[80,128]{1,0:T(8,128)(2,1)S(1)}, u32[]{:S(2)}, u32[]{:S(2)}) collective-permute-start(bf16[80,128]{1,0:T(8,128)(2,1)S(1)} %get-tuple-element.26), channel_id=1, source_target_pairs={{4,0},{8,4},{12,8},{20,16},{24,20},{28,24},{36,32},{40,36},{44,40}... | collective-permute-start | bytes 61448 | tf_op jit(solution)/shard_map/ppermute | solution.py:364
  28.4 9.5 %collective-permute-start.2 = (bf16[80,128]{1,0:T(8,128)(2,1)S(1)}, bf16[80,128]{1,0:T(8,128)(2,1)S(1)}, u32[]{:S(2)}, u32[]{:S(2)}) collective-permute-start(bf16[80,128]{1,0:T(8,128)(2,1)S(1)} %pad_maximum_fusion), channel_id=1, source_target_pairs={{0,16},{4,20},{8,24},{12,28},{16,32},{20,36},{24,40},{28,44},{32,4... | collective-permute-start | bytes 61448 | tf_op jit(solution)/shard_map/ppermute | solution.py:364
  34.2 7.5 %collective-permute-start.3 = (bf16[80,128]{1,0:T(8,128)(2,1)S(1)}, bf16[80,128]{1,0:T(8,128)(2,1)S(1)}, u32[]{:S(2)}, u32[]{:S(2)}) collective-permute-start(bf16[80,128]{1,0:T(8,128)(2,1)S(1)} %pad_maximum_fusion.1), channel_id=1, source_target_pairs={{16,0},{20,4},{24,8},{28,12},{32,16},{36,20},{40,24},{44,28},{48,3... | collective-permute-start | bytes 61448 | tf_op jit(solution)/shard_map/ppermute | solution.py:364
  81.5 14.9 %all-to-all-start.4 = ((bf16[16,56,128]{2,1,0:T(8,128)(2,1)}), bf16[16,56,128]{2,1,0:T(8,128)(2,1)S(1)}, u32[]{:S(2)}, u32[]{:S(2)}) async-start(bf16[16,56,128]{2,1,0:T(8,128)(2,1)} %bitcast.16), calls=%async_computation.4 | async-start | bytes 458752 | tf_op jit(solution)/shard_map/all_to_all | solution.py:379

commit v11 on v10

--- a/solution.py
+++ b/solution.py
@@ -67,8 +67,9 @@
 
 
 def rims_kernel(send, mask, gathered, local, to_b, face_a):
-    for brick in range(2):
-        rows = gathered[:, brick].reshape(128, 512).astype(F32) * mask[brick : brick + 1, :]
+    both = gathered[...].reshape(128, 2, 512).astype(F32)
+    for brick in range(2):
+        rows = both[:, brick] * mask[brick : brick + 1, :]
         local[brick] = rows.T.reshape(8, 8, 8, 128)
 
     def chosen(move):
@@ -392,7 +393,7 @@
     place = jnp.stack([where % GROUP, where // GROUP])
     planes = lax.axis_size("space") // GROUP
     mask = unpack_mask(mask_packed)
-    gathered = from_all_chan(features.transpose(1, 0, 2))
+    gathered = from_all_chan(features)
     by_lanes = cotangent.reshape(32, 8, 128).transpose(1, 0, 2)
     (extra,) = call(
         copies_kernel, "copies", [], [weights, by_lanes], [((4, 35, 32, 128), BF)], [], 16,

time: 97.8 us -> 98 us (level)
    broadcast_in_dim x1, local copies, waits for them, and re-layouts: 0.72 us -> 1.72 us  [from_all_chan(): copies = jnp.broadcast_to(part[None], (count,) + part.shape)]
where the time goes in v11:
time: 98 us; the launch traced here: 97.4 us
  blocking collectives  35.1 us (36%)
  starting transfers between devices  28.9 us (29%)
  waiting for transfers between devices  16.7 us (17%)
  Pallas kernels  9.96 us (10%)
  local copies, waits for them, and re-layouts  4.98 us (5%)
    all_to_all x2, blocking collectives, exchanged(): lax.all_to_all(values, 'space', 0, 0, tiled=True, axis_index_groups=groups)  35.1 us
    ppermute x4, starting transfers between devices, passed_along(): return lax.ppermute(shard, 'space', pairs)  16.8 us
    pallas_call x7, Pallas kernels, call(): pl.pallas_call(kernel, out_shape=shapes, in_specs=[SMEM] * len(smem) + [V...  9.96 us
    all_to_all x1, waiting for transfers between devices, exchanged(): lax.all_to_all(values, 'space', 0, 0, tiled=True, axis_index_groups=groups)  8.9 us
    ppermute x4, waiting for transfers between devices, passed_along(): return lax.ppermute(shard, 'space', pairs)  5.38 us
    all_to_all x1, starting transfers between devices, from_all_chan(): return lax.all_to_all(copies, 'chan', 0, 0, tiled=True)  4.84 us
    all_to_all x1, starting transfers between devices, exchanged(): lax.all_to_all(values, 'space', 0, 0, tiled=True, axis_index_groups=groups)  3.73 us
    all_to_all x1, starting transfers between devices, on_device(): extra = lax.all_to_all(extra, 'chan', 0, 0, tiled=True)  3.52 us
  transfers between devices with their start and end apart: 7, of which 4 were waited for; matrix products, arithmetic and copies ran while one was open for 3% of the time, Pallas kernels for 5%

profile of v11, /device:TPU:1, one launch (start us, length us, event | category | flops | bytes accessed | tf_op | source)
XLA Modules:
  0.0 97.4 jit_solution(5070953450806707982)
XLA Ops:
  0.6 1.7 %broadcast_in_dim.2 = bf16[4,32,2,512]{3,2,1,0:T(2,128)(2,1)} broadcast(bf16[32,2,512]{2,1,0:T(2,128)(2,1)} %param.6), dimensions={1,2,3} | broadcast | bytes 327680 | tf_op jit(solution)/shard_map/broadcast_in_dim | solution.py:385
  2.4 4.8 %all-to-all-start = ((bf16[4,32,2,512]{3,2,1,0:T(2,128)(2,1)}), bf16[4,32,2,512]{3,2,1,0:T(2,128)(2,1)S(1)}, u32[]{:S(2)}, u32[]{:S(2)}) async-start(bf16[4,32,2,512]{3,2,1,0:T(2,128)(2,1)} %broadcast_in_dim.2), calls=%async_computation | async-start | bytes 524288 | tf_op jit(solution)/shard_map/all_to_all | solution.py:386
  7.3 0.7 shift_right_logical.20
  8.1 0.9 reshape.34
  9.1 1.2 %copies.1 = bf16[4,35,32,128]{3,2,1,0:T(8,128)(2,1)} custom-call(bf16[27,32,128]{2,1,0:T(8,128)(2,1)S(1)} %copy-done, bf16[8,32,128]{2,1,0:T(8,128)(2,1)S(1)} %bitcast.31), custom_call_target="tpu_custom_call" | custom-call | bytes 8388608 | tf_op jit(solution)/shard_map/copies/pallas_call | solution.py:348
  10.3 2.4 %all-to-all-done.gathered = bf16[4,32,2,512]{3,2,1,0:T(2,128)(2,1)S(1)} async-done(((bf16[4,32,2,512]{3,2,1,0:T(2,128)(2,1)}), bf16[4,32,2,512]{3,2,1,0:T(2,128)(2,1)S(1)}, u32[]{:S(2)}, u32[]{:S(2)}) %all-to-all-start) | async-done | bytes 262176 | tf_op jit(solution)/shard_map/all_to_all | solution.py:386
  12.7 3.5 %all-to-all-start.1 = ((bf16[4,35,32,128]{3,2,1,0:T(8,128)(2,1)}), bf16[4,35,32,128]{3,2,1,0:T(8,128)(2,1)S(1)}, u32[]{:S(2)}, u32[]{:S(2)}) async-start(bf16[4,35,32,128]{3,2,1,0:T(8,128)(2,1)} %copies.1), calls=%async_computation.1 | async-start | bytes 2293760 | tf_op jit(solution)/shard_map/all_to_all | solution.py:402
  16.3 0.8 rims.1
  17.1 6.0 %collective-permute-start = (bf16[80,128]{1,0:T(8,128)(2,1)S(1)}, bf16[80,128]{1,0:T(8,128)(2,1)S(1)}, u32[]{:S(2)}, u32[]{:S(2)}) collective-permute-start(bf16[80,128]{1,0:T(8,128)(2,1)S(1)} %get-tuple-element.25), channel_id=1, source_target_pairs={{0,4},{4,8},{8,12},{16,20},{20,24},{24,28},{32,36},{36,40},{40,44}... | collective-permute-start | bytes 61448 | tf_op jit(solution)/shard_map/ppermute | solution.py:365
  23.1 3.8 %collective-permute-start.1 = (bf16[80,128]{1,0:T(8,128)(2,1)S(1)}, bf16[80,128]{1,0:T(8,128)(2,1)S(1)}, u32[]{:S(2)}, u32[]{:S(2)}) collective-permute-start(bf16[80,128]{1,0:T(8,128)(2,1)S(1)} %get-tuple-element.26), channel_id=1, source_target_pairs={{4,0},{8,4},{12,8},{20,16},{24,20},{28,24},{36,32},{40,36},{44,40}... | collective-permute-start | bytes 61448 | tf_op jit(solution)/shard_map/ppermute | solution.py:365
  26.9 1.6 %collective-permute-done.1.from_bp = bf16[80,128]{1,0:T(8,128)(2,1)S(1)} collective-permute-done((bf16[80,128]{1,0:T(8,128)(2,1)S(1)}, bf16[80,128]{1,0:T(8,128)(2,1)S(1)}, u32[]{:S(2)}, u32[]{:S(2)}) %collective-permute-start.1) | collective-permute-done | bytes 20512 | tf_op jit(solution)/shard_map/ppermute | solution.py:365
  28.5 5.8 %collective-permute-start.2 = (bf16[80,128]{1,0:T(8,128)(2,1)S(1)}, bf16[80,128]{1,0:T(8,128)(2,1)S(1)}, u32[]{:S(2)}, u32[]{:S(2)}) collective-permute-start(bf16[80,128]{1,0:T(8,128)(2,1)S(1)} %pad_maximum_fusion), channel_id=1, source_target_pairs={{0,16},{4,20},{8,24},{12,28},{16,32},{20,36},{24,40},{28,44},{32,4... | collective-permute-start | bytes 61448 | tf_op jit(solution)/shard_map/ppermute | solution.py:365
  34.3 1.3 %collective-permute-start.3 = (bf16[80,128]{1,0:T(8,128)(2,1)S(1)}, bf16[80,128]{1,0:T(8,128)(2,1)S(1)}, u32[]{:S(2)}, u32[]{:S(2)}) collective-permute-start(bf16[80,128]{1,0:T(8,128)(2,1)S(1)} %pad_maximum_fusion.1), channel_id=1, source_target_pairs={{16,0},{20,4},{24,8},{28,12},{32,16},{36,20},{40,24},{44,28},{48,3... | collective-permute-start | bytes 61448 | tf_op jit(solution)/shard_map/ppermute | solution.py:365
  35.7 2.4 %center.1 = (f32[8,8,16,128]{3,2,1,0:T(8,128)S(1)}, bf16[8,10,16,128]{3,2,1,0:T(8,128)(2,1)S(1)}) custom-call(s32[2,26]{1,0:T(2,128)S(1)} %copy-done.2, s32[1]{0:T(128)} %bitcast.chan, f32[2,8,8,8,128]{4,3,2,1,0:T(8,128)S(1)} %get-tuple-element.11.local, bf16[80,128]{1,0:T(8,128)(2,1)S(1)} %collective-permute-done.from_bm, ...), custom_call_target="tpu_custom_call" | custom-call | flops 1073741824 | bytes 3145728 | tf_op jit(solution)/shard_map/center/pallas_call | solution.py:348
  38.1 3.8 %collective-permute-done.3.from_ap = bf16[80,128]{1,0:T(8,128)(2,1)S(1)} collective-permute-done((bf16[80,128]{1,0:T(8,128)(2,1)S(1)}, bf16[80,128]{1,0:T(8,128)(2,1)S(1)}, u32[]{:S(2)}, u32[]{:S(2)}) %collective-permute-start.3) | collective-permute-done | bytes 20512 | tf_op jit(solution)/shard_map/ppermute | solution.py:365
  41.8 3.3 %conv.1 = (bf16[2,32,512]{2,1,0:T(8,128)(2,1)S(1)}, bf16[1152,128]{1,0:T(8,128)(2,1)S(1)}, f32[2,8,8,8,128]{4,3,2,1,0:T(8,128)S(1)}) custom-call(s32[2,26]{1,0:T(2,128)S(1)} %copy-done.2, s32[1]{0:T(128)} %bitcast.chan, s32[2]{0:T(128)S(1)} %pad_add_fusion.place, f32[2,512]{1,0:T(2,128)S(1)} %and_convert_fusion.mask, ...), custom_call_target="tpu_custom_call" | custom-call | tf_op jit(solution)/shard_map/conv/pallas_call | solution.py:348
  45.1 18.2 %all_to_all.44 = bf16[16,72,128]{2,1,0:T(8,128)(2,1)S(1)} all-to-all(bf16[16,72,128]{2,1,0:T(8,128)(2,1)S(1)} %bitcast.30), channel_id=1, replica_groups={{0,4,8,12,16,20,24,28,32,36,40,44,48,52,56,60},{64,68,72,76,80,84,88,92..., dimensions={0} | all-to-all | bytes 589824 | tf_op jit(solution)/shard_map/all_to_all | solution.py:380
  63.3 0.8 middle.1
  64.1 16.9 %all_to_all.45 = bf16[8,80,128]{2,1,0:T(8,128)(2,1)S(1)} all-to-all(bf16[8,80,128]{2,1,0:T(8,128)(2,1)S(1)} %bitcast.29), channel_id=1, replica_groups={{0,64,128,192,256,320,384,448},{4,68,132,196,260,324,388,452},{8,72,136..., dimensions={0} | all-to-all | bytes 327680 | tf_op jit(solution)/shard_map/all_to_all | solution.py:380
  81.0 0.7 sums.1
  81.7 3.7 %all-to-all-start.4 = ((bf16[16,56,128]{2,1,0:T(8,128)(2,1)}), bf16[16,56,128]{2,1,0:T(8,128)(2,1)S(1)}, u32[]{:S(2)}, u32[]{:S(2)}) async-start(bf16[16,56,128]{2,1,0:T(8,128)(2,1)} %bitcast.15), calls=%async_computation.4 | async-start | bytes 458752 | tf_op jit(solution)/shard_map/all_to_all | solution.py:380
  86.1 0.9 grad.1
  87.7 8.9 %all-to-all-done.4 = bf16[16,56,128]{2,1,0:T(8,128)(2,1)S(1)} async-done(((bf16[16,56,128]{2,1,0:T(8,128)(2,1)}), bf16[16,56,128]{2,1,0:T(8,128)(2,1)S(1)}, u32[]{:S(2)}, u32[]{:S(2)}) %all-to-all-start.4) | async-done | bytes 229408 | tf_op jit(solution)/shard_map/all_to_all | solution.py:380
  96.6 0.8 convert.1
  (24 shorter events, 1.7 us)
Async XLA Ops:
  0.6 8.5 %copy-start = (bf16[27,32,128]{2,1,0:T(8,128)(2,1)S(1)}, bf16[27,32,128]{2,1,0:T(8,128)(2,1)}, u32[]{:S(2)}) copy-start(bf16[27,32,128]{2,1,0:T(8,128)(2,1)} %own_weights.1) | copy-start | bytes 663556
  2.4 10.4 %all-to-all-start = ((bf16[4,32,2,512]{3,2,1,0:T(2,128)(2,1)}), bf16[4,32,2,512]{3,2,1,0:T(2,128)(2,1)S(1)}, u32[]{:S(2)}, u32[]{:S(2)}) async-start(bf16[4,32,2,512]{3,2,1,0:T(2,128)(2,1)} %broadcast_in_dim.2), calls=%async_computation | async-start | bytes 524288 | tf_op jit(solution)/shard_map/all_to_all | solution.py:386
  10.3 6.0 %copy-start.1 = (s32[1,8,1]{1,2,0:T(1,128)S(1)}, s32[1,8,1]{1,2,0:T(1,128)}, u32[]{:S(2)}) copy-start(s32[1,8,1]{1,2,0:T(1,128)} %param.9) | copy-start | bytes 100
  10.3 25.3 %copy-start.2 = (s32[2,26]{1,0:T(2,128)S(1)}, s32[2,26]{1,0:T(2,128)}, u32[]{:S(2)}) copy-start(s32[2,26]{1,0:T(2,128)} %near.3) | copy-start | bytes 628
  12.7 22.9 %all-to-all-start.1 = ((bf16[4,35,32,128]{3,2,1,0:T(8,128)(2,1)}), bf16[4,35,32,128]{3,2,1,0:T(8,128)(2,1)S(1)}, u32[]{:S(2)}, u32[]{:S(2)}) async-start(bf16[4,35,32,128]{3,2,1,0:T(8,128)(2,1)} %copies.1), calls=%async_computation.1 | async-start | bytes 2293760 | tf_op jit(solution)/shard_map/all_to_all | solution.py:402
  17.1 9.8 %collective-permute-start = (bf16[80,128]{1,0:T(8,128)(2,1)S(1)}, bf16[80,128]{1,0:T(8,128)(2,1)S(1)}, u32[]{:S(2)}, u32[]{:S(2)}) collective-permute-start(bf16[80,128]{1,0:T(8,128)(2,1)S(1)} %get-tuple-element.25), channel_id=1, source_target_pairs={{0,4},{4,8},{8,12},{16,20},{20,24},{24,28},{32,36},{36,40},{40,44}... | collective-permute-start | bytes 61448 | tf_op jit(solution)/shard_map/ppermute | solution.py:365
  23.1 5.4 %collective-permute-start.1 = (bf16[80,128]{1,0:T(8,128)(2,1)S(1)}, bf16[80,128]{1,0:T(8,128)(2,1)S(1)}, u32[]{:S(2)}, u32[]{:S(2)}) collective-permute-start(bf16[80,128]{1,0:T(8,128)(2,1)S(1)} %get-tuple-element.26), channel_id=1, source_target_pairs={{4,0},{8,4},{12,8},{20,16},{24,20},{28,24},{36,32},{40,36},{44,40}... | collective-permute-start | bytes 61448 | tf_op jit(solution)/shard_map/ppermute | solution.py:365
  28.5 9.5 %collective-permute-start.2 = (bf16[80,128]{1,0:T(8,128)(2,1)S(1)}, bf16[80,128]{1,0:T(8,128)(2,1)S(1)}, u32[]{:S(2)}, u32[]{:S(2)}) collective-permute-start(bf16[80,128]{1,0:T(8,128)(2,1)S(1)} %pad_maximum_fusion), channel_id=1, source_target_pairs={{0,16},{4,20},{8,24},{12,28},{16,32},{20,36},{24,40},{28,44},{32,4... | collective-permute-start | bytes 61448 | tf_op jit(solution)/shard_map/ppermute | solution.py:365
  34.3 7.5 %collective-permute-start.3 = (bf16[80,128]{1,0:T(8,128)(2,1)S(1)}, bf16[80,128]{1,0:T(8,128)(2,1)S(1)}, u32[]{:S(2)}, u32[]{:S(2)}) collective-permute-start(bf16[80,128]{1,0:T(8,128)(2,1)S(1)} %pad_maximum_fusion.1), channel_id=1, source_target_pairs={{16,0},{20,4},{24,8},{28,12},{32,16},{36,20},{40,24},{44,28},{48,3... | collective-permute-start | bytes 61448 | tf_op jit(solution)/shard_map/ppermute | solution.py:365
  81.7 14.9 %all-to-all-start.4 = ((bf16[16,56,128]{2,1,0:T(8,128)(2,1)}), bf16[16,56,128]{2,1,0:T(8,128)(2,1)S(1)}, u32[]{:S(2)}, u32[]{:S(2)}) async-start(bf16[16,56,128]{2,1,0:T(8,128)(2,1)} %bitcast.15), calls=%async_computation.4 | async-start | bytes 458752 | tf_op jit(solution)/shard_map/all_to_all | solution.py:380

commit v12 on v11

--- a/solution.py
+++ b/solution.py
@@ -58,6 +58,12 @@
 
 def rows_of(index, stride, first, count):
     return pl.ds(pl.multiple_of(index * stride + first, 8), count)
+
+
+def feature_copies_kernel(features, out):
+    value = features[...]
+    for i in range(out.shape[0]):
+        out[i] = value
 
 
 def copies_kernel(weights, by_lanes, out):
@@ -380,12 +386,6 @@
     return lax.all_to_all(values, "space", 0, 0, tiled=True, axis_index_groups=groups)
 
 
-def from_all_chan(part):
-    count = lax.axis_size("chan")
-    copies = jnp.broadcast_to(part[None], (count,) + part.shape)
-    return lax.all_to_all(copies, "chan", 0, 0, tiled=True)
-
-
 def on_device(features, mask_packed, neighbours, send_list, weights, cotangent):
     chan = lax.axis_index("chan").astype(jnp.int32).reshape(1)
     send = send_list.reshape(8)
@@ -393,7 +393,8 @@
     place = jnp.stack([where % GROUP, where // GROUP])
     planes = lax.axis_size("space") // GROUP
     mask = unpack_mask(mask_packed)
-    gathered = from_all_chan(features)
+    (copies,) = call(feature_copies_kernel, "sent", [], [features], [((4, 32, 2, 512), BF)], [], 16)
+    gathered = lax.all_to_all(copies, "chan", 0, 0, tiled=True)
     by_lanes = cotangent.reshape(32, 8, 128).transpose(1, 0, 2)
     (extra,) = call(
         copies_kernel, "copies", [], [weights, by_lanes], [((4, 35, 32, 128), BF)], [], 16,

time: 98 us -> 97.9 us (level)
    broadcast_in_dim x1 -> x0, local copies, waits for them, and re-layouts: 1.72 us -> none  [from_all_chan(): copies = jnp.broadcast_to(part[None], (count,) + part.shape)]
    unnamed x8 -> x10, local copies, waits for them, and re-layouts: 1.42 us -> 2.29 us
    pallas_call x7 -> x8, Pallas kernels: 9.96 us -> 10.7 us  [call(): pl.pallas_call(kernel, out_shape=shapes, in_specs=[SMEM] * len(smem) + [V...]
where the time goes in v12:
time: 97.9 us; the launch traced here: 97.3 us
  blocking collectives  35.1 us (36%)
  starting transfers between devices  28.9 us (30%)
  waiting for transfers between devices  16.7 us (17%)
  Pallas kernels  10.7 us (11%)
  local copies, waits for them, and re-layouts  4.13 us (4%)
    all_to_all x2, blocking collectives, exchanged(): lax.all_to_all(values, 'space', 0, 0, tiled=True, axis_index_groups=groups)  35.1 us
    ppermute x4, starting transfers between devices, passed_along(): return lax.ppermute(shard, 'space', pairs)  16.9 us
    pallas_call x8, Pallas kernels, call(): pl.pallas_call(kernel, out_shape=shapes, in_specs=[SMEM] * len(smem) + [V...  10.7 us
    all_to_all x1, waiting for transfers between devices, exchanged(): lax.all_to_all(values, 'space', 0, 0, tiled=True, axis_index_groups=groups)  8.9 us
    ppermute x4, waiting for transfers between devices, passed_along(): return lax.ppermute(shard, 'space', pairs)  5.39 us
    all_to_all x1, starting transfers between devices, on_device(): gathered = lax.all_to_all(copies, 'chan', 0, 0, tiled=True)  4.84 us
    all_to_all x1, starting transfers between devices, exchanged(): lax.all_to_all(values, 'space', 0, 0, tiled=True, axis_index_groups=groups)  3.73 us
    all_to_all x1, starting transfers between devices, on_device(): extra = lax.all_to_all(extra, 'chan', 0, 0, tiled=True)  3.52 us
  transfers between devices with their start and end apart: 7, of which 4 were waited for; matrix products, arithmetic and copies ran while one was open for 3% of the time, Pallas kernels for 5%

profile of v12, /device:TPU:1, one launch (start us, length us, event | category | flops | bytes accessed | tf_op | source)
XLA Modules:
  0.0 97.3 jit_solution(106297057455871975)
XLA Ops:
  0.6 0.9 copy-done.1
  1.5 0.7 sent.1
  2.3 4.8 %all-to-all-start = ((bf16[4,32,2,512]{3,2,1,0:T(2,128)(2,1)}), bf16[4,32,2,512]{3,2,1,0:T(2,128)(2,1)S(1)}, u32[]{:S(2)}, u32[]{:S(2)}) async-start(bf16[4,32,2,512]{3,2,1,0:T(2,128)(2,1)} %sent.1), calls=%async_computation | async-start | bytes 524288 | tf_op jit(solution)/shard_map/all_to_all | solution.py:397
  7.2 0.7 shift_right_logical.20
  8.0 0.9 reshape.33
  9.0 1.2 %copies.1 = bf16[4,35,32,128]{3,2,1,0:T(8,128)(2,1)} custom-call(bf16[27,32,128]{2,1,0:T(8,128)(2,1)S(1)} %copy-done, bf16[8,32,128]{2,1,0:T(8,128)(2,1)S(1)} %bitcast.31), custom_call_target="tpu_custom_call" | custom-call | bytes 8388608 | tf_op jit(solution)/shard_map/copies/pallas_call | solution.py:354
  10.2 2.4 %all-to-all-done.gathered = bf16[4,32,2,512]{3,2,1,0:T(2,128)(2,1)S(1)} async-done(((bf16[4,32,2,512]{3,2,1,0:T(2,128)(2,1)}), bf16[4,32,2,512]{3,2,1,0:T(2,128)(2,1)S(1)}, u32[]{:S(2)}, u32[]{:S(2)}) %all-to-all-start) | async-done | bytes 262176 | tf_op jit(solution)/shard_map/all_to_all | solution.py:397
  12.6 3.5 %all-to-all-start.1 = ((bf16[4,35,32,128]{3,2,1,0:T(8,128)(2,1)}), bf16[4,35,32,128]{3,2,1,0:T(8,128)(2,1)S(1)}, u32[]{:S(2)}, u32[]{:S(2)}) async-start(bf16[4,35,32,128]{3,2,1,0:T(8,128)(2,1)} %copies.1), calls=%async_computation.1 | async-start | bytes 2293760 | tf_op jit(solution)/shard_map/all_to_all | solution.py:403
  16.2 0.8 rims.1
  17.0 6.0 %collective-permute-start = (bf16[80,128]{1,0:T(8,128)(2,1)S(1)}, bf16[80,128]{1,0:T(8,128)(2,1)S(1)}, u32[]{:S(2)}, u32[]{:S(2)}) collective-permute-start(bf16[80,128]{1,0:T(8,128)(2,1)S(1)} %get-tuple-element.25), channel_id=1, source_target_pairs={{0,4},{4,8},{8,12},{16,20},{20,24},{24,28},{32,36},{36,40},{40,44}... | collective-permute-start | bytes 61448 | tf_op jit(solution)/shard_map/ppermute | solution.py:371
  23.0 3.8 %collective-permute-start.1 = (bf16[80,128]{1,0:T(8,128)(2,1)S(1)}, bf16[80,128]{1,0:T(8,128)(2,1)S(1)}, u32[]{:S(2)}, u32[]{:S(2)}) collective-permute-start(bf16[80,128]{1,0:T(8,128)(2,1)S(1)} %get-tuple-element.26), channel_id=1, source_target_pairs={{4,0},{8,4},{12,8},{20,16},{24,20},{28,24},{36,32},{40,36},{44,40}... | collective-permute-start | bytes 61448 | tf_op jit(solution)/shard_map/ppermute | solution.py:371
  26.8 1.6 %collective-permute-done.1.from_bp = bf16[80,128]{1,0:T(8,128)(2,1)S(1)} collective-permute-done((bf16[80,128]{1,0:T(8,128)(2,1)S(1)}, bf16[80,128]{1,0:T(8,128)(2,1)S(1)}, u32[]{:S(2)}, u32[]{:S(2)}) %collective-permute-start.1) | collective-permute-done | bytes 20512 | tf_op jit(solution)/shard_map/ppermute | solution.py:371
  28.4 5.8 %collective-permute-start.2 = (bf16[80,128]{1,0:T(8,128)(2,1)S(1)}, bf16[80,128]{1,0:T(8,128)(2,1)S(1)}, u32[]{:S(2)}, u32[]{:S(2)}) collective-permute-start(bf16[80,128]{1,0:T(8,128)(2,1)S(1)} %pad_maximum_fusion), channel_id=1, source_target_pairs={{0,16},{4,20},{8,24},{12,28},{16,32},{20,36},{24,40},{28,44},{32,4... | collective-permute-start | bytes 61448 | tf_op jit(solution)/shard_map/ppermute | solution.py:371
  34.2 1.3 %collective-permute-start.3 = (bf16[80,128]{1,0:T(8,128)(2,1)S(1)}, bf16[80,128]{1,0:T(8,128)(2,1)S(1)}, u32[]{:S(2)}, u32[]{:S(2)}) collective-permute-start(bf16[80,128]{1,0:T(8,128)(2,1)S(1)} %pad_maximum_fusion.1), channel_id=1, source_target_pairs={{16,0},{20,4},{24,8},{28,12},{32,16},{36,20},{40,24},{44,28},{48,3... | collective-permute-start | bytes 61448 | tf_op jit(solution)/shard_map/ppermute | solution.py:371
  35.6 2.4 %center.1 = (f32[8,8,16,128]{3,2,1,0:T(8,128)S(1)}, bf16[8,10,16,128]{3,2,1,0:T(8,128)(2,1)S(1)}) custom-call(s32[2,26]{1,0:T(2,128)S(1)} %copy-done.3, s32[1]{0:T(128)} %bitcast.chan, f32[2,8,8,8,128]{4,3,2,1,0:T(8,128)S(1)} %get-tuple-element.11.local, bf16[80,128]{1,0:T(8,128)(2,1)S(1)} %collective-permute-done.from_bm, ...), custom_call_target="tpu_custom_call" | custom-call | flops 1073741824 | bytes 3145728 | tf_op jit(solution)/shard_map/center/pallas_call | solution.py:354
  38.0 3.8 %collective-permute-done.3.from_ap = bf16[80,128]{1,0:T(8,128)(2,1)S(1)} collective-permute-done((bf16[80,128]{1,0:T(8,128)(2,1)S(1)}, bf16[80,128]{1,0:T(8,128)(2,1)S(1)}, u32[]{:S(2)}, u32[]{:S(2)}) %collective-permute-start.3) | collective-permute-done | bytes 20512 | tf_op jit(solution)/shard_map/ppermute | solution.py:371
  41.7 3.3 %conv.1 = (bf16[2,32,512]{2,1,0:T(8,128)(2,1)S(1)}, bf16[1152,128]{1,0:T(8,128)(2,1)S(1)}, f32[2,8,8,8,128]{4,3,2,1,0:T(8,128)S(1)}) custom-call(s32[2,26]{1,0:T(2,128)S(1)} %copy-done.3, s32[1]{0:T(128)} %bitcast.chan, s32[2]{0:T(128)S(1)} %pad_add_fusion.place, f32[2,512]{1,0:T(2,128)S(1)} %and_convert_fusion.mask, ...), custom_call_target="tpu_custom_call" | custom-call | tf_op jit(solution)/shard_map/conv/pallas_call | solution.py:354
  45.0 18.2 %all_to_all.44 = bf16[16,72,128]{2,1,0:T(8,128)(2,1)S(1)} all-to-all(bf16[16,72,128]{2,1,0:T(8,128)(2,1)S(1)} %bitcast.30), channel_id=1, replica_groups={{0,4,8,12,16,20,24,28,32,36,40,44,48,52,56,60},{64,68,72,76,80,84,88,92..., dimensions={0} | all-to-all | bytes 589824 | tf_op jit(solution)/shard_map/all_to_all | solution.py:386
  63.2 0.8 middle.1
  64.0 16.9 %all_to_all.45 = bf16[8,80,128]{2,1,0:T(8,128)(2,1)S(1)} all-to-all(bf16[8,80,128]{2,1,0:T(8,128)(2,1)S(1)} %bitcast.29), channel_id=1, replica_groups={{0,64,128,192,256,320,384,448},{4,68,132,196,260,324,388,452},{8,72,136..., dimensions={0} | all-to-all | bytes 327680 | tf_op jit(solution)/shard_map/all_to_all | solution.py:386
  81.6 3.7 %all-to-all-start.4 = ((bf16[16,56,128]{2,1,0:T(8,128)(2,1)}), bf16[16,56,128]{2,1,0:T(8,128)(2,1)S(1)}, u32[]{:S(2)}, u32[]{:S(2)}) async-start(bf16[16,56,128]{2,1,0:T(8,128)(2,1)} %bitcast.15), calls=%async_computation.4 | async-start | bytes 458752 | tf_op jit(solution)/shard_map/all_to_all | solution.py:386
  86.0 0.9 grad.1
  87.6 8.9 %all-to-all-done.4 = bf16[16,56,128]{2,1,0:T(8,128)(2,1)S(1)} async-done(((bf16[16,56,128]{2,1,0:T(8,128)(2,1)}), bf16[16,56,128]{2,1,0:T(8,128)(2,1)S(1)}, u32[]{:S(2)}, u32[]{:S(2)}) %all-to-all-start.4) | async-done | bytes 229408 | tf_op jit(solution)/shard_map/all_to_all | solution.py:386
  96.5 0.8 convert.1
  (26 shorter events, 2.4 us)
Async XLA Ops:
  0.6 8.4 %copy-start = (bf16[27,32,128]{2,1,0:T(8,128)(2,1)S(1)}, bf16[27,32,128]{2,1,0:T(8,128)(2,1)}, u32[]{:S(2)}) copy-start(bf16[27,32,128]{2,1,0:T(8,128)(2,1)} %own_weights.1) | copy-start | bytes 663556
  0.6 0.9 copy-start.1
  2.3 10.4 %all-to-all-start = ((bf16[4,32,2,512]{3,2,1,0:T(2,128)(2,1)}), bf16[4,32,2,512]{3,2,1,0:T(2,128)(2,1)S(1)}, u32[]{:S(2)}, u32[]{:S(2)}) async-start(bf16[4,32,2,512]{3,2,1,0:T(2,128)(2,1)} %sent.1), calls=%async_computation | async-start | bytes 524288 | tf_op jit(solution)/shard_map/all_to_all | solution.py:397
  10.2 5.9 %copy-start.2 = (s32[1,8,1]{1,2,0:T(1,128)S(1)}, s32[1,8,1]{1,2,0:T(1,128)}, u32[]{:S(2)}) copy-start(s32[1,8,1]{1,2,0:T(1,128)} %param.9) | copy-start | bytes 100
  10.2 25.3 %copy-start.3 = (s32[2,26]{1,0:T(2,128)S(1)}, s32[2,26]{1,0:T(2,128)}, u32[]{:S(2)}) copy-start(s32[2,26]{1,0:T(2,128)} %near.3) | copy-start | bytes 628
  12.6 22.9 %all-to-all-start.1 = ((bf16[4,35,32,128]{3,2,1,0:T(8,128)(2,1)}), bf16[4,35,32,128]{3,2,1,0:T(8,128)(2,1)S(1)}, u32[]{:S(2)}, u32[]{:S(2)}) async-start(bf16[4,35,32,128]{3,2,1,0:T(8,128)(2,1)} %copies.1), calls=%async_computation.1 | async-start | bytes 2293760 | tf_op jit(solution)/shard_map/all_to_all | solution.py:403
  17.0 9.8 %collective-permute-start = (bf16[80,128]{1,0:T(8,128)(2,1)S(1)}, bf16[80,128]{1,0:T(8,128)(2,1)S(1)}, u32[]{:S(2)}, u32[]{:S(2)}) collective-permute-start(bf16[80,128]{1,0:T(8,128)(2,1)S(1)} %get-tuple-element.25), channel_id=1, source_target_pairs={{0,4},{4,8},{8,12},{16,20},{20,24},{24,28},{32,36},{36,40},{40,44}... | collective-permute-start | bytes 61448 | tf_op jit(solution)/shard_map/ppermute | solution.py:371
  23.0 5.4 %collective-permute-start.1 = (bf16[80,128]{1,0:T(8,128)(2,1)S(1)}, bf16[80,128]{1,0:T(8,128)(2,1)S(1)}, u32[]{:S(2)}, u32[]{:S(2)}) collective-permute-start(bf16[80,128]{1,0:T(8,128)(2,1)S(1)} %get-tuple-element.26), channel_id=1, source_target_pairs={{4,0},{8,4},{12,8},{20,16},{24,20},{28,24},{36,32},{40,36},{44,40}... | collective-permute-start | bytes 61448 | tf_op jit(solution)/shard_map/ppermute | solution.py:371
  28.4 9.5 %collective-permute-start.2 = (bf16[80,128]{1,0:T(8,128)(2,1)S(1)}, bf16[80,128]{1,0:T(8,128)(2,1)S(1)}, u32[]{:S(2)}, u32[]{:S(2)}) collective-permute-start(bf16[80,128]{1,0:T(8,128)(2,1)S(1)} %pad_maximum_fusion), channel_id=1, source_target_pairs={{0,16},{4,20},{8,24},{12,28},{16,32},{20,36},{24,40},{28,44},{32,4... | collective-permute-start | bytes 61448 | tf_op jit(solution)/shard_map/ppermute | solution.py:371
  34.2 7.5 %collective-permute-start.3 = (bf16[80,128]{1,0:T(8,128)(2,1)S(1)}, bf16[80,128]{1,0:T(8,128)(2,1)S(1)}, u32[]{:S(2)}, u32[]{:S(2)}) collective-permute-start(bf16[80,128]{1,0:T(8,128)(2,1)S(1)} %pad_maximum_fusion.1), channel_id=1, source_target_pairs={{16,0},{20,4},{24,8},{28,12},{32,16},{36,20},{40,24},{44,28},{48,3... | collective-permute-start | bytes 61448 | tf_op jit(solution)/shard_map/ppermute | solution.py:371
  81.6 14.9 %all-to-all-start.4 = ((bf16[16,56,128]{2,1,0:T(8,128)(2,1)}), bf16[16,56,128]{2,1,0:T(8,128)(2,1)S(1)}, u32[]{:S(2)}, u32[]{:S(2)}) async-start(bf16[16,56,128]{2,1,0:T(8,128)(2,1)} %bitcast.15), calls=%async_computation.4 | async-start | bytes 458752 | tf_op jit(solution)/shard_map/all_to_all | solution.py:386

commit v13 on v12

--- a/solution.py
+++ b/solution.py
@@ -400,11 +400,12 @@
         copies_kernel, "copies", [], [weights, by_lanes], [((4, 35, 32, 128), BF)], [], 16,
         pl.CostEstimate(flops=0, bytes_accessed=8 << 20, transcendentals=0),
     )
-    extra = lax.all_to_all(extra, "chan", 0, 0, tiled=True)
     local, to_b, face_a = call(
         rims_kernel, "rims", [send], [mask, gathered],
         [((2, 8, 8, 8, 128), F32), ((2, 80, 128), BF), ((2, 64, 128), BF)], [], 16,
     )
+    extra, to_b = lax.optimization_barrier((extra, to_b))
+    extra = lax.all_to_all(extra, "chan", 0, 0, tiled=True)
     from_bm, from_bp = passed_along(to_b[0], 1), passed_along(to_b[1], -1)
     to_am = jnp.concatenate([face_a[0], from_bm[64:72], from_bp[64:72]], axis=0)
     to_ap = jnp.concatenate([face_a[1], from_bm[72:80], from_bp[72:80]], axis=0)

time: 97.9 us -> 98.1 us (level)
  no operation moved by 1% of the time
where the time goes in v13:
time: 98.1 us; the launch traced here: 97.5 us
  blocking collectives  35.1 us (36%)
  starting transfers between devices  29.1 us (30%)
  waiting for transfers between devices  16.7 us (17%)
  Pallas kernels  10.7 us (11%)
  local copies, waits for them, and re-layouts  4.13 us (4%)
    all_to_all x2, blocking collectives, exchanged(): lax.all_to_all(values, 'space', 0, 0, tiled=True, axis_index_groups=groups)  35.1 us
    ppermute x4, starting transfers between devices, passed_along(): return lax.ppermute(shard, 'space', pairs)  16.9 us
    pallas_call x8, Pallas kernels, call(): pl.pallas_call(kernel, out_shape=shapes, in_specs=[SMEM] * len(smem) + [V...  10.7 us
    all_to_all x1, waiting for transfers between devices, exchanged(): lax.all_to_all(values, 'space', 0, 0, tiled=True, axis_index_groups=groups)  8.9 us
    ppermute x4, waiting for transfers between devices, passed_along(): return lax.ppermute(shard, 'space', pairs)  5.38 us
    all_to_all x1, starting transfers between devices, on_device(): gathered = lax.all_to_all(copies, 'chan', 0, 0, tiled=True)  4.97 us
    all_to_all x1, starting transfers between devices, exchanged(): lax.all_to_all(values, 'space', 0, 0, tiled=True, axis_index_groups=groups)  3.73 us
    all_to_all x1, starting transfers between devices, on_device(): extra = lax.all_to_all(extra, 'chan', 0, 0, tiled=True)  3.54 us
  transfers between devices with their start and end apart: 7, of which 4 were waited for; matrix products, arithmetic and copies ran while one was open for 3% of the time, Pallas kernels for 5%

profile of v13, /device:TPU:1, one launch (start us, length us, event | category | flops | bytes accessed | tf_op | source)
XLA Modules:
  0.0 97.5 jit_solution(17095023568640870561)
XLA Ops:
  0.6 0.9 copy-done.1
  1.5 0.7 sent.1
  2.3 5.0 %all-to-all-start = ((bf16[4,32,2,512]{3,2,1,0:T(2,128)(2,1)}), bf16[4,32,2,512]{3,2,1,0:T(2,128)(2,1)S(1)}, u32[]{:S(2)}, u32[]{:S(2)}) async-start(bf16[4,32,2,512]{3,2,1,0:T(2,128)(2,1)} %sent.1), calls=%async_computation | async-start | bytes 524288 | tf_op jit(solution)/shard_map/all_to_all | solution.py:397
  7.3 0.7 shift_right_logical.20
  8.2 0.9 reshape.33
  9.2 1.2 %copies.1 = bf16[4,35,32,128]{3,2,1,0:T(8,128)(2,1)} custom-call(bf16[27,32,128]{2,1,0:T(8,128)(2,1)S(1)} %copy-done, bf16[8,32,128]{2,1,0:T(8,128)(2,1)S(1)} %bitcast.31), custom_call_target="tpu_custom_call" | custom-call | bytes 8388608 | tf_op jit(solution)/shard_map/copies/pallas_call | solution.py:354
  10.4 2.4 %all-to-all-done.gathered = bf16[4,32,2,512]{3,2,1,0:T(2,128)(2,1)S(1)} async-done(((bf16[4,32,2,512]{3,2,1,0:T(2,128)(2,1)}), bf16[4,32,2,512]{3,2,1,0:T(2,128)(2,1)S(1)}, u32[]{:S(2)}, u32[]{:S(2)}) %all-to-all-start) | async-done | bytes 262176 | tf_op jit(solution)/shard_map/all_to_all | solution.py:397
  12.8 0.8 rims.1
  13.6 3.5 %all-to-all-start.1 = ((bf16[4,35,32,128]{3,2,1,0:T(8,128)(2,1)}), bf16[4,35,32,128]{3,2,1,0:T(8,128)(2,1)S(1)}, u32[]{:S(2)}, u32[]{:S(2)}) async-start(bf16[4,35,32,128]{3,2,1,0:T(8,128)(2,1)} %copies.1), calls=%async_computation.1 | async-start | bytes 2293760 | tf_op jit(solution)/shard_map/all_to_all | solution.py:408
  17.2 6.0 %collective-permute-start = (bf16[80,128]{1,0:T(8,128)(2,1)S(1)}, bf16[80,128]{1,0:T(8,128)(2,1)S(1)}, u32[]{:S(2)}, u32[]{:S(2)}) collective-permute-start(bf16[80,128]{1,0:T(8,128)(2,1)S(1)} %get-tuple-element.29), channel_id=1, source_target_pairs={{0,4},{4,8},{8,12},{16,20},{20,24},{24,28},{32,36},{36,40},{40,44}... | collective-permute-start | bytes 61448 | tf_op jit(solution)/shard_map/ppermute | solution.py:371
  23.2 3.8 %collective-permute-start.1 = (bf16[80,128]{1,0:T(8,128)(2,1)S(1)}, bf16[80,128]{1,0:T(8,128)(2,1)S(1)}, u32[]{:S(2)}, u32[]{:S(2)}) collective-permute-start(bf16[80,128]{1,0:T(8,128)(2,1)S(1)} %get-tuple-element.30), channel_id=1, source_target_pairs={{4,0},{8,4},{12,8},{20,16},{24,20},{28,24},{36,32},{40,36},{44,40}... | collective-permute-start | bytes 61448 | tf_op jit(solution)/shard_map/ppermute | solution.py:371
  27.0 1.6 %collective-permute-done.1.from_bp = bf16[80,128]{1,0:T(8,128)(2,1)S(1)} collective-permute-done((bf16[80,128]{1,0:T(8,128)(2,1)S(1)}, bf16[80,128]{1,0:T(8,128)(2,1)S(1)}, u32[]{:S(2)}, u32[]{:S(2)}) %collective-permute-start.1) | collective-permute-done | bytes 20512 | tf_op jit(solution)/shard_map/ppermute | solution.py:371
  28.6 5.8 %collective-permute-start.2 = (bf16[80,128]{1,0:T(8,128)(2,1)S(1)}, bf16[80,128]{1,0:T(8,128)(2,1)S(1)}, u32[]{:S(2)}, u32[]{:S(2)}) collective-permute-start(bf16[80,128]{1,0:T(8,128)(2,1)S(1)} %pad_maximum_fusion), channel_id=1, source_target_pairs={{0,16},{4,20},{8,24},{12,28},{16,32},{20,36},{24,40},{28,44},{32,4... | collective-permute-start | bytes 61448 | tf_op jit(solution)/shard_map/ppermute | solution.py:371
  34.4 1.3 %collective-permute-start.3 = (bf16[80,128]{1,0:T(8,128)(2,1)S(1)}, bf16[80,128]{1,0:T(8,128)(2,1)S(1)}, u32[]{:S(2)}, u32[]{:S(2)}) collective-permute-start(bf16[80,128]{1,0:T(8,128)(2,1)S(1)} %pad_maximum_fusion.1), channel_id=1, source_target_pairs={{16,0},{20,4},{24,8},{28,12},{32,16},{36,20},{40,24},{44,28},{48,3... | collective-permute-start | bytes 61448 | tf_op jit(solution)/shard_map/ppermute | solution.py:371
  35.7 2.4 %center.1 = (f32[8,8,16,128]{3,2,1,0:T(8,128)S(1)}, bf16[8,10,16,128]{3,2,1,0:T(8,128)(2,1)S(1)}) custom-call(s32[2,26]{1,0:T(2,128)S(1)} %copy-done.3, s32[1]{0:T(128)} %bitcast.chan, f32[2,8,8,8,128]{4,3,2,1,0:T(8,128)S(1)} %get-tuple-element.13.local, bf16[80,128]{1,0:T(8,128)(2,1)S(1)} %collective-permute-done.from_bm, ...), custom_call_target="tpu_custom_call" | custom-call | flops 1073741824 | bytes 3145728 | tf_op jit(solution)/shard_map/center/pallas_call | solution.py:354
  38.1 3.8 %collective-permute-done.3.from_ap = bf16[80,128]{1,0:T(8,128)(2,1)S(1)} collective-permute-done((bf16[80,128]{1,0:T(8,128)(2,1)S(1)}, bf16[80,128]{1,0:T(8,128)(2,1)S(1)}, u32[]{:S(2)}, u32[]{:S(2)}) %collective-permute-start.3) | collective-permute-done | bytes 20512 | tf_op jit(solution)/shard_map/ppermute | solution.py:371
  41.9 3.3 %conv.1 = (bf16[2,32,512]{2,1,0:T(8,128)(2,1)S(1)}, bf16[1152,128]{1,0:T(8,128)(2,1)S(1)}, f32[2,8,8,8,128]{4,3,2,1,0:T(8,128)S(1)}) custom-call(s32[2,26]{1,0:T(2,128)S(1)} %copy-done.3, s32[1]{0:T(128)} %bitcast.chan, s32[2]{0:T(128)S(1)} %pad_add_fusion.place, f32[2,512]{1,0:T(2,128)S(1)} %and_convert_fusion.mask, ...), custom_call_target="tpu_custom_call" | custom-call | tf_op jit(solution)/shard_map/conv/pallas_call | solution.py:354
  45.2 18.2 %all_to_all.44 = bf16[16,72,128]{2,1,0:T(8,128)(2,1)S(1)} all-to-all(bf16[16,72,128]{2,1,0:T(8,128)(2,1)S(1)} %bitcast.30), channel_id=1, replica_groups={{0,4,8,12,16,20,24,28,32,36,40,44,48,52,56,60},{64,68,72,76,80,84,88,92..., dimensions={0} | all-to-all | bytes 589824 | tf_op jit(solution)/shard_map/all_to_all | solution.py:386
  63.4 0.8 middle.1
  64.1 16.9 %all_to_all.45 = bf16[8,80,128]{2,1,0:T(8,128)(2,1)S(1)} all-to-all(bf16[8,80,128]{2,1,0:T(8,128)(2,1)S(1)} %bitcast.29), channel_id=1, replica_groups={{0,64,128,192,256,320,384,448},{4,68,132,196,260,324,388,452},{8,72,136..., dimensions={0} | all-to-all | bytes 327680 | tf_op jit(solution)/shard_map/all_to_all | solution.py:386
  81.8 3.7 %all-to-all-start.4 = ((bf16[16,56,128]{2,1,0:T(8,128)(2,1)}), bf16[16,56,128]{2,1,0:T(8,128)(2,1)S(1)}, u32[]{:S(2)}, u32[]{:S(2)}) async-start(bf16[16,56,128]{2,1,0:T(8,128)(2,1)} %bitcast.15), calls=%async_computation.4 | async-start | bytes 458752 | tf_op jit(solution)/shard_map/all_to_all | solution.py:386
  86.2 0.9 grad.1
  87.7 8.9 %all-to-all-done.4 = bf16[16,56,128]{2,1,0:T(8,128)(2,1)S(1)} async-done(((bf16[16,56,128]{2,1,0:T(8,128)(2,1)}), bf16[16,56,128]{2,1,0:T(8,128)(2,1)S(1)}, u32[]{:S(2)}, u32[]{:S(2)}) %all-to-all-start.4) | async-done | bytes 229408 | tf_op jit(solution)/shard_map/all_to_all | solution.py:386
  96.7 0.8 convert.1
  (26 shorter events, 2.4 us)
Async XLA Ops:
  0.6 8.5 %copy-start = (bf16[27,32,128]{2,1,0:T(8,128)(2,1)S(1)}, bf16[27,32,128]{2,1,0:T(8,128)(2,1)}, u32[]{:S(2)}) copy-start(bf16[27,32,128]{2,1,0:T(8,128)(2,1)} %own_weights.1) | copy-start | bytes 663556
  0.6 0.9 copy-start.1
  2.3 10.5 %copy-start.2 = (s32[1,8,1]{1,2,0:T(1,128)S(1)}, s32[1,8,1]{1,2,0:T(1,128)}, u32[]{:S(2)}) copy-start(s32[1,8,1]{1,2,0:T(1,128)} %param.9) | copy-start | bytes 100
  2.3 10.5 %all-to-all-start = ((bf16[4,32,2,512]{3,2,1,0:T(2,128)(2,1)}), bf16[4,32,2,512]{3,2,1,0:T(2,128)(2,1)S(1)}, u32[]{:S(2)}, u32[]{:S(2)}) async-start(bf16[4,32,2,512]{3,2,1,0:T(2,128)(2,1)} %sent.1), calls=%async_computation | async-start | bytes 524288 | tf_op jit(solution)/shard_map/all_to_all | solution.py:397
  13.6 22.1 %copy-start.3 = (s32[2,26]{1,0:T(2,128)S(1)}, s32[2,26]{1,0:T(2,128)}, u32[]{:S(2)}) copy-start(s32[2,26]{1,0:T(2,128)} %near.3) | copy-start | bytes 628
  13.6 22.1 %all-to-all-start.1 = ((bf16[4,35,32,128]{3,2,1,0:T(8,128)(2,1)}), bf16[4,35,32,128]{3,2,1,0:T(8,128)(2,1)S(1)}, u32[]{:S(2)}, u32[]{:S(2)}) async-start(bf16[4,35,32,128]{3,2,1,0:T(8,128)(2,1)} %copies.1), calls=%async_computation.1 | async-start | bytes 2293760 | tf_op jit(solution)/shard_map/all_to_all | solution.py:408
  17.2 9.8 %collective-permute-start = (bf16[80,128]{1,0:T(8,128)(2,1)S(1)}, bf16[80,128]{1,0:T(8,128)(2,1)S(1)}, u32[]{:S(2)}, u32[]{:S(2)}) collective-permute-start(bf16[80,128]{1,0:T(8,128)(2,1)S(1)} %get-tuple-element.29), channel_id=1, source_target_pairs={{0,4},{4,8},{8,12},{16,20},{20,24},{24,28},{32,36},{36,40},{40,44}... | collective-permute-start | bytes 61448 | tf_op jit(solution)/shard_map/ppermute | solution.py:371
  23.2 5.4 %collective-permute-start.1 = (bf16[80,128]{1,0:T(8,128)(2,1)S(1)}, bf16[80,128]{1,0:T(8,128)(2,1)S(1)}, u32[]{:S(2)}, u32[]{:S(2)}) collective-permute-start(bf16[80,128]{1,0:T(8,128)(2,1)S(1)} %get-tuple-element.30), channel_id=1, source_target_pairs={{4,0},{8,4},{12,8},{20,16},{24,20},{28,24},{36,32},{40,36},{44,40}... | collective-permute-start | bytes 61448 | tf_op jit(solution)/shard_map/ppermute | solution.py:371
  28.6 9.5 %collective-permute-start.2 = (bf16[80,128]{1,0:T(8,128)(2,1)S(1)}, bf16[80,128]{1,0:T(8,128)(2,1)S(1)}, u32[]{:S(2)}, u32[]{:S(2)}) collective-permute-start(bf16[80,128]{1,0:T(8,128)(2,1)S(1)} %pad_maximum_fusion), channel_id=1, source_target_pairs={{0,16},{4,20},{8,24},{12,28},{16,32},{20,36},{24,40},{28,44},{32,4... | collective-permute-start | bytes 61448 | tf_op jit(solution)/shard_map/ppermute | solution.py:371
  34.4 7.5 %collective-permute-start.3 = (bf16[80,128]{1,0:T(8,128)(2,1)S(1)}, bf16[80,128]{1,0:T(8,128)(2,1)S(1)}, u32[]{:S(2)}, u32[]{:S(2)}) collective-permute-start(bf16[80,128]{1,0:T(8,128)(2,1)S(1)} %pad_maximum_fusion.1), channel_id=1, source_target_pairs={{16,0},{20,4},{24,8},{28,12},{32,16},{36,20},{40,24},{44,28},{48,3... | collective-permute-start | bytes 61448 | tf_op jit(solution)/shard_map/ppermute | solution.py:371
  81.8 14.9 %all-to-all-start.4 = ((bf16[16,56,128]{2,1,0:T(8,128)(2,1)}), bf16[16,56,128]{2,1,0:T(8,128)(2,1)S(1)}, u32[]{:S(2)}, u32[]{:S(2)}) async-start(bf16[16,56,128]{2,1,0:T(8,128)(2,1)} %bitcast.15), calls=%async_computation.4 | async-start | bytes 458752 | tf_op jit(solution)/shard_map/all_to_all | solution.py:386

commit v14 on v12

--- a/solution.py
+++ b/solution.py
@@ -400,12 +400,13 @@
         copies_kernel, "copies", [], [weights, by_lanes], [((4, 35, 32, 128), BF)], [], 16,
         pl.CostEstimate(flops=0, bytes_accessed=8 << 20, transcendentals=0),
     )
-    extra = lax.all_to_all(extra, "chan", 0, 0, tiled=True)
     local, to_b, face_a = call(
         rims_kernel, "rims", [send], [mask, gathered],
         [((2, 8, 8, 8, 128), F32), ((2, 80, 128), BF), ((2, 64, 128), BF)], [], 16,
     )
     from_bm, from_bp = passed_along(to_b[0], 1), passed_along(to_b[1], -1)
+    extra, from_bm = lax.optimization_barrier((extra, from_bm))
+    extra = lax.all_to_all(extra, "chan", 0, 0, tiled=True)
     to_am = jnp.concatenate([face_a[0], from_bm[64:72], from_bp[64:72]], axis=0)
     to_ap = jnp.concatenate([face_a[1], from_bm[72:80], from_bp[72:80]], axis=0)
     from_am, from_ap = passed_along(to_am, 4), passed_along(to_ap, -4)

time: 97.9 us -> 105 us (1.073)
  waiting for transfers between devices: 16.7 us -> 24.5 us
  starting transfers between devices: 28.9 us -> 27.2 us
  blocking collectives: 35.1 us -> 36.3 us
    all_to_all x1, waiting for transfers between devices: 0.01 us -> 11 us  [on_device(): extra = lax.all_to_all(extra, 'chan', 0, 0, tiled=True)]
    ppermute x4, waiting for transfers between devices: 5.39 us -> 0.01 us  [passed_along(): return lax.ppermute(shard, 'space', pairs)]
    all_to_all x1, waiting for transfers between devices: 2.39 us -> 4.6 us  [on_device(): gathered = lax.all_to_all(copies, 'chan', 0, 0, tiled=True)]
    ppermute x4, starting transfers between devices: 16.9 us -> 15.1 us  [passed_along(): return lax.ppermute(shard, 'space', pairs)]
    all_to_all x2, blocking collectives: 35.1 us -> 36.3 us  [exchanged(): lax.all_to_all(values, 'space', 0, 0, tiled=True, axis_index_groups=groups)]
    unnamed x10 -> x14, local copies, waits for them, and re-layouts: 2.29 us -> 2.95 us
  transfers between devices with their start and end apart: 7 -> 7, of which waited for: 4 -> 3; matrix products, arithmetic and copies ran while one was open for 3% -> 2% of each run, Pallas kernels for 5% -> 4%
where the time goes in v14:
time: 105 us; the launch traced here: 104 us
  blocking collectives  36.3 us (35%)
  starting transfers between devices  27.2 us (26%)
  waiting for transfers between devices  24.5 us (23%)
  Pallas kernels  10.7 us (10%)
  local copies, waits for them, and re-layouts  3.95 us (4%)
    all_to_all x2, blocking collectives, exchanged(): lax.all_to_all(values, 'space', 0, 0, tiled=True, axis_index_groups=groups)  36.3 us
    ppermute x4, starting transfers between devices, passed_along(): return lax.ppermute(shard, 'space', pairs)  15.1 us
    all_to_all x1, waiting for transfers between devices, on_device(): extra = lax.all_to_all(extra, 'chan', 0, 0, tiled=True)  11 us
    pallas_call x8, Pallas kernels, call(): pl.pallas_call(kernel, out_shape=shapes, in_specs=[SMEM] * len(smem) + [V...  10.7 us
    all_to_all x1, waiting for transfers between devices, exchanged(): lax.all_to_all(values, 'space', 0, 0, tiled=True, axis_index_groups=groups)  8.89 us
    all_to_all x1, starting transfers between devices, on_device(): gathered = lax.all_to_all(copies, 'chan', 0, 0, tiled=True)  4.84 us
    all_to_all x1, waiting for transfers between devices, on_device(): gathered = lax.all_to_all(copies, 'chan', 0, 0, tiled=True)  4.6 us
    all_to_all x1, starting transfers between devices, exchanged(): lax.all_to_all(values, 'space', 0, 0, tiled=True, axis_index_groups=groups)  3.73 us
  transfers between devices with their start and end apart: 7, of which 3 were waited for; matrix products, arithmetic and copies ran while one was open for 2% of the time, Pallas kernels for 4%

profile of v14, /device:TPU:1, one launch (start us, length us, event | category | flops | bytes accessed | tf_op | source)
XLA Modules:
  0.0 104.5 jit_solution(13678872841736562652)
XLA Ops:
  0.7 0.9 copy-done.1
  1.5 0.7 sent.1
  2.3 4.8 %all-to-all-start = ((bf16[4,32,2,512]{3,2,1,0:T(2,128)(2,1)}), bf16[4,32,2,512]{3,2,1,0:T(2,128)(2,1)S(1)}, u32[]{:S(2)}, u32[]{:S(2)}) async-start(bf16[4,32,2,512]{3,2,1,0:T(2,128)(2,1)} %sent.1), calls=%async_computation | async-start | bytes 524288 | tf_op jit(solution)/shard_map/all_to_all | solution.py:397
  7.2 0.7 shift_right_logical.20
  8.0 4.6 %all-to-all-done.gathered = bf16[4,32,2,512]{3,2,1,0:T(2,128)(2,1)S(1)} async-done(((bf16[4,32,2,512]{3,2,1,0:T(2,128)(2,1)}), bf16[4,32,2,512]{3,2,1,0:T(2,128)(2,1)S(1)}, u32[]{:S(2)}, u32[]{:S(2)}) %all-to-all-start) | async-done | bytes 262176 | tf_op jit(solution)/shard_map/all_to_all | solution.py:397
  13.3 0.8 rims.1
  14.1 6.0 %collective-permute-start = (bf16[80,128]{1,0:T(8,128)(2,1)S(1)}, bf16[80,128]{1,0:T(8,128)(2,1)S(1)}, u32[]{:S(2)}, u32[]{:S(2)}) collective-permute-start(bf16[80,128]{1,0:T(8,128)(2,1)S(1)} %get-tuple-element.29), channel_id=1, source_target_pairs={{0,4},{4,8},{8,12},{16,20},{20,24},{24,28},{32,36},{36,40},{40,44}... | collective-permute-start | bytes 61448 | tf_op jit(solution)/shard_map/ppermute | solution.py:371
  20.3 1.2 %copies.1 = bf16[4,35,32,128]{3,2,1,0:T(8,128)(2,1)} custom-call(bf16[27,32,128]{2,1,0:T(8,128)(2,1)S(1)} %copy-done, bf16[8,32,128]{2,1,0:T(8,128)(2,1)S(1)} %bitcast.32), custom_call_target="tpu_custom_call" | custom-call | bytes 8388608 | tf_op jit(solution)/shard_map/copies/pallas_call | solution.py:354
  21.5 3.9 %collective-permute-start.1 = (bf16[80,128]{1,0:T(8,128)(2,1)S(1)}, bf16[80,128]{1,0:T(8,128)(2,1)S(1)}, u32[]{:S(2)}, u32[]{:S(2)}) collective-permute-start(bf16[80,128]{1,0:T(8,128)(2,1)S(1)} %get-tuple-element.30), channel_id=1, source_target_pairs={{4,0},{8,4},{12,8},{20,16},{24,20},{28,24},{36,32},{40,36},{44,40}... | collective-permute-start | bytes 61448 | tf_op jit(solution)/shard_map/ppermute | solution.py:371
  25.4 3.5 %all-to-all-start.1 = ((bf16[4,35,32,128]{3,2,1,0:T(8,128)(2,1)}), bf16[4,35,32,128]{3,2,1,0:T(8,128)(2,1)S(1)}, u32[]{:S(2)}, u32[]{:S(2)}) async-start(bf16[4,35,32,128]{3,2,1,0:T(8,128)(2,1)} %copies.1), calls=%async_computation.1 | async-start | bytes 2293760 | tf_op jit(solution)/shard_map/all_to_all | solution.py:409
  29.0 4.0 %collective-permute-start.2 = (bf16[80,128]{1,0:T(8,128)(2,1)S(1)}, bf16[80,128]{1,0:T(8,128)(2,1)S(1)}, u32[]{:S(2)}, u32[]{:S(2)}) collective-permute-start(bf16[80,128]{1,0:T(8,128)(2,1)S(1)} %pad_maximum_fusion), channel_id=1, source_target_pairs={{0,16},{4,20},{8,24},{12,28},{16,32},{20,36},{24,40},{28,44},{32,4... | collective-permute-start | bytes 61448 | tf_op jit(solution)/shard_map/ppermute | solution.py:371
  33.0 1.3 %collective-permute-start.3 = (bf16[80,128]{1,0:T(8,128)(2,1)S(1)}, bf16[80,128]{1,0:T(8,128)(2,1)S(1)}, u32[]{:S(2)}, u32[]{:S(2)}) collective-permute-start(bf16[80,128]{1,0:T(8,128)(2,1)S(1)} %pad_maximum_fusion.1), channel_id=1, source_target_pairs={{16,0},{20,4},{24,8},{28,12},{32,16},{36,20},{40,24},{44,28},{48,3... | collective-permute-start | bytes 61448 | tf_op jit(solution)/shard_map/ppermute | solution.py:371
  34.3 11.0 %all-to-all-done.1.extra = bf16[4,35,32,128]{3,2,1,0:T(8,128)(2,1)S(1)} async-done(((bf16[4,35,32,128]{3,2,1,0:T(8,128)(2,1)}), bf16[4,35,32,128]{3,2,1,0:T(8,128)(2,1)S(1)}, u32[]{:S(2)}, u32[]{:S(2)}) %all-to-all-start.1) | async-done | bytes 1146912 | tf_op jit(solution)/shard_map/all_to_all | solution.py:409
  45.3 2.4 %center.1 = (f32[8,8,16,128]{3,2,1,0:T(8,128)S(1)}, bf16[8,10,16,128]{3,2,1,0:T(8,128)(2,1)S(1)}) custom-call(s32[2,26]{1,0:T(2,128)S(1)} %copy-done.4, s32[1]{0:T(128)} %bitcast.chan, f32[2,8,8,8,128]{4,3,2,1,0:T(8,128)S(1)} %get-tuple-element.13.local, bf16[80,128]{1,0:T(8,128)(2,1)S(1)} %collective-permute-done.from_bm, ...), custom_call_target="tpu_custom_call" | custom-call | flops 1073741824 | bytes 3145728 | tf_op jit(solution)/shard_map/center/pallas_call | solution.py:354
  47.7 3.3 %conv.1 = (bf16[2,32,512]{2,1,0:T(8,128)(2,1)S(1)}, bf16[1152,128]{1,0:T(8,128)(2,1)S(1)}, f32[2,8,8,8,128]{4,3,2,1,0:T(8,128)S(1)}) custom-call(s32[2,26]{1,0:T(2,128)S(1)} %copy-done.4, s32[1]{0:T(128)} %bitcast.chan, s32[2]{0:T(128)S(1)} %pad_add_fusion.place, f32[2,512]{1,0:T(2,128)S(1)} %and_convert_fusion.mask, ...), custom_call_target="tpu_custom_call" | custom-call | tf_op jit(solution)/shard_map/conv/pallas_call | solution.py:354
  51.0 19.4 %all_to_all.44 = bf16[16,72,128]{2,1,0:T(8,128)(2,1)S(1)} all-to-all(bf16[16,72,128]{2,1,0:T(8,128)(2,1)S(1)} %bitcast.30), channel_id=1, replica_groups={{0,4,8,12,16,20,24,28,32,36,40,44,48,52,56,60},{64,68,72,76,80,84,88,92..., dimensions={0} | all-to-all | bytes 589824 | tf_op jit(solution)/shard_map/all_to_all | solution.py:386
  70.3 0.8 middle.1
  71.1 16.9 %all_to_all.45 = bf16[8,80,128]{2,1,0:T(8,128)(2,1)S(1)} all-to-all(bf16[8,80,128]{2,1,0:T(8,128)(2,1)S(1)} %bitcast.29), channel_id=1, replica_groups={{0,64,128,192,256,320,384,448},{4,68,132,196,260,324,388,452},{8,72,136..., dimensions={0} | all-to-all | bytes 327680 | tf_op jit(solution)/shard_map/all_to_all | solution.py:386
  88.0 0.7 sums.1
  88.7 3.7 %all-to-all-start.4 = ((bf16[16,56,128]{2,1,0:T(8,128)(2,1)}), bf16[16,56,128]{2,1,0:T(8,128)(2,1)S(1)}, u32[]{:S(2)}, u32[]{:S(2)}) async-start(bf16[16,56,128]{2,1,0:T(8,128)(2,1)} %bitcast.15), calls=%async_computation.4 | async-start | bytes 458752 | tf_op jit(solution)/shard_map/all_to_all | solution.py:386
  93.2 0.9 grad.1
  94.0 0.7 copy.13
  94.7 8.9 %all-to-all-done.4 = bf16[16,56,128]{2,1,0:T(8,128)(2,1)S(1)} async-done(((bf16[16,56,128]{2,1,0:T(8,128)(2,1)}), bf16[16,56,128]{2,1,0:T(8,128)(2,1)S(1)}, u32[]{:S(2)}, u32[]{:S(2)}) %all-to-all-start.4) | async-done | bytes 229408 | tf_op jit(solution)/shard_map/all_to_all | solution.py:386
  103.6 0.8 convert.1
  (30 shorter events, 1.7 us)
Async XLA Ops:
  0.6 19.6 %copy-start = (bf16[27,32,128]{2,1,0:T(8,128)(2,1)S(1)}, bf16[27,32,128]{2,1,0:T(8,128)(2,1)}, u32[]{:S(2)}) copy-start(bf16[27,32,128]{2,1,0:T(8,128)(2,1)} %own_weights.1) | copy-start | bytes 663556
  0.6 0.9 copy-start.1
  1.5 18.7 %copy-start.5 = (bf16[32,2,512]{2,1,0:T(2,128)(2,1)S(1)}, bf16[32,2,512]{2,1,0:T(2,128)(2,1)}, u32[]{:S(2)}) copy-start(bf16[32,2,512]{2,1,0:T(2,128)(2,1)} %param.11) | copy-start | bytes 196612
  2.3 10.4 %all-to-all-start = ((bf16[4,32,2,512]{3,2,1,0:T(2,128)(2,1)}), bf16[4,32,2,512]{3,2,1,0:T(2,128)(2,1)S(1)}, u32[]{:S(2)}, u32[]{:S(2)}) async-start(bf16[4,32,2,512]{3,2,1,0:T(2,128)(2,1)} %sent.1), calls=%async_computation | async-start | bytes 524288 | tf_op jit(solution)/shard_map/all_to_all | solution.py:397
  12.6 0.7 copy-start.2
  14.1 11.3 %collective-permute-start = (bf16[80,128]{1,0:T(8,128)(2,1)S(1)}, bf16[80,128]{1,0:T(8,128)(2,1)S(1)}, u32[]{:S(2)}, u32[]{:S(2)}) collective-permute-start(bf16[80,128]{1,0:T(8,128)(2,1)S(1)} %get-tuple-element.29), channel_id=1, source_target_pairs={{0,4},{4,8},{8,12},{16,20},{20,24},{24,28},{32,36},{36,40},{40,44}... | collective-permute-start | bytes 61448 | tf_op jit(solution)/shard_map/ppermute | solution.py:371
  21.5 23.8 %copy-start.4 = (s32[2,26]{1,0:T(2,128)S(1)}, s32[2,26]{1,0:T(2,128)}, u32[]{:S(2)}) copy-start(s32[2,26]{1,0:T(2,128)} %near.3) | copy-start | bytes 628
  21.5 7.5 %collective-permute-start.1 = (bf16[80,128]{1,0:T(8,128)(2,1)S(1)}, bf16[80,128]{1,0:T(8,128)(2,1)S(1)}, u32[]{:S(2)}, u32[]{:S(2)}) collective-permute-start(bf16[80,128]{1,0:T(8,128)(2,1)S(1)} %get-tuple-element.30), channel_id=1, source_target_pairs={{4,0},{8,4},{12,8},{20,16},{24,20},{28,24},{36,32},{40,36},{44,40}... | collective-permute-start | bytes 61448 | tf_op jit(solution)/shard_map/ppermute | solution.py:371
  25.4 19.9 %all-to-all-start.1 = ((bf16[4,35,32,128]{3,2,1,0:T(8,128)(2,1)}), bf16[4,35,32,128]{3,2,1,0:T(8,128)(2,1)S(1)}, u32[]{:S(2)}, u32[]{:S(2)}) async-start(bf16[4,35,32,128]{3,2,1,0:T(8,128)(2,1)} %copies.1), calls=%async_computation.1 | async-start | bytes 2293760 | tf_op jit(solution)/shard_map/all_to_all | solution.py:409
  29.0 18.7 %collective-permute-start.2 = (bf16[80,128]{1,0:T(8,128)(2,1)S(1)}, bf16[80,128]{1,0:T(8,128)(2,1)S(1)}, u32[]{:S(2)}, u32[]{:S(2)}) collective-permute-start(bf16[80,128]{1,0:T(8,128)(2,1)S(1)} %pad_maximum_fusion), channel_id=1, source_target_pairs={{0,16},{4,20},{8,24},{12,28},{16,32},{20,36},{24,40},{28,44},{32,4... | collective-permute-start | bytes 61448 | tf_op jit(solution)/shard_map/ppermute | solution.py:371
  33.0 14.7 %collective-permute-start.3 = (bf16[80,128]{1,0:T(8,128)(2,1)S(1)}, bf16[80,128]{1,0:T(8,128)(2,1)S(1)}, u32[]{:S(2)}, u32[]{:S(2)}) collective-permute-start(bf16[80,128]{1,0:T(8,128)(2,1)S(1)} %pad_maximum_fusion.1), channel_id=1, source_target_pairs={{16,0},{20,4},{24,8},{28,12},{32,16},{36,20},{40,24},{44,28},{48,3... | collective-permute-start | bytes 61448 | tf_op jit(solution)/shard_map/ppermute | solution.py:371
  51.0 42.2 %copy-start.3 = (s32[1,8,1]{1,2,0:T(1,128)S(1)}, s32[1,8,1]{1,2,0:T(1,128)}, u32[]{:S(2)}) copy-start(s32[1,8,1]{1,2,0:T(1,128)} %param.9) | copy-start | bytes 100
  88.7 14.9 %all-to-all-start.4 = ((bf16[16,56,128]{2,1,0:T(8,128)(2,1)}), bf16[16,56,128]{2,1,0:T(8,128)(2,1)S(1)}, u32[]{:S(2)}, u32[]{:S(2)}) async-start(bf16[16,56,128]{2,1,0:T(8,128)(2,1)} %bitcast.15), calls=%async_computation.4 | async-start | bytes 458752 | tf_op jit(solution)/shard_map/all_to_all | solution.py:386

commit v15 on v12

--- a/solution.py
+++ b/solution.py
@@ -122,7 +122,13 @@
     return jnp.where(wanted, 1.0, 0.0).astype(BF)
 
 
-def center_kernel(near, chan, local, from_bm, from_bp, extra, pre_out, own_out, blocks):
+def center_kernel(
+    near, chan, local, from_bm, from_bp, extra, own_weights, pre_out, own_out, turned, blocks
+):
+    for i in range(9):
+        piece = own_weights[3 * i : 3 * i + 3].reshape(96, 128).astype(F32)
+        piece = jnp.concatenate([piece, jnp.zeros((32, 128), F32)], axis=0)
+        turned[i] = piece.T.astype(BF)
     for i in range(3):
         for plane in (0, 9):
             blocks[i, plane] = jnp.zeros((10, 16, 128), BF)
@@ -161,7 +167,7 @@
 
 
 def main_kernel(
-    near, chan, place, mask, local, from_am, from_ap, center_pre, center_own, extra, own_weights,
+    near, chan, place, mask, local, from_am, from_ap, center_pre, center_own, extra, turned,
     act_out, sent, own_out,
     rim, grads, own_block, act_all, terms, stage,
 ):
@@ -219,9 +225,9 @@
         ]
         product = jnp.dot(back_t, jnp.concatenate(windows, axis=1), preferred_element_type=F32)
         for i in range(len(windows)):
-            turned = product[:, 128 * i : 128 * i + 128].T
+            flipped = product[:, 128 * i : 128 * i + 128].T
             for tile in range(12):
-                put_part(12 * (first + i) + tile, turned[8 * tile : 8 * tile + 8])
+                put_part(12 * (first + i) + tile, flipped[8 * tile : 8 * tile + 8])
     for tile in range(108, 112):
         put_part(tile, jnp.zeros((8, 128), F32))
     for j in range(GROUP):
@@ -237,13 +243,7 @@
         )
 
     def grad_rights(dy):
-        pieces = []
-        for dx in (-1, 0, 1):
-            first = (dx + 1) * 9 + (dy + 1) * 3
-            piece = own_weights[first : first + 3].reshape(96, 128).astype(F32)
-            piece = jnp.concatenate([piece, jnp.zeros((32, 128), F32)], axis=0)
-            pieces.append(piece.T.astype(BF))
-        return jnp.concatenate(pieces, axis=0)
+        return jnp.concatenate([turned[3 * dx + dy + 1] for dx in range(3)], axis=0)
 
     pair = jnp.concatenate([grad_rights(1), grad_rights(0)], axis=1)
     pair = jnp.dot(grad_lefts(0, 11), pair, preferred_element_type=F32).reshape(10, 11, 16, 256)
@@ -409,14 +409,14 @@
     to_am = jnp.concatenate([face_a[0], from_bm[64:72], from_bp[64:72]], axis=0)
     to_ap = jnp.concatenate([face_a[1], from_bm[72:80], from_bp[72:80]], axis=0)
     from_am, from_ap = passed_along(to_am, 4), passed_along(to_ap, -4)
-    center_pre, center_own = call(
-        center_kernel, "center", [neighbours, chan], [local, from_bm, from_bp, extra],
-        [((8, 8, 16, 128), F32), ((8, 10, 16, 128), BF)], [((3, 10, 10, 16, 128), BF)], 24,
+    center_pre, center_own, turned = call(
+        center_kernel, "center", [neighbours, chan], [local, from_bm, from_bp, extra, weights],
+        [((8, 8, 16, 128), F32), ((8, 10, 16, 128), BF), ((9, 128, 128), BF)], [((3, 10, 10, 16, 128), BF)], 24,
         pl.CostEstimate(flops=1 << 30, bytes_accessed=3 << 20, transcendentals=0),
     )
     act, sent, own = call(
         main_kernel, "conv", [neighbours, chan, place],
-        [mask, local, from_am, from_ap, center_pre, center_own, extra, weights],
+        [mask, local, from_am, from_ap, center_pre, center_own, extra, turned],
         [
             ((2, 32, 512), BF), ((GROUP * SENT, 128), BF), ((2, 8, 8, 8, 128), F32),
         ],

time: 97.9 us -> 97.9 us (level)
  no operation moved by 1% of the time
where the time goes in v15:
time: 97.9 us; the launch traced here: 97.3 us
  blocking collectives  35.1 us (36%)
  starting transfers between devices  28.9 us (30%)
  waiting for transfers between devices  16.7 us (17%)
  Pallas kernels  10.7 us (11%)
  local copies, waits for them, and re-layouts  4.13 us (4%)
    all_to_all x2, blocking collectives, exchanged(): lax.all_to_all(values, 'space', 0, 0, tiled=True, axis_index_groups=groups)  35.1 us
    ppermute x4, starting transfers between devices, passed_along(): return lax.ppermute(shard, 'space', pairs)  16.9 us
    pallas_call x8, Pallas kernels, call(): pl.pallas_call(kernel, out_shape=shapes, in_specs=[SMEM] * len(smem) + [V...  10.7 us
    all_to_all x1, waiting for transfers between devices, exchanged(): lax.all_to_all(values, 'space', 0, 0, tiled=True, axis_index_groups=groups)  8.9 us
    ppermute x4, waiting for transfers between devices, passed_along(): return lax.ppermute(shard, 'space', pairs)  5.39 us
    all_to_all x1, starting transfers between devices, on_device(): gathered = lax.all_to_all(copies, 'chan', 0, 0, tiled=True)  4.84 us
    all_to_all x1, starting transfers between devices, exchanged(): lax.all_to_all(values, 'space', 0, 0, tiled=True, axis_index_groups=groups)  3.73 us
    all_to_all x1, starting transfers between devices, on_device(): extra = lax.all_to_all(extra, 'chan', 0, 0, tiled=True)  3.52 us
  transfers between devices with their start and end apart: 7, of which 4 were waited for; matrix products, arithmetic and copies ran while one was open for 3% of the time, Pallas kernels for 5%

profile of v15, /device:TPU:1, one launch (start us, length us, event | category | flops | bytes accessed | tf_op | source)
XLA Modules:
  0.0 97.3 jit_solution(14559397977974923239)
XLA Ops:
  0.6 0.9 copy-done.1
  1.5 0.7 sent.1
  2.3 4.8 %all-to-all-start = ((bf16[4,32,2,512]{3,2,1,0:T(2,128)(2,1)}), bf16[4,32,2,512]{3,2,1,0:T(2,128)(2,1)S(1)}, u32[]{:S(2)}, u32[]{:S(2)}) async-start(bf16[4,32,2,512]{3,2,1,0:T(2,128)(2,1)} %sent.1), calls=%async_computation | async-start | bytes 524288 | tf_op jit(solution)/shard_map/all_to_all | solution.py:397
  7.2 0.7 shift_right_logical.20
  8.0 0.9 reshape.33
  9.0 1.2 %copies.1 = bf16[4,35,32,128]{3,2,1,0:T(8,128)(2,1)} custom-call(bf16[27,32,128]{2,1,0:T(8,128)(2,1)S(1)} %copy-done, bf16[8,32,128]{2,1,0:T(8,128)(2,1)S(1)} %bitcast.31), custom_call_target="tpu_custom_call" | custom-call | bytes 8388608 | tf_op jit(solution)/shard_map/copies/pallas_call | solution.py:354
  10.2 2.4 %all-to-all-done.gathered = bf16[4,32,2,512]{3,2,1,0:T(2,128)(2,1)S(1)} async-done(((bf16[4,32,2,512]{3,2,1,0:T(2,128)(2,1)}), bf16[4,32,2,512]{3,2,1,0:T(2,128)(2,1)S(1)}, u32[]{:S(2)}, u32[]{:S(2)}) %all-to-all-start) | async-done | bytes 262176 | tf_op jit(solution)/shard_map/all_to_all | solution.py:397
  12.6 3.5 %all-to-all-start.1 = ((bf16[4,35,32,128]{3,2,1,0:T(8,128)(2,1)}), bf16[4,35,32,128]{3,2,1,0:T(8,128)(2,1)S(1)}, u32[]{:S(2)}, u32[]{:S(2)}) async-start(bf16[4,35,32,128]{3,2,1,0:T(8,128)(2,1)} %copies.1), calls=%async_computation.1 | async-start | bytes 2293760 | tf_op jit(solution)/shard_map/all_to_all | solution.py:403
  16.2 0.8 rims.1
  17.0 6.0 %collective-permute-start = (bf16[80,128]{1,0:T(8,128)(2,1)S(1)}, bf16[80,128]{1,0:T(8,128)(2,1)S(1)}, u32[]{:S(2)}, u32[]{:S(2)}) collective-permute-start(bf16[80,128]{1,0:T(8,128)(2,1)S(1)} %get-tuple-element.27), channel_id=1, source_target_pairs={{0,4},{4,8},{8,12},{16,20},{20,24},{24,28},{32,36},{36,40},{40,44}... | collective-permute-start | bytes 61448 | tf_op jit(solution)/shard_map/ppermute | solution.py:371
  23.0 3.8 %collective-permute-start.1 = (bf16[80,128]{1,0:T(8,128)(2,1)S(1)}, bf16[80,128]{1,0:T(8,128)(2,1)S(1)}, u32[]{:S(2)}, u32[]{:S(2)}) collective-permute-start(bf16[80,128]{1,0:T(8,128)(2,1)S(1)} %get-tuple-element.28), channel_id=1, source_target_pairs={{4,0},{8,4},{12,8},{20,16},{24,20},{28,24},{36,32},{40,36},{44,40}... | collective-permute-start | bytes 61448 | tf_op jit(solution)/shard_map/ppermute | solution.py:371
  26.8 1.6 %collective-permute-done.1.from_bp = bf16[80,128]{1,0:T(8,128)(2,1)S(1)} collective-permute-done((bf16[80,128]{1,0:T(8,128)(2,1)S(1)}, bf16[80,128]{1,0:T(8,128)(2,1)S(1)}, u32[]{:S(2)}, u32[]{:S(2)}) %collective-permute-start.1) | collective-permute-done | bytes 20512 | tf_op jit(solution)/shard_map/ppermute | solution.py:371
  28.4 5.8 %collective-permute-start.2 = (bf16[80,128]{1,0:T(8,128)(2,1)S(1)}, bf16[80,128]{1,0:T(8,128)(2,1)S(1)}, u32[]{:S(2)}, u32[]{:S(2)}) collective-permute-start(bf16[80,128]{1,0:T(8,128)(2,1)S(1)} %pad_maximum_fusion), channel_id=1, source_target_pairs={{0,16},{4,20},{8,24},{12,28},{16,32},{20,36},{24,40},{28,44},{32,4... | collective-permute-start | bytes 61448 | tf_op jit(solution)/shard_map/ppermute | solution.py:371
  34.2 1.3 %collective-permute-start.3 = (bf16[80,128]{1,0:T(8,128)(2,1)S(1)}, bf16[80,128]{1,0:T(8,128)(2,1)S(1)}, u32[]{:S(2)}, u32[]{:S(2)}) collective-permute-start(bf16[80,128]{1,0:T(8,128)(2,1)S(1)} %pad_maximum_fusion.1), channel_id=1, source_target_pairs={{16,0},{20,4},{24,8},{28,12},{32,16},{36,20},{40,24},{44,28},{48,3... | collective-permute-start | bytes 61448 | tf_op jit(solution)/shard_map/ppermute | solution.py:371
  35.6 2.4 %center.1 = (f32[8,8,16,128]{3,2,1,0:T(8,128)S(1)}, bf16[8,10,16,128]{3,2,1,0:T(8,128)(2,1)S(1)}, bf16[9,128,128]{2,1,0:T(8,128)(2,1)S(1)}) custom-call(s32[2,26]{1,0:T(2,128)S(1)} %copy-done.3, s32[1]{0:T(128)} %bitcast.chan, f32[2,8,8,8,128]{4,3,2,1,0:T(8,128)S(1)} %get-tuple-element.12.local, bf16[80,128]{1,0:T(8,128)(2,1)S(1)} %collective-permute-done.from_bm, ...), custom_call_target="tpu_custom_call" | custom-call | flops 1073741824 | bytes 3145728 | tf_op jit(solution)/shard_map/center/pallas_call | solution.py:354
  38.0 3.8 %collective-permute-done.3.from_ap = bf16[80,128]{1,0:T(8,128)(2,1)S(1)} collective-permute-done((bf16[80,128]{1,0:T(8,128)(2,1)S(1)}, bf16[80,128]{1,0:T(8,128)(2,1)S(1)}, u32[]{:S(2)}, u32[]{:S(2)}) %collective-permute-start.3) | collective-permute-done | bytes 20512 | tf_op jit(solution)/shard_map/ppermute | solution.py:371
  41.7 3.2 %conv.1 = (bf16[2,32,512]{2,1,0:T(8,128)(2,1)S(1)}, bf16[1152,128]{1,0:T(8,128)(2,1)S(1)}, f32[2,8,8,8,128]{4,3,2,1,0:T(8,128)S(1)}) custom-call(s32[2,26]{1,0:T(2,128)S(1)} %copy-done.3, s32[1]{0:T(128)} %bitcast.chan, s32[2]{0:T(128)S(1)} %pad_add_fusion.place, f32[2,512]{1,0:T(2,128)S(1)} %and_convert_fusion.mask, ...), custom_call_target="tpu_custom_call" | custom-call | tf_op jit(solution)/shard_map/conv/pallas_call | solution.py:354
  45.0 18.2 %all_to_all.44 = bf16[16,72,128]{2,1,0:T(8,128)(2,1)S(1)} all-to-all(bf16[16,72,128]{2,1,0:T(8,128)(2,1)S(1)} %bitcast.30), channel_id=1, replica_groups={{0,4,8,12,16,20,24,28,32,36,40,44,48,52,56,60},{64,68,72,76,80,84,88,92..., dimensions={0} | all-to-all | bytes 589824 | tf_op jit(solution)/shard_map/all_to_all | solution.py:386
  63.2 0.8 middle.1
  63.9 16.9 %all_to_all.45 = bf16[8,80,128]{2,1,0:T(8,128)(2,1)S(1)} all-to-all(bf16[8,80,128]{2,1,0:T(8,128)(2,1)S(1)} %bitcast.29), channel_id=1, replica_groups={{0,64,128,192,256,320,384,448},{4,68,132,196,260,324,388,452},{8,72,136..., dimensions={0} | all-to-all | bytes 327680 | tf_op jit(solution)/shard_map/all_to_all | solution.py:386
  81.6 3.7 %all-to-all-start.4 = ((bf16[16,56,128]{2,1,0:T(8,128)(2,1)}), bf16[16,56,128]{2,1,0:T(8,128)(2,1)S(1)}, u32[]{:S(2)}, u32[]{:S(2)}) async-start(bf16[16,56,128]{2,1,0:T(8,128)(2,1)} %bitcast.15), calls=%async_computation.4 | async-start | bytes 458752 | tf_op jit(solution)/shard_map/all_to_all | solution.py:386
  86.0 0.9 grad.1
  87.6 8.9 %all-to-all-done.4 = bf16[16,56,128]{2,1,0:T(8,128)(2,1)S(1)} async-done(((bf16[16,56,128]{2,1,0:T(8,128)(2,1)}), bf16[16,56,128]{2,1,0:T(8,128)(2,1)S(1)}, u32[]{:S(2)}, u32[]{:S(2)}) %all-to-all-start.4) | async-done | bytes 229408 | tf_op jit(solution)/shard_map/all_to_all | solution.py:386
  96.5 0.8 convert.1
  (26 shorter events, 2.4 us)
Async XLA Ops:
  0.6 8.4 %copy-start = (bf16[27,32,128]{2,1,0:T(8,128)(2,1)S(1)}, bf16[27,32,128]{2,1,0:T(8,128)(2,1)}, u32[]{:S(2)}) copy-start(bf16[27,32,128]{2,1,0:T(8,128)(2,1)} %own_weights.1) | copy-start | bytes 663556
  0.6 0.9 copy-start.1
  2.3 10.4 %all-to-all-start = ((bf16[4,32,2,512]{3,2,1,0:T(2,128)(2,1)}), bf16[4,32,2,512]{3,2,1,0:T(2,128)(2,1)S(1)}, u32[]{:S(2)}, u32[]{:S(2)}) async-start(bf16[4,32,2,512]{3,2,1,0:T(2,128)(2,1)} %sent.1), calls=%async_computation | async-start | bytes 524288 | tf_op jit(solution)/shard_map/all_to_all | solution.py:397
  10.2 5.9 %copy-start.2 = (s32[1,8,1]{1,2,0:T(1,128)S(1)}, s32[1,8,1]{1,2,0:T(1,128)}, u32[]{:S(2)}) copy-start(s32[1,8,1]{1,2,0:T(1,128)} %param.9) | copy-start | bytes 100
  10.2 25.3 %copy-start.3 = (s32[2,26]{1,0:T(2,128)S(1)}, s32[2,26]{1,0:T(2,128)}, u32[]{:S(2)}) copy-start(s32[2,26]{1,0:T(2,128)} %near.3) | copy-start | bytes 628
  12.6 22.9 %all-to-all-start.1 = ((bf16[4,35,32,128]{3,2,1,0:T(8,128)(2,1)}), bf16[4,35,32,128]{3,2,1,0:T(8,128)(2,1)S(1)}, u32[]{:S(2)}, u32[]{:S(2)}) async-start(bf16[4,35,32,128]{3,2,1,0:T(8,128)(2,1)} %copies.1), calls=%async_computation.1 | async-start | bytes 2293760 | tf_op jit(solution)/shard_map/all_to_all | solution.py:403
  17.0 9.8 %collective-permute-start = (bf16[80,128]{1,0:T(8,128)(2,1)S(1)}, bf16[80,128]{1,0:T(8,128)(2,1)S(1)}, u32[]{:S(2)}, u32[]{:S(2)}) collective-permute-start(bf16[80,128]{1,0:T(8,128)(2,1)S(1)} %get-tuple-element.27), channel_id=1, source_target_pairs={{0,4},{4,8},{8,12},{16,20},{20,24},{24,28},{32,36},{36,40},{40,44}... | collective-permute-start | bytes 61448 | tf_op jit(solution)/shard_map/ppermute | solution.py:371
  23.0 5.4 %collective-permute-start.1 = (bf16[80,128]{1,0:T(8,128)(2,1)S(1)}, bf16[80,128]{1,0:T(8,128)(2,1)S(1)}, u32[]{:S(2)}, u32[]{:S(2)}) collective-permute-start(bf16[80,128]{1,0:T(8,128)(2,1)S(1)} %get-tuple-element.28), channel_id=1, source_target_pairs={{4,0},{8,4},{12,8},{20,16},{24,20},{28,24},{36,32},{40,36},{44,40}... | collective-permute-start | bytes 61448 | tf_op jit(solution)/shard_map/ppermute | solution.py:371
  28.4 9.5 %collective-permute-start.2 = (bf16[80,128]{1,0:T(8,128)(2,1)S(1)}, bf16[80,128]{1,0:T(8,128)(2,1)S(1)}, u32[]{:S(2)}, u32[]{:S(2)}) collective-permute-start(bf16[80,128]{1,0:T(8,128)(2,1)S(1)} %pad_maximum_fusion), channel_id=1, source_target_pairs={{0,16},{4,20},{8,24},{12,28},{16,32},{20,36},{24,40},{28,44},{32,4... | collective-permute-start | bytes 61448 | tf_op jit(solution)/shard_map/ppermute | solution.py:371
  34.2 7.5 %collective-permute-start.3 = (bf16[80,128]{1,0:T(8,128)(2,1)S(1)}, bf16[80,128]{1,0:T(8,128)(2,1)S(1)}, u32[]{:S(2)}, u32[]{:S(2)}) collective-permute-start(bf16[80,128]{1,0:T(8,128)(2,1)S(1)} %pad_maximum_fusion.1), channel_id=1, source_target_pairs={{16,0},{20,4},{24,8},{28,12},{32,16},{36,20},{40,24},{44,28},{48,3... | collective-permute-start | bytes 61448 | tf_op jit(solution)/shard_map/ppermute | solution.py:371
  81.6 14.9 %all-to-all-start.4 = ((bf16[16,56,128]{2,1,0:T(8,128)(2,1)}), bf16[16,56,128]{2,1,0:T(8,128)(2,1)S(1)}, u32[]{:S(2)}, u32[]{:S(2)}) async-start(bf16[16,56,128]{2,1,0:T(8,128)(2,1)} %bitcast.15), calls=%async_computation.4 | async-start | bytes 458752 | tf_op jit(solution)/shard_map/all_to_all | solution.py:386
